TPU v7x, 512 devices: a whole 4x4x16 slice. The times are simulated.
512 devices in a mesh: tm: 64 (over z, y), space: 8 (over x, core).
Axes of the slice: x: 4, y: 4, z: 16, core: 2. Of those that a mesh axis runs over, the one named last changes fastest.
Arguments:
- frames: bfloat16 [256, 256, 4096], P('tm', 'space'), may hold values from -6 to 6
- norm_gain: float32 [4096], replicated, may hold values from 0.1 to 1.9
- w_qkv: bfloat16 [4096, 3, 2048], P('tm', None, 'space'), may hold values from -2 to 2
Outputs:
- attended: bfloat16 [256, 256, 2048], P('tm', None, 'space')
All inputs are finite; a program needn't handle non-finite values.
Results may differ from a plain program's by a relative error of at most 0.0068.
Values may be sent and summed in bfloat16 or wider, within the bound.
No kernel may reach another device: no remote copies, remote signals or barrier semaphores. Data moves between devices by JAX's collectives and lax.ppermute only.
A program may use at most 64 MiB of HBM per device.

v0:
```python
import jax
import jax.numpy as jnp
from jax import lax
from jax.sharding import PartitionSpec as P

HEAD = 128


def normalize(inputs, norm_gain):
    widened = inputs.astype(jnp.float32)
    mean_square = jnp.mean(widened * widened, axis=-1, keepdims=True)
    return (widened * lax.rsqrt(mean_square + 1e-05) * norm_gain).astype(jnp.bfloat16)


def attend(query, key_block, values):
    scores = jnp.einsum(
        "fpha,gpha->phfg", query, key_block, preferred_element_type=jnp.float32
    ) * query.shape[-1] ** (-0.5)
    row_index = lax.broadcasted_iota(jnp.int32, scores.shape, 2)
    col_index = lax.broadcasted_iota(jnp.int32, scores.shape, 3)
    scores = jnp.where(col_index <= row_index, scores, -jnp.inf)
    row_max = jnp.max(scores, axis=-1, keepdims=True)
    exp_scores = jnp.exp(scores - row_max)
    attn_weights = (exp_scores / jnp.sum(exp_scores, axis=-1, keepdims=True)).astype(jnp.bfloat16)
    mixed = jnp.einsum("phfg,gpha->fpha", attn_weights, values, preferred_element_type=jnp.float32)
    return mixed.astype(jnp.bfloat16)


def temporal(per_patch):
    query = per_patch[:, :, 0]
    key_block = per_patch[:, :, 1]
    values = per_patch[:, :, 2]
    return attend(query, key_block, values)


def shards(frames, norm_gain, w_qkv):
    frame_count = frames.shape[0]
    model_width = frames.shape[2]
    raw_tokens = lax.all_gather(frames, "space", axis=1, tiled=True)
    gathered = normalize(raw_tokens, norm_gain)
    patch_count = gathered.shape[1]
    token_rows = gathered.reshape(frame_count * patch_count, model_width)
    local_columns = w_qkv.shape[2]
    qkv_width = 3 * local_columns
    all_weights = lax.all_gather(w_qkv, "tm", axis=0, tiled=True)
    flat_weights = all_weights.reshape(model_width, qkv_width)
    projected = jnp.dot(token_rows, flat_weights, preferred_element_type=jnp.float32)
    local_heads = local_columns // HEAD
    packed = projected.astype(jnp.bfloat16).reshape(frame_count, patch_count, 3, local_heads, HEAD)
    mixed = temporal(lax.all_to_all(packed, "tm", split_axis=1, concat_axis=0, tiled=True))
    returned = lax.all_to_all(mixed, "tm", split_axis=0, concat_axis=1, tiled=True)
    return returned.reshape(frame_count, patch_count, local_columns)


def solution(mesh):
    placed = (P("tm", "space", None), P(), P("tm", None, "space"))
    return jax.shard_map(
        shards, mesh=mesh, in_specs=placed, out_specs=P("tm", None, "space"), check_vma=False
    )
```

profile of v0, /device:TPU:6, one launch (start us, length us, event | category | flops | bytes accessed | tf_op | source)
XLA Modules:
  0.0 390.4 jit_solution(1773227738809785212)
XLA Ops:
  6.5 0.0 all-gather.5.cloned.1.call-start
  6.5 0.7 all-gather.5.cloned.1.call-update
  7.3 0.0 all-gather.3.cloned.1.call-start
  7.3 0.7 all-gather.3.cloned.1.call-update
  8.0 158.4 %all-gather.5.cloned.1.call-done = bf16[4096,3,256]{2,0,1:T(8,128)(2,1)} async-done(((bf16[64,3,256]{2,0,1:T(8,128)(2,1)}), bf16[4096,3,256]{2,0,1:T(8,128)(2,1)}) %all-gather.5.cloned.1.call-update) | async-done | bytes 6291472 | tf_op jit(solution)/shard_map/all_gather | solution.py:45
  166.4 8.8 %copy.19 = bf16[4096,3,256]{0,2,1:T(8,128)(2,1)} copy(bf16[4096,3,256]{2,0,1:T(8,128)(2,1)} %all-gather.5.cloned.1.call-done) | data formatting | bytes 12582912 | tf_op jit(solution)/shard_map/all_gather | solution.py:45
  175.2 0.0 copy-start
  175.2 43.9 %all-gather.3.cloned.1.call-done = bf16[4,256,4096]{2,1,0:T(8,128)(2,1)} async-done(((bf16[4,32,4096]{2,1,0:T(8,128)(2,1)}), bf16[4,256,4096]{2,1,0:T(8,128)(2,1)}) %all-gather.3.cloned.1.call-update) | async-done | bytes 8388624 | tf_op jit(solution)/shard_map/all_gather | solution.py:39
  219.1 5.1 %fusion.1 = f32[4,256]{1,0:T(4,128)S(1)} fusion(bf16[4,256,4096]{2,1,0:T(8,128)(2,1)} %all-gather.3.cloned.1.call-done), kind=kLoop, calls=%fused_computation.3 | loop fusion | flops 12581888 | bytes 8392704 | tf_op jit(solution)/shard_map/reduce_sum | solution.py:11
  224.2 0.0 copy-done
  224.2 10.3 %fusion.3 = bf16[4,256,4096]{2,1,0:T(8,128)(2,1)} fusion(bf16[4,256,4096]{2,1,0:T(8,128)(2,1)} %all-gather.3.cloned.1.call-done, f32[4096]{0:T(1024)S(1)} %copy-done, f32[4,256]{1,0:T(4,128)S(1)} %add_rsqrt_fusion), kind=kLoop, calls=%fused_computation.5 | loop fusion | flops 16777216 | bytes 16797696 | tf_op jit(solution)/shard_map/convert_element_type | solution.py:12
  234.5 11.0 %convolution_convert_fusion = bf16[1024,768]{1,0:T(8,128)(2,1)S(1)} fusion(bf16[1024,4096]{1,0:T(8,128)(2,1)} %bitcast.46, bf16[4096,768]{0,1:T(8,128)(2,1)} %bitcast.47), kind=kOutput, calls=%fused_computation.11 | convolution fusion | flops 6443237376 | bytes 16252928 | tf_op jit(solution)/shard_map/dot_general | solution.py:47
  245.5 0.4 reshape.26
  245.9 1.1 copy.20
  247.0 93.8 %all_to_all.33 = bf16[4,256,3,2,128]{4,3,2,0,1:T(2,128)(2,1)S(1)} all-to-all(bf16[4,256,3,2,128]{4,3,2,0,1:T(2,128)(2,1)S(1)} %copy.20), channel_id=1, replica_groups=mesh['tm'=64,'space'=8] {'tm'}, dimensions={1} | all-to-all | bytes 3145728 | tf_op jit(solution)/shard_map/all_to_all | solution.py:50
  340.8 0.8 copy.21
  341.5 0.6 fusion.15
  342.2 1.0 fusion.5
  343.1 0.5 copy.24
  343.6 38.2 %all_to_all.34 = bf16[256,4,2,128]{3,2,1,0:T(2,128)(2,1)S(1)} all-to-all(bf16[256,4,2,128]{3,2,1,0:T(2,128)(2,1)S(1)} %copy.24), channel_id=1, replica_groups=mesh['tm'=64,'space'=8] {'tm'}, dimensions={0} | all-to-all | bytes 1048576 | tf_op jit(solution)/shard_map/all_to_all | solution.py:51
  381.8 0.1 copy.25
  381.9 0.5 copy.26
  382.4 1.1 reshape.27
  (1 shorter events, 0.0 us)
Async XLA Ops:
  6.5 159.9 %all-gather.5.cloned.1.call-start = ((), (), s32[]{:S(2)}) async-start(), calls=%async_computation.3 | async-start | bytes 6389760 | tf_op jit(solution)/shard_map/all_gather | solution.py:45
  7.3 211.8 %all-gather.3.cloned.1.call-start = ((), (), s32[]{:S(2)}) async-start(), calls=%async_computation.2 | async-start | bytes 9437184 | tf_op jit(solution)/shard_map/all_gather | solution.py:39
  175.2 49.0 %copy-start = (f32[4096]{0:T(1024)S(1)}, f32[4096]{0:T(1024)}, u32[]{:S(2)}) copy-start(f32[4096]{0:T(1024)} %param.4) | copy-start | bytes 49156
Sparse Core Ops, SparseCore 0:
  10.3 156.0 all-gather.4
  168.5 50.5 all-gather.2
where the time goes:
time: 392 us; the launch traced here: 390 us
  waiting for transfers between devices  204 us (52%)
  blocking collectives  132 us (34%)
  other arithmetic  15.4 us (4%)
  between operations  13.5 us (3%)
  local copies, waits for them, and re-layouts  13.3 us (3%)
  matrix products  12.6 us (3%)
    all_gather x1, waiting for transfers between devices, shards(): all_weights = lax.all_gather(w_qkv, 'tm', axis=0, tiled=True)  158 us
    all_to_all x1, blocking collectives, shards(): lax.all_to_all(packed, 'tm', split_axis=1, concat_axis=0, tiled=True)  93.8 us
    all_gather x1, waiting for transfers between devices, shards(): raw_tokens = lax.all_gather(frames, 'space', axis=1, tiled=True)  43.9 us
    all_to_all x1, blocking collectives, shards(): lax.all_to_all(mixed, 'tm', split_axis=0, concat_axis=1, tiled=True)  38.2 us
    dot_general x1, matrix products, shards(): jnp.dot(token_rows, flat_weights, preferred_element_type=jnp.float32)  11 us
    convert_element_type x1, other arithmetic, normalize(): (widened * lax.rsqrt(mean_square + 1e-05) * norm_gain).astype(jnp.bfloat16)  10.3 us
    all_gather x1, local copies, waits for them, and re-layouts, shards(): all_weights = lax.all_gather(w_qkv, 'tm', axis=0, tiled=True)  8.78 us
  transfers between devices with their start and end apart: 2, of which 2 were waited for; matrix products, arithmetic and copies ran while one was open for 2% of the time, Pallas kernels for 0%

commit v1 on v0

v1 whole, which is shorter than its diff:
```python
import jax
import jax.numpy as jnp
from jax import lax
from jax.experimental import pallas as pl
from jax.experimental.pallas import tpu as pltpu
from jax.sharding import Mesh, PartitionSpec as P

BF, F32 = jnp.bfloat16, jnp.float32
Z, Y, X, C = 16, 4, 4, 2
D, HEAD = 4096, 128
VMEM = pltpu.VMEM


def iota(shape, dim):
    return lax.broadcasted_iota(jnp.int32, shape, dim)


def one_hot(source):
    return lambda n, m: jnp.where(source(iota((n, m), 0)) == iota((n, m), 1), 1.0, 0.0).astype(BF)


def pick(matrix, rows):
    return jnp.dot(matrix, rows, preferred_element_type=F32)


def normalize_kernel(frames_ref, gain_ref, out_ref):
    rows = frames_ref[...].reshape(128, D).astype(F32)
    scale = lax.rsqrt(jnp.mean(rows * rows, axis=-1, keepdims=True) + 1e-05)
    shuffle = one_hot(lambda i: (i & 3) * 32 + (i >> 3) * 2 + ((i >> 2) & 1))(128, 128)
    spread = one_hot(lambda i: ((i >> 6) & 3) * 128 + (i >> 8) * 64 + (i & 63))(512, 512)
    for j in range(8):
        cut = slice(512 * j, 512 * (j + 1))
        normed = (rows[:, cut] * scale * gain_ref[:, cut]).astype(BF)
        moved = pick(pick(shuffle, normed).astype(BF), spread).astype(BF)
        for y in range(Y):
            out_ref[:, 1024 * y + 128 * j : 1024 * y + 128 * (j + 1)] = moved[:, 128 * y : 128 * (y + 1)]


def project_kernel(y_ref, tokens_ref, own_ref, below_ref, above_ref, far_low_ref, far_high_ref, out_ref):
    y = y_ref[0]

    def slab(where, width):
        return tokens_ref[:, pl.ds(pl.multiple_of(where, 512), width)]

    own = slab(y * 1024, 1024)
    below = slab(((y + 3) & 3) * 1024, 1024)
    above = slab(((y + 1) & 3) * 1024, 1024)
    far_low = slab(((y + 2) & 3) * 1024, 512)
    far_high = slab(((y + 2) & 3) * 1024 + 512, 512)
    for c in range(3):
        total = None
        for part, ref in (
            (own, own_ref), (below, below_ref), (above, above_ref), (far_low, far_low_ref), (far_high, far_high_ref),
        ):
            weights = ref[:, c].reshape(ref.shape[0] * 64, 256)
            term = jnp.dot(part, weights, preferred_element_type=F32)
            total = term if total is None else total + term
        out_ref[:, 256 * c : 256 * (c + 1)] = total.astype(BF)


def attend_kernel(qkv_ref, out_ref):
    def source(i):
        return ((i >> 2) & 3) * 128 + ((i >> 4) & 15) * 8 + (i >> 8) * 4 + (i & 3)

    order = one_hot(source)(512, 512)
    back = one_hot(lambda i: ((i >> 2) & 1) * 256 + (i >> 3) * 4 + (i & 3))(512, 512)
    keep = iota((256, 256), 1) <= iota((256, 256), 0)
    halves = []
    for c in range(C):
        rows = pick(order, qkv_ref[:, 128 * c : 128 * (c + 1)].reshape(512, 768)).astype(BF)
        patches = []
        for p in range(2):
            mine = rows[256 * p : 256 * (p + 1)]
            heads = []
            for h in range(2):
                query, key, value = (mine[:, 256 * k + 128 * h : 256 * k + 128 * (h + 1)] for k in range(3))
                scores = lax.dot_general(query, key, (((1,), (1,)), ((), ())), preferred_element_type=F32) * HEAD**-0.5
                scores = jnp.where(keep, scores, -jnp.inf)
                grown = jnp.exp(scores - jnp.max(scores, axis=-1, keepdims=True))
                probs = (grown / jnp.sum(grown, axis=-1, keepdims=True)).astype(BF)
                heads.append(jnp.dot(probs, value, preferred_element_type=F32).astype(BF))
            patches.append(jnp.concatenate(heads, axis=1))
        halves.append(pick(back, jnp.concatenate(patches, axis=0)).reshape(64, 8, 256))
    out_ref[...] = jnp.concatenate(halves, axis=1).astype(BF)


def place_kernel(mixed_ref, out_ref):
    order = one_hot(lambda i: ((i >> 1) & 15) * 16 + ((i >> 5) & 1) * 8 + (i & 1) * 4 + (i >> 6))(256, 256)
    for y in range(Y):
        rows = pick(order, mixed_ref[:, y].reshape(256, 256)).astype(BF)
        for f in range(4):
            out_ref[f, 64 * y : 64 * (y + 1)] = rows[64 * f : 64 * (f + 1)]


def whole():
    return pl.BlockSpec(memory_space=VMEM)


def call(kernel, out_shape, *operands, **kwargs):
    return pl.pallas_call(
        kernel,
        out_shape=jax.ShapeDtypeStruct(out_shape, BF),
        in_specs=[whole()] * len(operands),
        out_specs=whole(),
        compiler_params=pltpu.CompilerParams(vmem_limit_bytes=40 * 2**20),
        **kwargs,
    )(*operands)


def shift(x, axis, by):
    n = {"z": Z, "y": Y, "x": X, "c": C}[axis]
    return lax.ppermute(x, axis, [(i, (i + by) % n) for i in range(n)])


def shards(frames, norm_gain, w_qkv):
    weights = lax.all_gather(jnp.transpose(w_qkv, (1, 0, 2)), "z", axis=0)
    packed = call(normalize_kernel, (128, D), frames, norm_gain.reshape(1, D))
    tokens = lax.all_to_all(packed.reshape(Z, 8, D), "z", 0, 0, tiled=True).reshape(128, D)
    below = shift(weights, "y", 1)
    above = shift(weights, "y", -1)
    far_low = shift(below[:8], "y", 1)
    far_high = shift(above[8:], "y", -1)
    gathered = lax.all_gather(tokens, ("x", "c"), axis=0, tiled=True)
    here = lax.axis_index("y").astype(jnp.int32).reshape(1)
    rows = 256
    fixed = lambda k: pl.BlockSpec((k, 3, 64, 256), lambda i: (0, 0, 0, 0))
    qkv = pl.pallas_call(
        project_kernel,
        grid=(1024 // rows,),
        out_shape=jax.ShapeDtypeStruct((1024, 768), BF),
        in_specs=[pl.BlockSpec(memory_space=pltpu.SMEM), pl.BlockSpec((rows, D), lambda i: (i, 0)),
                  fixed(16), fixed(16), fixed(16), fixed(8), fixed(8)],
        out_specs=pl.BlockSpec((rows, 768), lambda i: (i, 0)),
        compiler_params=pltpu.CompilerParams(vmem_limit_bytes=48 * 2**20),
    )(here, gathered, weights, below, above, far_low, far_high)
    qkv = lax.all_to_all(qkv.reshape(Y, 256, 768), "y", 0, 0, tiled=True)
    mixed = call(attend_kernel, (64, 16, 256), qkv)
    mixed = lax.all_to_all(mixed, ("z", "y"), 0, 0, tiled=True)
    return call(place_kernel, (4, 256, 256), mixed.reshape(Z, Y, 16, 256))


def solution(mesh):
    grid = Mesh(mesh.devices.reshape(Z, Y, X, C), ("z", "y", "x", "c"))
    rows, columns = ("z", "y"), ("x", "c")
    return jax.shard_map(
        shards, mesh=grid, in_specs=(P(rows, columns, None), P(), P(rows, None, columns)),
        out_specs=P(rows, None, columns), check_vma=False,
    )
```

time: 392 us -> 266 us (0.68)
  waiting for transfers between devices: 204 us -> 129 us
  blocking collectives: 132 us -> 69.9 us
  starting transfers between devices: 0.04 us -> 28.9 us
  Pallas kernels: 0 us -> 17.3 us
  other arithmetic: 15.4 us -> 0 us
  matrix products: 12.6 us -> 0 us
  local copies, waits for them, and re-layouts: 13.3 us -> 5.09 us
    all_gather x2, waiting for transfers between devices: 202 us -> 34.5 us  [the longest x1 34.5 us: shards(): weights = lax.all_gather(jnp.transpose(w_qkv, (1, 0, 2)), 'z', axis=0)]
    all_to_all x2, blocking collectives: 132 us -> 69.9 us  [the longest x1 45.7 us: shards(): mixed = lax.all_to_all(mixed, ('z', 'y'), 0, 0, tiled=True)]
    all_to_all x0 -> x1, waiting for transfers between devices: none -> 53.6 us  [shards(): lax.all_to_all(packed.reshape(Z, 8, D), 'z', 0, 0, tiled=True)]
    ppermute x0 -> x4, waiting for transfers between devices: none -> 39.9 us  [shift(): return lax.ppermute(x, axis, [(i, (i + by) % n) for i in range(n)])]
    pallas_call x0 -> x4, Pallas kernels: none -> 17.3 us  [the longest x1 9.79 us: shards(): pl.pallas_call(project_kernel, grid=(1024 // rows,), out_shape=jax.ShapeD...]
    all_to_all x0 -> x1, starting transfers between devices: none -> 15.2 us  [shards(): lax.all_to_all(packed.reshape(Z, 8, D), 'z', 0, 0, tiled=True)]
    ppermute x0 -> x4, starting transfers between devices: none -> 13.7 us  [shift(): return lax.ppermute(x, axis, [(i, (i + by) % n) for i in range(n)])]
    dot_general x2 -> x0, matrix products: 11.9 us -> none  [the longest x1 11 us: shards(): jnp.dot(token_rows, flat_weights, preferred_element_type=jnp.float32)]
  transfers between devices with their start and end apart: 2 -> 7, of which waited for: 2 -> 5; matrix products, arithmetic and copies ran while one was open for 2% -> 1% of each run, Pallas kernels for 0% -> 0%
where the time goes in v1:
time: 266 us; the launch traced here: 263 us
  waiting for transfers between devices  129 us (48%)
  blocking collectives  69.9 us (26%)
  starting transfers between devices  28.9 us (11%)
  Pallas kernels  17.3 us (7%)
  between operations  13.5 us (5%)
  local copies, waits for them, and re-layouts  5.09 us (2%)
    all_to_all x1, waiting for transfers between devices, shards(): lax.all_to_all(packed.reshape(Z, 8, D), 'z', 0, 0, tiled=True)  53.6 us
    all_to_all x1, blocking collectives, shards(): mixed = lax.all_to_all(mixed, ('z', 'y'), 0, 0, tiled=True)  45.7 us
    ppermute x4, waiting for transfers between devices, shift(): return lax.ppermute(x, axis, [(i, (i + by) % n) for i in range(n)])  39.9 us
    all_gather x1, waiting for transfers between devices, shards(): weights = lax.all_gather(jnp.transpose(w_qkv, (1, 0, 2)), 'z', axis=0)  34.5 us
    all_to_all x1, blocking collectives, shards(): qkv = lax.all_to_all(qkv.reshape(Y, 256, 768), 'y', 0, 0, tiled=True)  24.2 us
    all_to_all x1, starting transfers between devices, shards(): lax.all_to_all(packed.reshape(Z, 8, D), 'z', 0, 0, tiled=True)  15.2 us
    ppermute x4, starting transfers between devices, shift(): return lax.ppermute(x, axis, [(i, (i + by) % n) for i in range(n)])  13.7 us
    pallas_call x1, Pallas kernels, shards(): pl.pallas_call(project_kernel, grid=(1024 // rows,), out_shape=jax.ShapeD...  9.79 us
  transfers between devices with their start and end apart: 7, of which 5 were waited for; matrix products, arithmetic and copies ran while one was open for 1% of the time, Pallas kernels for 0%

profile of v1, /device:TPU:6, one launch (start us, length us, event | category | flops | bytes accessed | tf_op | source)
XLA Modules:
  0.0 263.4 jit_solution(3577422824209459603)
XLA Ops:
  6.5 1.2 copy-done.1
  7.8 0.0 copy-start.2
  7.8 0.7 copy-done.2
  8.5 3.2 %shard_map.37 = bf16[128,4096]{1,0:T(8,128)(2,1)} custom-call(bf16[4,32,4096]{2,1,0:T(8,128)(2,1)S(1)} %copy-done.1, f32[1,4096]{1,0:T(1,128)S(1)} %bitcast.13), custom_call_target="tpu_custom_call" | custom-call | tf_op jit(solution)/shard_map/pallas_call | solution.py:100
  11.6 15.2 %all-to-all-start = ((bf16[16,8,4096]{2,1,0:T(8,128)(2,1)}), bf16[16,8,4096]{2,1,0:T(8,128)(2,1)S(1)}, u32[]{:S(2)}, u32[]{:S(2)}) async-start(bf16[16,8,4096]{2,1,0:T(8,128)(2,1)} %bitcast.2), calls=%async_computation | async-start | bytes 2097152 | tf_op jit(solution)/shard_map/all_to_all | solution.py:118
  26.8 0.0 all-gather.6.cloned.1.call-start
  26.9 0.7 all-gather.6.cloned.1.call-update
  27.6 0.0 all-gather.4.cloned.1.call-start
  27.6 53.6 %all-to-all-done = bf16[16,8,4096]{2,1,0:T(8,128)(2,1)S(1)} async-done(((bf16[16,8,4096]{2,1,0:T(8,128)(2,1)}), bf16[16,8,4096]{2,1,0:T(8,128)(2,1)S(1)}, u32[]{:S(2)}, u32[]{:S(2)}) %all-to-all-start) | async-done | bytes 1048608 | tf_op jit(solution)/shard_map/all_to_all | solution.py:118
  81.2 0.0 copy-start.3
  81.2 1.0 copy-done.3
  82.2 0.0 all-gather.4.cloned.1.call-update
  82.2 34.5 %all-gather.6.cloned.1.call-done = bf16[48,64,256]{2,1,0:T(8,128)(2,1)} async-done(((bf16[3,64,256]{2,1,0:T(8,128)(2,1)}), bf16[48,64,256]{2,1,0:T(8,128)(2,1)}) %all-gather.6.cloned.1.call-update) | async-done | bytes 1572880 | tf_op jit(solution)/shard_map/all_gather | solution.py:116
  116.7 4.9 %collective-permute-start.1 = (bf16[16,3,64,256]{3,2,1,0:T(8,128)(2,1)}, bf16[16,3,64,256]{3,2,1,0:T(8,128)(2,1)S(1)}, u32[]{:S(2)}, u32[]{:S(2)}) collective-permute-start(bf16[16,3,64,256]{3,2,1,0:T(8,128)(2,1)} %bitcast.10), channel_id=1, source_target_pairs={{0,24},{8,0},{16,8},{24,16},{1,25},{9,1},{17,9},{25,17},{2,26},{10... | collective-permute-start | bytes 4718600 | tf_op jit(solution)/shard_map/ppermute | solution.py:112
  121.6 1.9 collective-permute-start
  123.5 26.5 %collective-permute-done.1.above_ref = bf16[16,3,64,256]{3,2,1,0:T(8,128)(2,1)S(1)} collective-permute-done((bf16[16,3,64,256]{3,2,1,0:T(8,128)(2,1)}, bf16[16,3,64,256]{3,2,1,0:T(8,128)(2,1)S(1)}, u32[]{:S(2)}, u32[]{:S(2)}) %collective-permute-start.1) | collective-permute-done | bytes 1572896 | tf_op jit(solution)/shard_map/ppermute | solution.py:112
  150.0 1.0 slice.9
  151.1 5.0 %collective-permute-start.3 = (bf16[8,3,64,256]{3,2,1,0:T(8,128)(2,1)}, bf16[8,3,64,256]{3,2,1,0:T(8,128)(2,1)S(1)}, u32[]{:S(2)}, u32[]{:S(2)}) collective-permute-start(bf16[8,3,64,256]{3,2,1,0:T(8,128)(2,1)} %slice.9), channel_id=1, source_target_pairs={{0,24},{8,0},{16,8},{24,16},{1,25},{9,1},{17,9},{25,17},{2,26},{10... | collective-permute-start | bytes 2359304 | tf_op jit(solution)/shard_map/ppermute | solution.py:112
  156.1 0.0 collective-permute-done.below_ref
  156.1 0.0 copy-start.5
  156.1 1.1 slice.8
  157.2 0.0 copy-done.4
  157.2 1.9 collective-permute-start.2
  159.1 0.0 copy-done.5
  159.1 7.0 %collective-permute-done.3.far_high_ref = bf16[8,3,64,256]{3,2,1,0:T(8,128)(2,1)S(1)} collective-permute-done((bf16[8,3,64,256]{3,2,1,0:T(8,128)(2,1)}, bf16[8,3,64,256]{3,2,1,0:T(8,128)(2,1)S(1)}, u32[]{:S(2)}, u32[]{:S(2)}) %collective-permute-start.3) | collective-permute-done | bytes 786464 | tf_op jit(solution)/shard_map/ppermute | solution.py:112
  166.1 6.4 %collective-permute-done.2.far_low_ref = bf16[8,3,64,256]{3,2,1,0:T(8,128)(2,1)S(1)} collective-permute-done((bf16[8,3,64,256]{3,2,1,0:T(8,128)(2,1)}, bf16[8,3,64,256]{3,2,1,0:T(8,128)(2,1)S(1)}, u32[]{:S(2)}, u32[]{:S(2)}) %collective-permute-start.2) | collective-permute-done | bytes 786464 | tf_op jit(solution)/shard_map/ppermute | solution.py:112
  172.5 0.0 copy-done
  172.5 9.8 %shard_map.38 = bf16[1024,768]{1,0:T(8,128)(2,1)S(1)} custom-call(s32[1]{0:T(128)} %bitcast.y_ref, bf16[1024,4096]{1,0:T(8,128)(2,1)} %all-gather.4.cloned.1.call-done.tokens_ref, bf16[16,3,64,256]{3,2,1,0:T(8,128)(2,1)S(1)} %bitcast.12, bf16[16,3,64,256]{3,2,1,0:T(8,128)(2,1)} %copy-done.5, bf16[16,3,64,256]{3,2,1,0:T(8,128)(2,1)} %copy-done.4, ...), custom_call_target="tpu_custom_call" | custom-call | tf_op jit(solution)/shard_map/pallas_call | solution.py:127
  182.3 24.2 %all_to_all.15.qkv_ref = bf16[4,256,768]{2,1,0:T(8,128)(2,1)S(1)} all-to-all(bf16[4,256,768]{2,1,0:T(8,128)(2,1)S(1)} %bitcast.8), channel_id=1, replica_groups=mesh['z'=16,'y'=4,'x'=4,'c'=2] {'y'}, dimensions={0} | all-to-all | bytes 3145728 | tf_op jit(solution)/shard_map/all_to_all | solution.py:136
  206.5 3.3 %shard_map.39 = bf16[64,16,256]{2,1,0:T(8,128)(2,1)S(1)} custom-call(bf16[4,256,768]{2,1,0:T(8,128)(2,1)S(1)} %all_to_all.15.qkv_ref), custom_call_target="tpu_custom_call" | custom-call | tf_op jit(solution)/shard_map/pallas_call | solution.py:100
  209.8 45.7 %all_to_all.16 = bf16[64,16,256]{2,1,0:T(8,128)(2,1)S(1)} all-to-all(bf16[64,16,256]{2,1,0:T(8,128)(2,1)S(1)} %shard_map.39), channel_id=1, replica_groups=mesh['z'=16,'y'=4,'x'=4,'c'=2] {'z','y'}, dimensions={0} | all-to-all | bytes 1048576 | tf_op jit(solution)/shard_map/all_to_all | solution.py:138
  255.5 1.1 shard_map.40
  (4 shorter events, 0.0 us)
Async XLA Ops:
  6.5 1.2 copy-start.1
  7.8 0.7 copy-start.2
  11.6 69.6 %all-to-all-start = ((bf16[16,8,4096]{2,1,0:T(8,128)(2,1)}), bf16[16,8,4096]{2,1,0:T(8,128)(2,1)S(1)}, u32[]{:S(2)}, u32[]{:S(2)}) async-start(bf16[16,8,4096]{2,1,0:T(8,128)(2,1)} %bitcast.2), calls=%async_computation | async-start | bytes 2097152 | tf_op jit(solution)/shard_map/all_to_all | solution.py:118
  26.8 89.9 %all-gather.6.cloned.1.call-start = ((), (), s32[]{:S(2)}) async-start(), calls=%async_computation.4 | async-start | bytes 1671168 | tf_op jit(solution)/shard_map/all_gather | solution.py:116
  27.6 144.9 %all-gather.4.cloned.1.call-start = ((), (), s32[]{:S(2)}) async-start(), calls=%async_computation.3 | async-start | bytes 9437184 | tf_op jit(solution)/shard_map/all_gather | solution.py:123
  81.2 1.0 copy-start.3
  116.7 55.8 %copy-start = (bf16[48,64,256]{2,1,0:T(8,128)(2,1)S(1)}, bf16[48,64,256]{2,1,0:T(8,128)(2,1)}, u32[]{:S(2)}) copy-start(bf16[48,64,256]{2,1,0:T(8,128)(2,1)} %all-gather.6.cloned.1.call-done) | copy-start | bytes 4718596
  116.7 33.3 %collective-permute-start.1 = (bf16[16,3,64,256]{3,2,1,0:T(8,128)(2,1)}, bf16[16,3,64,256]{3,2,1,0:T(8,128)(2,1)S(1)}, u32[]{:S(2)}, u32[]{:S(2)}) collective-permute-start(bf16[16,3,64,256]{3,2,1,0:T(8,128)(2,1)} %bitcast.10), channel_id=1, source_target_pairs={{0,24},{8,0},{16,8},{24,16},{1,25},{9,1},{17,9},{25,17},{2,26},{10... | collective-permute-start | bytes 4718600 | tf_op jit(solution)/shard_map/ppermute | solution.py:112
  121.6 34.5 %collective-permute-start = (bf16[16,3,64,256]{3,2,1,0:T(8,128)(2,1)}, bf16[16,3,64,256]{3,2,1,0:T(8,128)(2,1)S(1)}, u32[]{:S(2)}, u32[]{:S(2)}) collective-permute-start(bf16[16,3,64,256]{3,2,1,0:T(8,128)(2,1)} %bitcast.11), channel_id=1, source_target_pairs={{0,8},{8,16},{16,24},{24,0},{1,9},{9,17},{17,25},{25,1},{2,10},{10... | collective-permute-start | bytes 4718600 | tf_op jit(solution)/shard_map/ppermute | solution.py:112
  150.0 7.2 %copy-start.4 = (bf16[16,3,64,256]{3,2,1,0:T(8,128)(2,1)}, bf16[16,3,64,256]{3,2,1,0:T(8,128)(2,1)S(1)}, u32[]{:S(2)}) copy-start(bf16[16,3,64,256]{3,2,1,0:T(8,128)(2,1)S(1)} %collective-permute-done.1.above_ref) | copy-start | bytes 4718596
  151.1 15.0 %collective-permute-start.3 = (bf16[8,3,64,256]{3,2,1,0:T(8,128)(2,1)}, bf16[8,3,64,256]{3,2,1,0:T(8,128)(2,1)S(1)}, u32[]{:S(2)}, u32[]{:S(2)}) collective-permute-start(bf16[8,3,64,256]{3,2,1,0:T(8,128)(2,1)} %slice.9), channel_id=1, source_target_pairs={{0,24},{8,0},{16,8},{24,16},{1,25},{9,1},{17,9},{25,17},{2,26},{10... | collective-permute-start | bytes 2359304 | tf_op jit(solution)/shard_map/ppermute | solution.py:112
  156.1 3.0 %copy-start.5 = (bf16[16,3,64,256]{3,2,1,0:T(8,128)(2,1)}, bf16[16,3,64,256]{3,2,1,0:T(8,128)(2,1)S(1)}, u32[]{:S(2)}) copy-start(bf16[16,3,64,256]{3,2,1,0:T(8,128)(2,1)S(1)} %collective-permute-done.below_ref) | copy-start | bytes 4718596
  157.2 15.3 %collective-permute-start.2 = (bf16[8,3,64,256]{3,2,1,0:T(8,128)(2,1)}, bf16[8,3,64,256]{3,2,1,0:T(8,128)(2,1)S(1)}, u32[]{:S(2)}, u32[]{:S(2)}) collective-permute-start(bf16[8,3,64,256]{3,2,1,0:T(8,128)(2,1)} %slice.8), channel_id=1, source_target_pairs={{0,8},{8,16},{16,24},{24,0},{1,9},{9,17},{17,25},{25,1},{2,10},{10... | collective-permute-start | bytes 2359304 | tf_op jit(solution)/shard_map/ppermute | solution.py:112
Sparse Core Ops, SparseCore 0:
  29.8 86.9 all-gather.5
  118.9 52.4 all-gather.3

commit v2 on v1

--- a/solution.py
+++ b/solution.py
@@ -27,11 +27,20 @@
     rows = frames_ref[...].reshape(128, D).astype(F32)
     scale = lax.rsqrt(jnp.mean(rows * rows, axis=-1, keepdims=True) + 1e-05)
     shuffle = one_hot(lambda i: (i & 3) * 32 + (i >> 3) * 2 + ((i >> 2) & 1))(128, 128)
-    spread = one_hot(lambda i: ((i >> 6) & 3) * 128 + (i >> 8) * 64 + (i & 63))(512, 512)
     for j in range(8):
         cut = slice(512 * j, 512 * (j + 1))
         normed = (rows[:, cut] * scale * gain_ref[:, cut]).astype(BF)
-        moved = pick(pick(shuffle, normed).astype(BF), spread).astype(BF)
+        out_ref[:, cut] = pick(shuffle, normed).astype(BF)
+
+
+def ready_kernel(weights_ref, out_ref):
+    out_ref[...] = jnp.zeros_like(out_ref)
+
+
+def spread_kernel(tokens_ref, ready_ref, out_ref):
+    spread = one_hot(lambda i: ((i >> 6) & 3) * 128 + (i >> 8) * 64 + (i & 63))(512, 512)
+    for j in range(8):
+        moved = pick(tokens_ref[:, 512 * j : 512 * (j + 1)], spread).astype(BF)
         for y in range(Y):
             out_ref[:, 1024 * y + 128 * j : 1024 * y + 128 * (j + 1)] = moved[:, 128 * y : 128 * (y + 1)]
 
@@ -116,6 +125,14 @@
     weights = lax.all_gather(jnp.transpose(w_qkv, (1, 0, 2)), "z", axis=0)
     packed = call(normalize_kernel, (128, D), frames, norm_gain.reshape(1, D))
     tokens = lax.all_to_all(packed.reshape(Z, 8, D), "z", 0, 0, tiled=True).reshape(128, D)
+    ready = pl.pallas_call(
+        ready_kernel,
+        out_shape=jax.ShapeDtypeStruct((16, 128), BF),
+        in_specs=[pl.BlockSpec(memory_space=pl.ANY)],
+        out_specs=whole(),
+        cost_estimate=pl.CostEstimate(flops=10**11, bytes_accessed=0, transcendentals=0),
+    )(weights)
+    tokens = call(spread_kernel, (128, D), tokens, ready)
     below = shift(weights, "y", 1)
     above = shift(weights, "y", -1)
     far_low = shift(below[:8], "y", 1)

time: 266 us -> 261 us (0.981)
  waiting for transfers between devices: 129 us -> 125 us
  blocking collectives: 69.9 us -> 67.1 us
    all_to_all x1, waiting for transfers between devices: 53.6 us -> 0.01 us  [shards(): lax.all_to_all(packed.reshape(Z, 8, D), 'z', 0, 0, tiled=True)]
    all_gather x1, waiting for transfers between devices: 34.5 us -> 83.9 us  [shards(): weights = lax.all_gather(jnp.transpose(w_qkv, (1, 0, 2)), 'z', axis=0)]
    all_to_all x1, blocking collectives: 24.2 us -> 21.3 us  [shards(): qkv = lax.all_to_all(qkv.reshape(Y, 256, 768), 'y', 0, 0, tiled=True)]
    pallas_call x3 -> x4, Pallas kernels: 7.53 us -> 7.99 us  [call(): pl.pallas_call(kernel, out_shape=jax.ShapeDtypeStruct(out_shape, BF), in_...]
  transfers between devices with their start and end apart: 7 -> 7, of which waited for: 5 -> 4; matrix products, arithmetic and copies ran while one was open for 1% -> 1% of each run, Pallas kernels for 0% -> 1%
where the time goes in v2:
time: 261 us; the launch traced here: 258 us
  waiting for transfers between devices  125 us (48%)
  blocking collectives  67.1 us (26%)
  starting transfers between devices  29.5 us (11%)
  Pallas kernels  18.4 us (7%)
  between operations  13.5 us (5%)
  local copies, waits for them, and re-layouts  4.79 us (2%)
    all_gather x1, waiting for transfers between devices, shards(): weights = lax.all_gather(jnp.transpose(w_qkv, (1, 0, 2)), 'z', axis=0)  83.9 us
    all_to_all x1, blocking collectives, shards(): mixed = lax.all_to_all(mixed, ('z', 'y'), 0, 0, tiled=True)  45.7 us
    ppermute x4, waiting for transfers between devices, shift(): return lax.ppermute(x, axis, [(i, (i + by) % n) for i in range(n)])  40.6 us
    all_to_all x1, blocking collectives, shards(): qkv = lax.all_to_all(qkv.reshape(Y, 256, 768), 'y', 0, 0, tiled=True)  21.3 us
    all_to_all x1, starting transfers between devices, shards(): lax.all_to_all(packed.reshape(Z, 8, D), 'z', 0, 0, tiled=True)  15.2 us
    ppermute x4, starting transfers between devices, shift(): return lax.ppermute(x, axis, [(i, (i + by) % n) for i in range(n)])  14.3 us
    pallas_call x1, Pallas kernels, shards(): pl.pallas_call(project_kernel, grid=(1024 // rows,), out_shape=jax.ShapeD...  9.79 us
    pallas_call x4, Pallas kernels, call(): pl.pallas_call(kernel, out_shape=jax.ShapeDtypeStruct(out_shape, BF), in_...  7.99 us
  transfers between devices with their start and end apart: 7, of which 4 were waited for; matrix products, arithmetic and copies ran while one was open for 1% of the time, Pallas kernels for 1%

profile of v2, /device:TPU:6, one launch (start us, length us, event | category | flops | bytes accessed | tf_op | source)
XLA Modules:
  0.0 258.5 jit_solution(16248542189307921314)
XLA Ops:
  6.5 0.0 all-gather.6.cloned.1.call-start
  6.5 0.7 all-gather.6.cloned.1.call-update
  7.3 0.0 copy-start.1
  7.3 1.2 copy-done.1
  8.5 0.7 copy-done.2
  9.2 1.7 shard_map.37
  10.9 15.2 %all-to-all-start = ((bf16[16,8,4096]{2,1,0:T(8,128)(2,1)}), bf16[16,8,4096]{2,1,0:T(8,128)(2,1)S(1)}, u32[]{:S(2)}, u32[]{:S(2)}) async-start(bf16[16,8,4096]{2,1,0:T(8,128)(2,1)} %bitcast.2), calls=%async_computation | async-start | bytes 2097152 | tf_op jit(solution)/shard_map/all_to_all | solution.py:127
  26.1 0.0 all-gather.4.cloned.1.call-start
  26.2 83.9 %all-gather.6.cloned.1.call-done = bf16[48,64,256]{2,1,0:T(8,128)(2,1)} async-done(((bf16[3,64,256]{2,1,0:T(8,128)(2,1)}), bf16[48,64,256]{2,1,0:T(8,128)(2,1)}) %all-gather.6.cloned.1.call-update) | async-done | bytes 1572880 | tf_op jit(solution)/shard_map/all_gather | solution.py:125
  110.1 0.6 shard_map.38.ready_ref
  110.7 0.0 all-to-all-done
  110.7 0.7 copy-done.3
  111.4 1.9 shard_map.39
  113.3 0.0 all-gather.4.cloned.1.call-update
  113.3 0.0 copy-done
  113.3 5.2 %collective-permute-start.1 = (bf16[16,3,64,256]{3,2,1,0:T(8,128)(2,1)S(1)}, bf16[16,3,64,256]{3,2,1,0:T(8,128)(2,1)S(1)}, u32[]{:S(2)}, u32[]{:S(2)}) collective-permute-start(bf16[16,3,64,256]{3,2,1,0:T(8,128)(2,1)S(1)} %bitcast.12), channel_id=1, source_target_pairs={{0,24},{8,0},{16,8},{24,16},{1,25},{9,1},{17,9},{25,17},{2,26},{10... | collective-permute-start | bytes 4718600 | tf_op jit(solution)/shard_map/ppermute | solution.py:121
  118.5 1.9 collective-permute-start
  120.4 26.5 %collective-permute-done.1.above_ref = bf16[16,3,64,256]{3,2,1,0:T(8,128)(2,1)S(1)} collective-permute-done((bf16[16,3,64,256]{3,2,1,0:T(8,128)(2,1)S(1)}, bf16[16,3,64,256]{3,2,1,0:T(8,128)(2,1)S(1)}, u32[]{:S(2)}, u32[]{:S(2)}) %collective-permute-start.1) | collective-permute-done | bytes 1572896 | tf_op jit(solution)/shard_map/ppermute | solution.py:121
  146.9 1.1 slice.9
  148.0 5.3 %collective-permute-start.3 = (bf16[8,3,64,256]{3,2,1,0:T(8,128)(2,1)}, bf16[8,3,64,256]{3,2,1,0:T(8,128)(2,1)S(1)}, u32[]{:S(2)}, u32[]{:S(2)}) collective-permute-start(bf16[8,3,64,256]{3,2,1,0:T(8,128)(2,1)} %slice.9), channel_id=1, source_target_pairs={{0,24},{8,0},{16,8},{24,16},{1,25},{9,1},{17,9},{25,17},{2,26},{10... | collective-permute-start | bytes 2359304 | tf_op jit(solution)/shard_map/ppermute | solution.py:121
  153.3 0.0 collective-permute-done.below_ref
  153.3 0.0 copy-start.5
  153.3 1.1 slice.8
  154.4 0.0 copy-done.4
  154.4 1.9 collective-permute-start.2
  156.3 7.8 %collective-permute-done.3.far_high_ref = bf16[8,3,64,256]{3,2,1,0:T(8,128)(2,1)S(1)} collective-permute-done((bf16[8,3,64,256]{3,2,1,0:T(8,128)(2,1)}, bf16[8,3,64,256]{3,2,1,0:T(8,128)(2,1)S(1)}, u32[]{:S(2)}, u32[]{:S(2)}) %collective-permute-start.3) | collective-permute-done | bytes 786464 | tf_op jit(solution)/shard_map/ppermute | solution.py:121
  164.1 6.3 %collective-permute-done.2.far_low_ref = bf16[8,3,64,256]{3,2,1,0:T(8,128)(2,1)S(1)} collective-permute-done((bf16[8,3,64,256]{3,2,1,0:T(8,128)(2,1)}, bf16[8,3,64,256]{3,2,1,0:T(8,128)(2,1)S(1)}, u32[]{:S(2)}, u32[]{:S(2)}) %collective-permute-start.2) | collective-permute-done | bytes 786464 | tf_op jit(solution)/shard_map/ppermute | solution.py:121
  170.4 9.8 %shard_map.40 = bf16[1024,768]{1,0:T(8,128)(2,1)S(1)} custom-call(s32[1]{0:T(128)} %bitcast.y_ref, bf16[1024,4096]{1,0:T(8,128)(2,1)} %all-gather.4.cloned.1.call-done.tokens_ref, bf16[16,3,64,256]{3,2,1,0:T(8,128)(2,1)S(1)} %bitcast.14, bf16[16,3,64,256]{3,2,1,0:T(8,128)(2,1)} %copy-done.5, bf16[16,3,64,256]{3,2,1,0:T(8,128)(2,1)} %copy-done.4, ...), custom_call_target="tpu_custom_call" | custom-call | tf_op jit(solution)/shard_map/pallas_call | solution.py:144
  180.2 21.3 %all_to_all.15.qkv_ref = bf16[4,256,768]{2,1,0:T(8,128)(2,1)S(1)} all-to-all(bf16[4,256,768]{2,1,0:T(8,128)(2,1)S(1)} %bitcast.8), channel_id=1, replica_groups=mesh['z'=16,'y'=4,'x'=4,'c'=2] {'y'}, dimensions={0} | all-to-all | bytes 3145728 | tf_op jit(solution)/shard_map/all_to_all | solution.py:153
  201.6 3.3 %shard_map.41 = bf16[64,16,256]{2,1,0:T(8,128)(2,1)S(1)} custom-call(bf16[4,256,768]{2,1,0:T(8,128)(2,1)S(1)} %all_to_all.15.qkv_ref), custom_call_target="tpu_custom_call" | custom-call | tf_op jit(solution)/shard_map/pallas_call | solution.py:109
  204.8 45.7 %all_to_all.16 = bf16[64,16,256]{2,1,0:T(8,128)(2,1)S(1)} all-to-all(bf16[64,16,256]{2,1,0:T(8,128)(2,1)S(1)} %shard_map.41), channel_id=1, replica_groups=mesh['z'=16,'y'=4,'x'=4,'c'=2] {'z','y'}, dimensions={0} | all-to-all | bytes 1048576 | tf_op jit(solution)/shard_map/all_to_all | solution.py:155
  250.5 1.1 shard_map.42
  (6 shorter events, 0.0 us)
Async XLA Ops:
  6.5 103.6 %all-gather.6.cloned.1.call-start = ((), (), s32[]{:S(2)}) async-start(), calls=%async_computation.4 | async-start | bytes 1671168 | tf_op jit(solution)/shard_map/all_gather | solution.py:125
  7.3 1.2 copy-start.1
  8.5 0.7 copy-start.2
  10.9 99.8 %all-to-all-start = ((bf16[16,8,4096]{2,1,0:T(8,128)(2,1)}), bf16[16,8,4096]{2,1,0:T(8,128)(2,1)S(1)}, u32[]{:S(2)}, u32[]{:S(2)}) async-start(bf16[16,8,4096]{2,1,0:T(8,128)(2,1)} %bitcast.2), calls=%async_computation | async-start | bytes 2097152 | tf_op jit(solution)/shard_map/all_to_all | solution.py:127
  26.1 144.3 %all-gather.4.cloned.1.call-start = ((), (), s32[]{:S(2)}) async-start(), calls=%async_computation.3 | async-start | bytes 9437184 | tf_op jit(solution)/shard_map/all_gather | solution.py:140
  110.7 0.7 copy-start.3
  111.4 1.9 copy-start
  113.3 33.6 %collective-permute-start.1 = (bf16[16,3,64,256]{3,2,1,0:T(8,128)(2,1)S(1)}, bf16[16,3,64,256]{3,2,1,0:T(8,128)(2,1)S(1)}, u32[]{:S(2)}, u32[]{:S(2)}) collective-permute-start(bf16[16,3,64,256]{3,2,1,0:T(8,128)(2,1)S(1)} %bitcast.12), channel_id=1, source_target_pairs={{0,24},{8,0},{16,8},{24,16},{1,25},{9,1},{17,9},{25,17},{2,26},{10... | collective-permute-start | bytes 4718600 | tf_op jit(solution)/shard_map/ppermute | solution.py:121
  118.5 34.8 %collective-permute-start = (bf16[16,3,64,256]{3,2,1,0:T(8,128)(2,1)S(1)}, bf16[16,3,64,256]{3,2,1,0:T(8,128)(2,1)S(1)}, u32[]{:S(2)}, u32[]{:S(2)}) collective-permute-start(bf16[16,3,64,256]{3,2,1,0:T(8,128)(2,1)S(1)} %bitcast.13), channel_id=1, source_target_pairs={{0,8},{8,16},{16,24},{24,0},{1,9},{9,17},{17,25},{25,1},{2,10},{10... | collective-permute-start | bytes 4718600 | tf_op jit(solution)/shard_map/ppermute | solution.py:121
  146.9 7.5 %copy-start.4 = (bf16[16,3,64,256]{3,2,1,0:T(8,128)(2,1)}, bf16[16,3,64,256]{3,2,1,0:T(8,128)(2,1)S(1)}, u32[]{:S(2)}) copy-start(bf16[16,3,64,256]{3,2,1,0:T(8,128)(2,1)S(1)} %collective-permute-done.1.above_ref) | copy-start | bytes 4718596
  148.0 16.1 %collective-permute-start.3 = (bf16[8,3,64,256]{3,2,1,0:T(8,128)(2,1)}, bf16[8,3,64,256]{3,2,1,0:T(8,128)(2,1)S(1)}, u32[]{:S(2)}, u32[]{:S(2)}) collective-permute-start(bf16[8,3,64,256]{3,2,1,0:T(8,128)(2,1)} %slice.9), channel_id=1, source_target_pairs={{0,24},{8,0},{16,8},{24,16},{1,25},{9,1},{17,9},{25,17},{2,26},{10... | collective-permute-start | bytes 2359304 | tf_op jit(solution)/shard_map/ppermute | solution.py:121
  153.3 3.0 %copy-start.5 = (bf16[16,3,64,256]{3,2,1,0:T(8,128)(2,1)}, bf16[16,3,64,256]{3,2,1,0:T(8,128)(2,1)S(1)}, u32[]{:S(2)}) copy-start(bf16[16,3,64,256]{3,2,1,0:T(8,128)(2,1)S(1)} %collective-permute-done.below_ref) | copy-start | bytes 4718596
  154.4 16.0 %collective-permute-start.2 = (bf16[8,3,64,256]{3,2,1,0:T(8,128)(2,1)}, bf16[8,3,64,256]{3,2,1,0:T(8,128)(2,1)S(1)}, u32[]{:S(2)}, u32[]{:S(2)}) collective-permute-start(bf16[8,3,64,256]{3,2,1,0:T(8,128)(2,1)} %slice.8), channel_id=1, source_target_pairs={{0,8},{8,16},{16,24},{24,0},{1,9},{9,17},{17,25},{25,1},{2,10},{10... | collective-permute-start | bytes 2359304 | tf_op jit(solution)/shard_map/ppermute | solution.py:121
Sparse Core Ops, SparseCore 0:
  9.4 100.6 all-gather.5
  113.4 52.9 all-gather.3

commit v3 on v2

v3 whole, which is shorter than its diff:
```python
import jax
import jax.numpy as jnp
from jax import lax
from jax.experimental import pallas as pl
from jax.experimental.pallas import tpu as pltpu
from jax.sharding import Mesh, PartitionSpec as P

BF, F32 = jnp.bfloat16, jnp.float32
Z, Y, X, C = 16, 4, 4, 2
D, HEAD = 4096, 128
VMEM = pltpu.VMEM


def iota(shape, dim):
    return lax.broadcasted_iota(jnp.int32, shape, dim)


def one_hot(source, n, m):
    return jnp.where(source(iota((n, m), 0)) == iota((n, m), 1), 1.0, 0.0).astype(BF)


def pick(matrix, rows):
    return jnp.dot(matrix, rows, preferred_element_type=F32).astype(BF)


def normalize_kernel(frames_ref, gain_ref, out_ref):
    rows = frames_ref[...].reshape(128, D).astype(F32)
    scale = lax.rsqrt(jnp.mean(rows * rows, axis=-1, keepdims=True) + 1e-05)
    shuffle = one_hot(
        lambda i: ((i >> 2) & 1) * 128 + ((i >> 4) & 3) * 32 + (i >> 6) * 8 + ((i >> 3) & 1) * 4 + (i & 3), 256, 256
    )
    for j in range(4):
        cuts = [slice(2048 * half + 512 * j, 2048 * half + 512 * (j + 1)) for half in range(2)]
        normed = jnp.concatenate([(rows[:, cut] * scale * gain_ref[:, cut]).astype(BF) for cut in cuts], axis=0)
        out_ref[:, 512 * j : 512 * (j + 1)] = pick(shuffle, normed)


def route_kernel(in_ref, out_ref):
    order = one_hot(
        lambda i: ((i >> 2) & 3) * 64 + (i >> 5) * 8 + ((i >> 1) & 1) * 4 + ((i >> 4) & 1) * 2 + (i & 1), 256, 256
    )
    for j in range(4):
        cut = slice(512 * j, 512 * (j + 1))
        out_ref[:, cut] = pick(order, in_ref[:, cut])


def ready_kernel(weights_ref, out_ref):
    out_ref[...] = jnp.zeros_like(out_ref)


def spread_kernel(tokens_ref, ready_ref, out_ref):
    spread = one_hot(lambda i: ((i >> 6) & 3) * 128 + (i >> 8) * 64 + (i & 63), 512, 512)
    for half in range(2):
        order = one_hot(lambda i: (i & 63) * 4 + half * 2 + (i >> 6), 128, 256)
        for j in range(4):
            moved = pick(pick(order, tokens_ref[:, 512 * j : 512 * (j + 1)]), spread)
            for y in range(Y):
                start = 1024 * y + 128 * (4 * half + j)
                out_ref[:, start : start + 128] = moved[:, 128 * y : 128 * (y + 1)]


def attend(query, key, value, keep):
    scores = lax.dot_general(query, key, (((1,), (1,)), ((), ())), preferred_element_type=F32) * HEAD**-0.5
    scores = jnp.where(keep, scores, -jnp.inf)
    grown = jnp.exp(scores - jnp.max(scores, axis=-1, keepdims=True))
    probs = (grown / jnp.sum(grown, axis=-1, keepdims=True)).astype(BF)
    return jnp.dot(probs, value, preferred_element_type=F32).astype(BF)


def patch_kernel(y_ref, tokens_ref, own_ref, below_ref, above_ref, far_low_ref, far_high_ref, out_ref, mixed_ref):
    step = pl.program_id(0)
    y = y_ref[0]

    def slab(where, width):
        return tokens_ref[:, 0, 0, :, pl.ds(pl.multiple_of(where, 512), width)].reshape(256, width)

    pairs = (
        (slab(y * 1024, 1024), own_ref),
        (slab(((y + 3) & 3) * 1024, 1024), below_ref),
        (slab(((y + 1) & 3) * 1024, 1024), above_ref),
        (slab(((y + 2) & 3) * 1024, 512), far_low_ref),
        (slab(((y + 2) & 3) * 1024 + 512, 512), far_high_ref),
    )
    qkv = []
    for c in range(3):
        total = None
        for part, ref in pairs:
            term = jnp.dot(part, ref[:, c].reshape(ref.shape[0] * 64, 256), preferred_element_type=F32)
            total = term if total is None else total + term
        qkv.append(total.astype(BF))
    frame = lambda i: (i & 63) * 4 + (i >> 6)
    keep = frame(iota((256, 256), 1)) <= frame(iota((256, 256), 0))
    heads = [attend(*(part[:, HEAD * h : HEAD * (h + 1)] for part in qkv), keep) for h in range(2)]
    mixed_ref[step] = jnp.concatenate(heads, axis=1)

    @pl.when(step == 3)
    def _():
        order = one_hot(lambda i: (i & 15) * 16 + (i >> 4), 256, 256)
        for k in range(4):
            rows = [mixed_ref[g, 64 * f + 16 * k : 64 * f + 16 * (k + 1)] for g in range(4) for f in range(4)]
            out_ref[16 * k : 16 * (k + 1)] = pick(order, jnp.concatenate(rows, axis=0)).reshape(16, 16, 256)


def place_kernel(mixed_ref, out_ref):
    order = one_hot(
        lambda i: ((i >> 1) & 1) * 64 + ((i >> 3) & 3) * 16 + ((i >> 2) & 1) * 8 + (i & 1) * 4 + (i >> 5), 128, 128
    )
    for g in range(8):
        rows = pick(order, mixed_ref[8 * g : 8 * (g + 1)].reshape(128, 256))
        for f in range(4):
            out_ref[f, 32 * g : 32 * (g + 1)] = rows[32 * f : 32 * (f + 1)]


def whole():
    return pl.BlockSpec(memory_space=VMEM)


def call(kernel, out_shape, *operands):
    return pl.pallas_call(
        kernel,
        out_shape=jax.ShapeDtypeStruct(out_shape, BF),
        in_specs=[whole()] * len(operands),
        out_specs=whole(),
        compiler_params=pltpu.CompilerParams(vmem_limit_bytes=40 * 2**20),
    )(*operands)


def shift(x, axis, by):
    n = {"z": Z, "y": Y, "x": X, "c": C}[axis]
    return lax.ppermute(x, axis, [(i, (i + by) % n) for i in range(n)])


def project_and_attend(tokens, here, *weights):
    fixed = lambda w: pl.BlockSpec(w.shape, lambda i: (0, 0, 0, 0))
    return pl.pallas_call(
        patch_kernel,
        grid=(4,),
        out_shape=jax.ShapeDtypeStruct((64, 16, 256), BF),
        in_specs=[pl.BlockSpec(memory_space=pltpu.SMEM),
                  pl.BlockSpec((4, 1, 1, 64, D), lambda i: (0, i // 2, i % 2, 0, 0))] + [fixed(w) for w in weights],
        out_specs=pl.BlockSpec((64, 16, 256), lambda i: (0, 0, 0)),
        scratch_shapes=[VMEM((4, 256, 256), BF)],
        compiler_params=pltpu.CompilerParams(vmem_limit_bytes=48 * 2**20),
    )(here, tokens, *weights)


def shards(frames, norm_gain, w_qkv):
    weights = lax.all_gather(jnp.transpose(w_qkv, (1, 0, 2)), "z", axis=0)
    packed = call(normalize_kernel, (256, 2048), frames, norm_gain.reshape(1, D))
    spread = lax.all_to_all(packed.reshape(32, 8, 2048), ("y", "x", "c"), 0, 0, tiled=True)
    routed = call(route_kernel, (256, 2048), spread.reshape(256, 2048))
    tokens = lax.all_to_all(routed.reshape(Z, 16, 2048), "z", 0, 0, tiled=True).reshape(256, 2048)
    ready = pl.pallas_call(
        ready_kernel,
        out_shape=jax.ShapeDtypeStruct((16, 128), BF),
        in_specs=[pl.BlockSpec(memory_space=pl.ANY)],
        out_specs=whole(),
        cost_estimate=pl.CostEstimate(flops=10**11, bytes_accessed=0, transcendentals=0),
    )(weights)
    tokens = call(spread_kernel, (128, D), tokens, ready)
    below = shift(weights, "y", 1)
    above = shift(weights, "y", -1)
    far_low = shift(below[:8], "y", 1)
    far_high = shift(above[8:], "y", -1)
    gathered = lax.all_gather(tokens, ("x", "c"), axis=0).reshape(4, 2, 2, 64, D)
    here = lax.axis_index("y").astype(jnp.int32).reshape(1)
    mixed = project_and_attend(gathered, here, weights, below, above, far_low, far_high)
    mixed = lax.all_to_all(mixed, ("z", "y"), 0, 0, tiled=True)
    return call(place_kernel, (4, 256, 256), mixed)


def solution(mesh):
    grid = Mesh(mesh.devices.reshape(Z, Y, X, C), ("z", "y", "x", "c"))
    rows, columns = ("z", "y"), ("x", "c")
    return jax.shard_map(
        shards, mesh=grid, in_specs=(P(rows, columns, None), P(), P(rows, None, columns)),
        out_specs=P(rows, None, columns), check_vma=False,
    )
```

time: 261 us -> 244 us (0.935)
  waiting for transfers between devices: 125 us -> 110 us
    all_gather x1, waiting for transfers between devices: 83.9 us -> 66.5 us  [shards(): weights = lax.all_gather(jnp.transpose(w_qkv, (1, 0, 2)), 'z', axis=0)]
    pallas_call x1, Pallas kernels: 9.79 us -> 13.2 us  [project_and_attend(): pl.pallas_call(patch_kernel, grid=(4,), out_shape=jax.ShapeDtypeStruct((6...]
    all_to_all x1, blocking collectives: 45.7 us -> 42.5 us  [shards(): mixed = lax.all_to_all(mixed, ('z', 'y'), 0, 0, tiled=True)]
    ppermute x4, waiting for transfers between devices: 40.6 us -> 43.2 us  [shift(): return lax.ppermute(x, axis, [(i, (i + by) % n) for i in range(n)])]
where the time goes in v3:
time: 244 us; the launch traced here: 242 us
  waiting for transfers between devices  110 us (45%)
  blocking collectives  65.7 us (27%)
  starting transfers between devices  27.3 us (11%)
  Pallas kernels  19.9 us (8%)
  between operations  13.5 us (6%)
  local copies, waits for them, and re-layouts  4.65 us (2%)
    all_gather x1, waiting for transfers between devices, shards(): weights = lax.all_gather(jnp.transpose(w_qkv, (1, 0, 2)), 'z', axis=0)  66.5 us
    ppermute x4, waiting for transfers between devices, shift(): return lax.ppermute(x, axis, [(i, (i + by) % n) for i in range(n)])  43.2 us
    all_to_all x1, blocking collectives, shards(): mixed = lax.all_to_all(mixed, ('z', 'y'), 0, 0, tiled=True)  42.5 us
    all_to_all x1, blocking collectives, shards(): lax.all_to_all(packed.reshape(32, 8, 2048), ('y', 'x', 'c'), 0, 0, tiled=...  23.3 us
    all_to_all x1, starting transfers between devices, shards(): lax.all_to_all(routed.reshape(Z, 16, 2048), 'z', 0, 0, tiled=True)  13.9 us
    ppermute x4, starting transfers between devices, shift(): return lax.ppermute(x, axis, [(i, (i + by) % n) for i in range(n)])  13.3 us
    pallas_call x1, Pallas kernels, project_and_attend(): pl.pallas_call(patch_kernel, grid=(4,), out_shape=jax.ShapeDtypeStruct((6...  13.2 us
    pallas_call x4, Pallas kernels, call(): pl.pallas_call(kernel, out_shape=jax.ShapeDtypeStruct(out_shape, BF), in_...  6.14 us
  transfers between devices with their start and end apart: 7, of which 4 were waited for; matrix products, arithmetic and copies ran while one was open for 1% of the time, Pallas kernels for 1%

profile of v3, /device:TPU:6, one launch (start us, length us, event | category | flops | bytes accessed | tf_op | source)
XLA Modules:
  0.0 241.5 jit_solution(4672836553817817763)
XLA Ops:
  6.5 0.0 all-gather.5.cloned.1.call-start
  6.5 0.7 all-gather.5.cloned.1.call-update
  7.3 0.0 copy-start.1
  7.3 1.2 copy-done.1
  8.5 0.0 copy-start.2
  8.5 0.7 copy-done.2
  9.2 0.8 shard_map.37
  10.0 23.3 %all_to_all.15 = bf16[32,8,2048]{2,1,0:T(8,128)(2,1)S(1)} all-to-all(bf16[32,8,2048]{2,1,0:T(8,128)(2,1)S(1)} %bitcast.11), channel_id=1, replica_groups=mesh['z'=16,'y'=4,'x'=4,'c'=2] {'y','x','c'}, dimensions={0} | all-to-all | bytes 2097152 | tf_op jit(solution)/shard_map/all_to_all | solution.py:150
  33.2 1.4 shard_map.38
  34.7 13.9 %all-to-all-start.1 = ((bf16[16,16,2048]{2,1,0:T(8,128)(2,1)}), bf16[16,16,2048]{2,1,0:T(8,128)(2,1)S(1)}, u32[]{:S(2)}, u32[]{:S(2)}) async-start(bf16[16,16,2048]{2,1,0:T(8,128)(2,1)} %bitcast.4), calls=%async_computation.1 | async-start | bytes 2097152 | tf_op jit(solution)/shard_map/all_to_all | solution.py:152
  48.6 0.0 all-gather.7.cloned.1.call-start
  48.7 66.5 %all-gather.5.cloned.1.call-done = bf16[48,64,256]{2,1,0:T(8,128)(2,1)} async-done(((bf16[3,64,256]{2,1,0:T(8,128)(2,1)}), bf16[48,64,256]{2,1,0:T(8,128)(2,1)}) %all-gather.5.cloned.1.call-update) | async-done | bytes 1572880 | tf_op jit(solution)/shard_map/all_gather | solution.py:148
  115.1 0.6 shard_map.39.ready_ref
  115.7 0.0 all-to-all-done.1
  115.7 0.7 copy-done.3
  116.4 2.9 %shard_map.40 = bf16[128,4096]{1,0:T(8,128)(2,1)} custom-call(bf16[256,2048]{1,0:T(8,128)(2,1)S(1)} %bitcast.9, bf16[16,128]{1,0:T(8,128)(2,1)S(1)} %copy-done.3), custom_call_target="tpu_custom_call" | custom-call | tf_op jit(solution)/shard_map/pallas_call | solution.py:119
  119.3 0.0 all-gather.7.cloned.1.call-update
  119.3 0.0 copy-done
  119.3 3.0 %collective-permute-start.1 = (bf16[16,3,64,256]{3,2,1,0:T(8,128)(2,1)S(1)}, bf16[16,3,64,256]{3,2,1,0:T(8,128)(2,1)S(1)}, u32[]{:S(2)}, u32[]{:S(2)}) collective-permute-start(bf16[16,3,64,256]{3,2,1,0:T(8,128)(2,1)S(1)} %bitcast.13), channel_id=1, source_target_pairs={{0,24},{8,0},{16,8},{24,16},{1,25},{9,1},{17,9},{25,17},{2,26},{10... | collective-permute-start | bytes 4718600 | tf_op jit(solution)/shard_map/ppermute | solution.py:130
  122.3 2.9 %collective-permute-start = (bf16[16,3,64,256]{3,2,1,0:T(8,128)(2,1)S(1)}, bf16[16,3,64,256]{3,2,1,0:T(8,128)(2,1)S(1)}, u32[]{:S(2)}, u32[]{:S(2)}) collective-permute-start(bf16[16,3,64,256]{3,2,1,0:T(8,128)(2,1)S(1)} %bitcast.14), channel_id=1, source_target_pairs={{0,8},{8,16},{16,24},{24,0},{1,9},{9,17},{17,25},{25,1},{2,10},{10... | collective-permute-start | bytes 4718600 | tf_op jit(solution)/shard_map/ppermute | solution.py:130
  125.2 27.1 %collective-permute-done.1.above_ref = bf16[16,3,64,256]{3,2,1,0:T(8,128)(2,1)S(1)} collective-permute-done((bf16[16,3,64,256]{3,2,1,0:T(8,128)(2,1)S(1)}, bf16[16,3,64,256]{3,2,1,0:T(8,128)(2,1)S(1)}, u32[]{:S(2)}, u32[]{:S(2)}) %collective-permute-start.1) | collective-permute-done | bytes 1572896 | tf_op jit(solution)/shard_map/ppermute | solution.py:130
  152.3 1.1 slice.9
  153.4 5.6 %collective-permute-start.3 = (bf16[8,3,64,256]{3,2,1,0:T(8,128)(2,1)}, bf16[8,3,64,256]{3,2,1,0:T(8,128)(2,1)}, u32[]{:S(2)}, u32[]{:S(2)}) collective-permute-start(bf16[8,3,64,256]{3,2,1,0:T(8,128)(2,1)} %slice.9), channel_id=1, source_target_pairs={{0,24},{8,0},{16,8},{24,16},{1,25},{9,1},{17,9},{25,17},{2,26},{10... | collective-permute-start | bytes 2359304 | tf_op jit(solution)/shard_map/ppermute | solution.py:130
  159.0 0.0 collective-permute-done.below_ref
  159.0 0.9 slice.8
  160.0 0.0 copy-done.4
  160.0 1.9 collective-permute-start.2
  161.9 9.8 %collective-permute-done.3.far_high_ref = bf16[8,3,64,256]{3,2,1,0:T(8,128)(2,1)} collective-permute-done((bf16[8,3,64,256]{3,2,1,0:T(8,128)(2,1)}, bf16[8,3,64,256]{3,2,1,0:T(8,128)(2,1)}, u32[]{:S(2)}, u32[]{:S(2)}) %collective-permute-start.3) | collective-permute-done | bytes 786464 | tf_op jit(solution)/shard_map/ppermute | solution.py:130
  171.7 6.3 %collective-permute-done.2.far_low_ref = bf16[8,3,64,256]{3,2,1,0:T(8,128)(2,1)} collective-permute-done((bf16[8,3,64,256]{3,2,1,0:T(8,128)(2,1)}, bf16[8,3,64,256]{3,2,1,0:T(8,128)(2,1)}, u32[]{:S(2)}, u32[]{:S(2)}) %collective-permute-start.2) | collective-permute-done | bytes 786464 | tf_op jit(solution)/shard_map/ppermute | solution.py:130
  178.0 13.2 %shard_map.41 = bf16[64,16,256]{2,1,0:T(8,128)(2,1)S(1)} custom-call(s32[1]{0:T(128)} %bitcast.y_ref, bf16[4,2,2,64,4096]{4,3,2,1,0:T(8,128)(2,1)} %bitcast.17, bf16[16,3,64,256]{3,2,1,0:T(8,128)(2,1)S(1)} %bitcast.15, bf16[16,3,64,256]{3,2,1,0:T(8,128)(2,1)S(1)} %collective-permute-done.below_ref, bf16[16,3,64,256]{3,2,1,0:T(8,128)(2,1)} %copy-done.4, ...), custom_call_target="tpu_custom_call" | custom-call | tf_op jit(solution)/shard_map/pallas_call | solution.py:135
  191.2 42.5 %all_to_all.16.mixed_ref = bf16[64,16,256]{2,1,0:T(8,128)(2,1)S(1)} all-to-all(bf16[64,16,256]{2,1,0:T(8,128)(2,1)S(1)} %shard_map.41), channel_id=1, replica_groups=mesh['z'=16,'y'=4,'x'=4,'c'=2] {'z','y'}, dimensions={0} | all-to-all | bytes 1048576 | tf_op jit(solution)/shard_map/all_to_all | solution.py:168
  233.6 1.1 shard_map.42
  (4 shorter events, 0.0 us)
Async XLA Ops:
  6.5 108.6 %all-gather.5.cloned.1.call-start = ((), (), s32[]{:S(2)}) async-start(), calls=%async_computation.3 | async-start | bytes 1671168 | tf_op jit(solution)/shard_map/all_gather | solution.py:148
  7.3 1.2 copy-start.1
  8.5 0.7 copy-start.2
  34.7 81.1 %all-to-all-start.1 = ((bf16[16,16,2048]{2,1,0:T(8,128)(2,1)}), bf16[16,16,2048]{2,1,0:T(8,128)(2,1)S(1)}, u32[]{:S(2)}, u32[]{:S(2)}) async-start(bf16[16,16,2048]{2,1,0:T(8,128)(2,1)} %bitcast.4), calls=%async_computation.1 | async-start | bytes 2097152 | tf_op jit(solution)/shard_map/all_to_all | solution.py:152
  48.6 129.4 %all-gather.7.cloned.1.call-start = ((), (), s32[]{:S(2)}) async-start(), calls=%async_computation.4 | async-start | bytes 9437184 | tf_op jit(solution)/shard_map/all_gather | solution.py:165
  115.7 0.7 copy-start.3
  116.4 2.9 %copy-start = (bf16[48,64,256]{2,1,0:T(8,128)(2,1)S(1)}, bf16[48,64,256]{2,1,0:T(8,128)(2,1)}, u32[]{:S(2)}) copy-start(bf16[48,64,256]{2,1,0:T(8,128)(2,1)} %all-gather.5.cloned.1.call-done) | copy-start | bytes 4718596
  119.3 33.0 %collective-permute-start.1 = (bf16[16,3,64,256]{3,2,1,0:T(8,128)(2,1)S(1)}, bf16[16,3,64,256]{3,2,1,0:T(8,128)(2,1)S(1)}, u32[]{:S(2)}, u32[]{:S(2)}) collective-permute-start(bf16[16,3,64,256]{3,2,1,0:T(8,128)(2,1)S(1)} %bitcast.13), channel_id=1, source_target_pairs={{0,24},{8,0},{16,8},{24,16},{1,25},{9,1},{17,9},{25,17},{2,26},{10... | collective-permute-start | bytes 4718600 | tf_op jit(solution)/shard_map/ppermute | solution.py:130
  122.3 36.7 %collective-permute-start = (bf16[16,3,64,256]{3,2,1,0:T(8,128)(2,1)S(1)}, bf16[16,3,64,256]{3,2,1,0:T(8,128)(2,1)S(1)}, u32[]{:S(2)}, u32[]{:S(2)}) collective-permute-start(bf16[16,3,64,256]{3,2,1,0:T(8,128)(2,1)S(1)} %bitcast.14), channel_id=1, source_target_pairs={{0,8},{8,16},{16,24},{24,0},{1,9},{9,17},{17,25},{25,1},{2,10},{10... | collective-permute-start | bytes 4718600 | tf_op jit(solution)/shard_map/ppermute | solution.py:130
  152.3 7.6 %copy-start.4 = (bf16[16,3,64,256]{3,2,1,0:T(8,128)(2,1)}, bf16[16,3,64,256]{3,2,1,0:T(8,128)(2,1)S(1)}, u32[]{:S(2)}) copy-start(bf16[16,3,64,256]{3,2,1,0:T(8,128)(2,1)S(1)} %collective-permute-done.1.above_ref) | copy-start | bytes 4718596
  153.4 18.3 %collective-permute-start.3 = (bf16[8,3,64,256]{3,2,1,0:T(8,128)(2,1)}, bf16[8,3,64,256]{3,2,1,0:T(8,128)(2,1)}, u32[]{:S(2)}, u32[]{:S(2)}) collective-permute-start(bf16[8,3,64,256]{3,2,1,0:T(8,128)(2,1)} %slice.9), channel_id=1, source_target_pairs={{0,24},{8,0},{16,8},{24,16},{1,25},{9,1},{17,9},{25,17},{2,26},{10... | collective-permute-start | bytes 2359304 | tf_op jit(solution)/shard_map/ppermute | solution.py:130
  160.0 18.0 %collective-permute-start.2 = (bf16[8,3,64,256]{3,2,1,0:T(8,128)(2,1)}, bf16[8,3,64,256]{3,2,1,0:T(8,128)(2,1)}, u32[]{:S(2)}, u32[]{:S(2)}) collective-permute-start(bf16[8,3,64,256]{3,2,1,0:T(8,128)(2,1)} %slice.8), channel_id=1, source_target_pairs={{0,8},{8,16},{16,24},{24,0},{1,9},{9,17},{17,25},{25,1},{2,10},{10... | collective-permute-start | bytes 2359304 | tf_op jit(solution)/shard_map/ppermute | solution.py:130
Sparse Core Ops, SparseCore 0:
  9.4 105.6 all-gather.4
  119.4 52.1 all-gather.6

commit v4 on v0

v4 whole, which is shorter than its diff:
```python
import jax
import jax.numpy as jnp
from jax import lax
from jax.experimental import pallas as pl
from jax.experimental.pallas import tpu as pltpu
from jax.sharding import Mesh, PartitionSpec as P

BF, F32 = jnp.bfloat16, jnp.float32
Z, Y, X, C = 16, 4, 4, 2
D, HEAD = 4096, 128
VMEM = pltpu.VMEM


def iota(shape, dim):
    return lax.broadcasted_iota(jnp.int32, shape, dim)


def one_hot(source, n, m):
    return jnp.where(source(iota((n, m), 0)) == iota((n, m), 1), 1.0, 0.0).astype(BF)


def pick(matrix, rows):
    return jnp.dot(matrix, rows, preferred_element_type=F32).astype(BF)


def normalize_kernel(frames_ref, gain_ref, out_ref):
    rows = frames_ref[...].reshape(128, D).astype(F32)
    scale = lax.rsqrt(jnp.mean(rows * rows, axis=-1, keepdims=True) + 1e-05)
    shuffle = one_hot(lambda i: (((i >> 4) & 1) * 2 + (i & 1)) * 32 + (i >> 5) * 8 + ((i >> 1) & 7), 128, 128)
    for j in range(8):
        cut = slice(512 * j, 512 * (j + 1))
        out_ref[:, cut] = pick(shuffle, (rows[:, cut] * scale * gain_ref[:, cut]).astype(BF))


def route_kernel(in_ref, out_ref):
    order = one_hot(lambda i: ((i >> 1) & 3) * 32 + (i >> 3) * 2 + (i & 1), 128, 128)
    for j in range(8):
        cut = slice(512 * j, 512 * (j + 1))
        out_ref[:, cut] = pick(order, in_ref[:, cut])


def stack_kernel(low_ref, high_ref, after_ref, out_ref):
    out_ref[:64] = low_ref[...]
    out_ref[64:] = high_ref[...]


def project(token_refs, weights_ref):
    totals = [None] * 3
    for k in range(4):
        cut = slice(1024 * k, 1024 * (k + 1))
        part = jnp.concatenate([ref[:, cut] for ref in token_refs], axis=0)
        for c in range(3):
            weights = weights_ref[4 * k : 4 * (k + 1), :, c].reshape(1024, 256)
            term = jnp.dot(part, weights, preferred_element_type=F32)
            totals[c] = term if totals[c] is None else totals[c] + term
    return [total.astype(BF) for total in totals]


def attend(qkv, patches, core):
    def frame(i):
        return ((i & 127) >> 1) * 4 + ((i >> 7) ^ core) * 2 + (i & 1)

    keep = frame(iota((256, 256), 1)) <= frame(iota((256, 256), 0))
    scale = HEAD**-0.5 * 1.4426950408889634
    across = (((1,), (1,)), ((), ()))
    mixed = []
    for p in range(patches):
        units = [[part[256 * p : 256 * (p + 1), HEAD * h : HEAD * (h + 1)] for part in qkv] for h in range(2)]
        scores = [lax.dot_general(q, k, across, preferred_element_type=F32) * scale for q, k, _ in units]
        scores = [jnp.where(keep, s, -jnp.inf) for s in scores]
        grown = [jnp.exp2(s - jnp.max(s, axis=-1, keepdims=True)) for s in scores]
        probs = [(g * (1.0 / jnp.sum(g, axis=-1, keepdims=True))).astype(BF) for g in grown]
        heads = [jnp.dot(w, v, preferred_element_type=F32).astype(BF) for w, (_, _, v) in zip(probs, units)]
        mixed.append(jnp.concatenate(heads, axis=1))
    return mixed


def near_kernel(place_ref, *refs):
    *token_refs, weights_ref, out_ref = refs
    for p, mixed in enumerate(attend(project(token_refs, weights_ref), 3, place_ref[1])):
        out_ref[256 * p : 256 * (p + 1)] = mixed


def far_kernel(place_ref, near_ref, far_ref, other_far_ref, weights_ref, out_ref):
    core = place_ref[1]
    (far,) = attend(project((far_ref, other_far_ref), weights_ref), 1, core)
    def source(i):
        return ((i >> 2) & 3) * 64 + (((i >> 1) & 1) ^ core) * 32 + (i >> 4) * 2 + (i & 1)

    order = one_hot(source, 256, 256)
    for k in range(4):
        cuts = [near_ref[128 * g + 32 * k : 128 * g + 32 * (k + 1)] for g in range(6)]
        cuts += [far[128 * g + 32 * k : 128 * g + 32 * (k + 1)] for g in range(2)]
        out_ref[16 * k : 16 * (k + 1)] = pick(order, jnp.concatenate(cuts, axis=0)).reshape(16, 16, 256)


def place_kernel(place_ref, mixed_ref, out_ref):
    def source(i):
        ahead = (((i >> 5) & 3) - place_ref[0]) & 3
        slot = jnp.where(ahead == 0, 0, jnp.where(ahead == 3, 1, ahead + 1))
        return (i & 7) * 64 + ((i >> 3) & 3) * 16 + slot * 4 + (i >> 7)

    order = one_hot(source, 512, 512)
    for core in range(C):
        rows = pick(order, mixed_ref[32 * core : 32 * (core + 1)].reshape(512, 256))
        for f in range(4):
            for x in range(X):
                out_ref[f, 64 * x + 32 * core : 64 * x + 32 * (core + 1)] = rows[128 * f + 32 * x : 128 * f + 32 * (x + 1)]


def call(kernel, out_shape, *operands, flops=10**7, far=()):
    def spec(i, operand):
        return pl.BlockSpec(memory_space=pltpu.SMEM if operand.dtype == jnp.int32 else pl.ANY if i in far else VMEM)

    return pl.pallas_call(
        kernel,
        out_shape=jax.ShapeDtypeStruct(out_shape, BF),
        in_specs=[spec(i, operand) for i, operand in enumerate(operands)],
        out_specs=pl.BlockSpec(memory_space=VMEM),
        compiler_params=pltpu.CompilerParams(vmem_limit_bytes=40 * 2**20),
        cost_estimate=pl.CostEstimate(flops=flops, bytes_accessed=2**21, transcendentals=0),
    )(*operands)


def shift(x, axis, by):
    n = {"z": Z, "y": Y, "x": X, "c": C}[axis]
    return lax.ppermute(x, axis, [(i, (i + by) % n) for i in range(n)])


def shards(frames, norm_gain, w_qkv):
    weights = jnp.broadcast_to(jnp.transpose(w_qkv, (1, 0, 2)), (Y, 3, 64, 256))
    weights = lax.all_to_all(weights, "y", 0, 0, tiled=True)
    weights = lax.all_gather(weights, "z", axis=0)
    packed = call(normalize_kernel, (128, D), frames, norm_gain.reshape(1, D))
    spread = lax.all_to_all(packed.reshape(8, 16, D), ("y", "c"), 0, 0, tiled=True).reshape(128, D)
    routed = call(route_kernel, (128, D), spread)
    own = lax.all_to_all(routed.reshape(Z, 8, D), "z", 0, 0, tiled=True).reshape(128, D)
    left = shift(own, "x", 1)
    right = shift(own, "x", -1)
    far_low = shift(left[:64], "x", 1)
    far_high = shift(right[64:], "x", -1)
    place = jnp.stack([lax.axis_index("x"), lax.axis_index("c")]).astype(jnp.int32)
    pairs = [part for mine in (own, left, right) for part in (mine, shift(mine, "c", 1))]
    near = call(near_kernel, (768, 256), place, *pairs, weights, flops=6 * 10**9)
    far = call(stack_kernel, (128, D), far_low, far_high, near, far=(2,))
    mixed = call(far_kernel, (64, 16, 256), place, near, far, shift(far, "c", 1), weights, flops=2 * 10**9)
    mixed = lax.all_to_all(mixed, ("z", "y"), 0, 0, tiled=True)
    return call(place_kernel, (4, 256, 256), place, mixed)


def solution(mesh):
    grid = Mesh(mesh.devices.reshape(Z, Y, X, C), ("z", "y", "x", "c"))
    rows, columns = ("z", "y"), ("x", "c")
    return jax.shard_map(
        shards, mesh=grid, in_specs=(P(rows, columns, None), P(), P(rows, None, columns)),
        out_specs=P(rows, None, columns), check_vma=False,
    )
```

time: 392 us -> 232 us (0.59)
  waiting for transfers between devices: 204 us -> 21.3 us
  blocking collectives: 132 us -> 153 us
  starting transfers between devices: 0.04 us -> 19.3 us
  other arithmetic: 15.4 us -> 0.08 us
  Pallas kernels: 0 us -> 15.3 us
  matrix products: 12.6 us -> 0 us
  local copies, waits for them, and re-layouts: 13.3 us -> 8.35 us
    all_gather x2 -> x1, waiting for transfers between devices: 202 us -> 0.02 us  [shards(): weights = lax.all_gather(weights, 'z', axis=0)]
    ppermute x0 -> x8, waiting for transfers between devices: none -> 21.3 us  [shift(): return lax.ppermute(x, axis, [(i, (i + by) % n) for i in range(n)])]
    all_to_all x2 -> x4, blocking collectives: 132 us -> 153 us  [the longest x1 75.8 us: shards(): lax.all_to_all(routed.reshape(Z, 8, D), 'z', 0, 0, tiled=True)]
    ppermute x0 -> x8, starting transfers between devices: none -> 19.3 us  [shift(): return lax.ppermute(x, axis, [(i, (i + by) % n) for i in range(n)])]
    pallas_call x0 -> x6, Pallas kernels: none -> 15.3 us  [call(): pl.pallas_call(kernel, out_shape=jax.ShapeDtypeStruct(out_shape, BF), in_...]
    dot_general x2 -> x0, matrix products: 11.9 us -> none  [the longest x1 11 us: shards(): jnp.dot(token_rows, flat_weights, preferred_element_type=jnp.float32)]
    convert_element_type x1 -> x0, other arithmetic: 10.3 us -> none  [normalize(): (widened * lax.rsqrt(mean_square + 1e-05) * norm_gain).astype(jnp.bfloat16)]
    all_gather x1 -> x0, local copies, waits for them, and re-layouts: 8.78 us -> none  [shards(): all_weights = lax.all_gather(w_qkv, 'tm', axis=0, tiled=True)]
  transfers between devices with their start and end apart: 2 -> 9, of which waited for: 2 -> 4; matrix products, arithmetic and copies ran while one was open for 2% -> 1% of each run, Pallas kernels for 0% -> 4%
where the time goes in v4:
time: 232 us; the launch traced here: 231 us
  blocking collectives  153 us (66%)
  waiting for transfers between devices  21.3 us (9%)
  starting transfers between devices  19.3 us (8%)
  Pallas kernels  15.3 us (7%)
  between operations  13.6 us (6%)
  local copies, waits for them, and re-layouts  8.35 us (4%)
    all_to_all x1, blocking collectives, shards(): lax.all_to_all(routed.reshape(Z, 8, D), 'z', 0, 0, tiled=True)  75.8 us
    all_to_all x1, blocking collectives, shards(): mixed = lax.all_to_all(mixed, ('z', 'y'), 0, 0, tiled=True)  46.2 us
    ppermute x8, waiting for transfers between devices, shift(): return lax.ppermute(x, axis, [(i, (i + by) % n) for i in range(n)])  21.3 us
    ppermute x8, starting transfers between devices, shift(): return lax.ppermute(x, axis, [(i, (i + by) % n) for i in range(n)])  19.3 us
    all_to_all x1, blocking collectives, shards(): lax.all_to_all(packed.reshape(8, 16, D), ('y', 'c'), 0, 0, tiled=True)  18.5 us
    pallas_call x6, Pallas kernels, call(): pl.pallas_call(kernel, out_shape=jax.ShapeDtypeStruct(out_shape, BF), in_...  15.3 us
    all_to_all x1, blocking collectives, shards(): weights = lax.all_to_all(weights, 'y', 0, 0, tiled=True)  12.4 us
    unnamed x8, local copies, waits for them, and re-layouts  4.72 us
  transfers between devices with their start and end apart: 9, of which 4 were waited for; matrix products, arithmetic and copies ran while one was open for 1% of the time, Pallas kernels for 4%

profile of v4, /device:TPU:6, one launch (start us, length us, event | category | flops | bytes accessed | tf_op | source)
XLA Modules:
  0.0 230.9 jit_solution(5740247453689937871)
XLA Ops:
  6.5 0.9 broadcast_in_dim.3
  7.5 12.4 %all_to_all.20 = bf16[4,3,64,256]{3,2,1,0:T(8,128)(2,1)} all-to-all(bf16[4,3,64,256]{3,2,1,0:T(8,128)(2,1)S(1)} %broadcast_in_dim.3), channel_id=1, replica_groups=mesh['z'=16,'y'=4,'x'=4,'c'=2] {'y'}, dimensions={0} | all-to-all | bytes 786432 | tf_op jit(solution)/shard_map/all_to_all | solution.py:132
  19.9 0.0 all-gather.3.cloned.1.call-update
  19.9 0.0 copy-start.2
  19.9 1.2 copy-done.2
  21.2 0.7 copy-done.3
  21.9 0.7 shard_map.37
  22.6 18.5 %all_to_all.21 = bf16[8,16,4096]{2,1,0:T(8,128)(2,1)S(1)} all-to-all(bf16[8,16,4096]{2,1,0:T(8,128)(2,1)S(1)} %bitcast.13), channel_id=1, replica_groups=mesh['z'=16,'y'=4,'x'=4,'c'=2] {'y','c'}, dimensions={0} | all-to-all | bytes 2097152 | tf_op jit(solution)/shard_map/all_to_all | solution.py:135
  41.1 0.4 shard_map.38
  41.6 75.8 %all_to_all.22 = bf16[16,8,4096]{2,1,0:T(8,128)(2,1)S(1)} all-to-all(bf16[16,8,4096]{2,1,0:T(8,128)(2,1)S(1)} %bitcast.12), channel_id=1, replica_groups=mesh['z'=16,'y'=4,'x'=4,'c'=2] {'z'}, dimensions={0} | all-to-all | bytes 2097152 | tf_op jit(solution)/shard_map/all_to_all | solution.py:137
  117.3 2.3 collective-permute-start.1
  119.6 3.5 %collective-permute-start.3 = (bf16[128,4096]{1,0:T(8,128)(2,1)S(1)}, bf16[128,4096]{1,0:T(8,128)(2,1)}, u32[]{:S(2)}, u32[]{:S(2)}) collective-permute-start(bf16[128,4096]{1,0:T(8,128)(2,1)S(1)} %bitcast.15), channel_id=1, source_target_pairs={{0,6},{2,0},{4,2},{6,4},{1,7},{3,1},{5,3},{7,5},{8,14},{10,8},{12,... | collective-permute-start | bytes 3145736 | tf_op jit(solution)/shard_map/ppermute | solution.py:127
  123.2 1.9 collective-permute-start
  125.1 15.2 %collective-permute-done.1.refs_2_ = bf16[128,4096]{1,0:T(8,128)(2,1)S(1)} collective-permute-done((bf16[128,4096]{1,0:T(8,128)(2,1)S(1)}, bf16[128,4096]{1,0:T(8,128)(2,1)S(1)}, u32[]{:S(2)}, u32[]{:S(2)}) %collective-permute-start.1) | collective-permute-done | bytes 1048608 | tf_op jit(solution)/shard_map/ppermute | solution.py:127
  140.3 1.9 collective-permute-start.2
  142.3 1.5 collective-permute-done.3.refs_4_
  143.8 1.9 collective-permute-start.4
  145.7 0.1 pad_add_fusion.place_ref
  145.8 0.8 slice.8
  146.6 2.6 %collective-permute-start.5 = (bf16[64,4096]{1,0:T(8,128)(2,1)}, bf16[64,4096]{1,0:T(8,128)(2,1)S(1)}, u32[]{:S(2)}, u32[]{:S(2)}) collective-permute-start(bf16[64,4096]{1,0:T(8,128)(2,1)} %slice.8), channel_id=1, source_target_pairs={{0,2},{2,4},{4,6},{6,0},{1,3},{3,5},{5,7},{7,1},{8,10},{10,12},{12... | collective-permute-start | bytes 1572872 | tf_op jit(solution)/shard_map/ppermute | solution.py:127
  149.2 1.9 slice.9
  151.1 3.2 %collective-permute-start.6 = (bf16[64,4096]{1,0:T(8,128)(2,1)}, bf16[64,4096]{1,0:T(8,128)(2,1)S(1)}, u32[]{:S(2)}, u32[]{:S(2)}) collective-permute-start(bf16[64,4096]{1,0:T(8,128)(2,1)} %slice.9), channel_id=1, source_target_pairs={{0,6},{2,0},{4,2},{6,4},{1,7},{3,1},{5,3},{7,5},{8,14},{10,8},{12,... | collective-permute-start | bytes 1572872 | tf_op jit(solution)/shard_map/ppermute | solution.py:127
  154.3 0.0 all-gather.3.cloned.1.call-done
  154.4 2.8 %copy-done = bf16[64,3,64,256]{3,2,1,0:T(8,128)(2,1)S(1)} copy-done((bf16[64,3,64,256]{3,2,1,0:T(8,128)(2,1)S(1)}, bf16[64,3,64,256]{3,2,1,0:T(8,128)(2,1)}, u32[]{:S(2)}) %copy-start) | copy-done | bytes 6291480
  157.1 9.0 %shard_map.39.after_ref.near_ref = bf16[768,256]{1,0:T(8,128)(2,1)S(1)} custom-call(s32[2]{0:T(128)S(1)} %pad_add_fusion.place_ref, bf16[128,4096]{1,0:T(8,128)(2,1)S(1)} %bitcast.17, bf16[128,4096]{1,0:T(8,128)(2,1)} %collective-permute-done.refs_1_, bf16[128,4096]{1,0:T(8,128)(2,1)S(1)} %collective-permute-done.1.refs_2_, ...), custom_call_target="tpu_custom_call" | custom-call | flops 6000000000 | bytes 2097152 | tf_op jit(solution)/shard_map/pallas_call | solution.py:115
  166.1 1.9 collective-permute-done.6.high_ref
  168.0 0.1 shard_map.40.far_ref
  168.1 1.9 collective-permute-start.7
  170.0 2.6 %collective-permute-done.7.other_far_ref = bf16[128,4096]{1,0:T(8,128)(2,1)S(1)} collective-permute-done((bf16[128,4096]{1,0:T(8,128)(2,1)S(1)}, bf16[128,4096]{1,0:T(8,128)(2,1)S(1)}, u32[]{:S(2)}, u32[]{:S(2)}) %collective-permute-start.7) | collective-permute-done | bytes 1048608 | tf_op jit(solution)/shard_map/ppermute | solution.py:127
  172.6 3.3 %shard_map.41 = bf16[64,16,256]{2,1,0:T(8,128)(2,1)S(1)} custom-call(s32[2]{0:T(128)S(1)} %pad_add_fusion.place_ref, bf16[768,256]{1,0:T(8,128)(2,1)S(1)} %shard_map.39.after_ref.near_ref, bf16[128,4096]{1,0:T(8,128)(2,1)S(1)} %shard_map.40.far_ref, bf16[128,4096]{1,0:T(8,128)(2,1)S(1)} %collective-permute-done.7.other_far_ref, ...), custom_call_target="tpu_custom_call" | custom-call | flops 2000000000 | bytes 2097152 | tf_op jit(solution)/shard_map/pallas_call | solution.py:115
  176.0 46.2 %all_to_all.23.mixed_ref = bf16[64,16,256]{2,1,0:T(8,128)(2,1)S(1)} all-to-all(bf16[64,16,256]{2,1,0:T(8,128)(2,1)S(1)} %shard_map.41), channel_id=1, replica_groups=mesh['z'=16,'y'=4,'x'=4,'c'=2] {'z','y'}, dimensions={0} | all-to-all | bytes 1048576 | tf_op jit(solution)/shard_map/all_to_all | solution.py:147
  222.2 1.8 shard_map.42
  (9 shorter events, 0.0 us)
Async XLA Ops:
  6.5 147.8 %all-gather.3.cloned.1.call-start = ((), (), s32[]{:S(2)}) async-start(), calls=%async_computation.4 | async-start | bytes 6684672 | tf_op jit(solution)/shard_map/all_gather | solution.py:133
  19.9 1.2 copy-start.2
  21.2 0.7 copy-start.3
  117.3 23.0 %collective-permute-start.1 = (bf16[128,4096]{1,0:T(8,128)(2,1)S(1)}, bf16[128,4096]{1,0:T(8,128)(2,1)S(1)}, u32[]{:S(2)}, u32[]{:S(2)}) collective-permute-start(bf16[128,4096]{1,0:T(8,128)(2,1)S(1)} %bitcast.14), channel_id=1, source_target_pairs={{0,2},{2,4},{4,6},{6,0},{1,3},{3,5},{5,7},{7,1},{8,10},{10,12},{12... | collective-permute-start | bytes 3145736 | tf_op jit(solution)/shard_map/ppermute | solution.py:127
  119.6 24.1 %collective-permute-start.3 = (bf16[128,4096]{1,0:T(8,128)(2,1)S(1)}, bf16[128,4096]{1,0:T(8,128)(2,1)}, u32[]{:S(2)}, u32[]{:S(2)}) collective-permute-start(bf16[128,4096]{1,0:T(8,128)(2,1)S(1)} %bitcast.15), channel_id=1, source_target_pairs={{0,6},{2,0},{4,2},{6,4},{1,7},{3,1},{5,3},{7,5},{8,14},{10,8},{12,... | collective-permute-start | bytes 3145736 | tf_op jit(solution)/shard_map/ppermute | solution.py:127
  123.2 31.1 %collective-permute-start = (bf16[128,4096]{1,0:T(8,128)(2,1)S(1)}, bf16[128,4096]{1,0:T(8,128)(2,1)}, u32[]{:S(2)}, u32[]{:S(2)}) collective-permute-start(bf16[128,4096]{1,0:T(8,128)(2,1)S(1)} %bitcast.16), channel_id=1, source_target_pairs={{0,1},{1,0},{2,3},{3,2},{4,5},{5,4},{6,7},{7,6},{8,9},{9,8},{10,11... | collective-permute-start | bytes 3145736 | tf_op jit(solution)/shard_map/ppermute | solution.py:127
  140.3 14.0 %collective-permute-start.2 = (bf16[128,4096]{1,0:T(8,128)(2,1)S(1)}, bf16[128,4096]{1,0:T(8,128)(2,1)}, u32[]{:S(2)}, u32[]{:S(2)}) collective-permute-start(bf16[128,4096]{1,0:T(8,128)(2,1)S(1)} %collective-permute-done.1.refs_2_), channel_id=1, source_target_pairs={{0,1},{1,0},{2,3},{3,2},{4,5},{5,4},{6,7},{7,6},{8,9},{9,8},{10,11... | collective-permute-start | bytes 3145736 | tf_op jit(solution)/shard_map/ppermute | solution.py:127
  143.8 10.6 %collective-permute-start.4 = (bf16[128,4096]{1,0:T(8,128)(2,1)}, bf16[128,4096]{1,0:T(8,128)(2,1)}, u32[]{:S(2)}, u32[]{:S(2)}) collective-permute-start(bf16[128,4096]{1,0:T(8,128)(2,1)} %collective-permute-done.3.refs_4_), channel_id=1, source_target_pairs={{0,1},{1,0},{2,3},{3,2},{4,5},{5,4},{6,7},{7,6},{8,9},{9,8},{10,11... | collective-permute-start | bytes 3145736 | tf_op jit(solution)/shard_map/ppermute | solution.py:127
  146.6 19.5 %collective-permute-start.5 = (bf16[64,4096]{1,0:T(8,128)(2,1)}, bf16[64,4096]{1,0:T(8,128)(2,1)S(1)}, u32[]{:S(2)}, u32[]{:S(2)}) collective-permute-start(bf16[64,4096]{1,0:T(8,128)(2,1)} %slice.8), channel_id=1, source_target_pairs={{0,2},{2,4},{4,6},{6,0},{1,3},{3,5},{5,7},{7,1},{8,10},{10,12},{12... | collective-permute-start | bytes 1572872 | tf_op jit(solution)/shard_map/ppermute | solution.py:127
  151.1 16.9 %collective-permute-start.6 = (bf16[64,4096]{1,0:T(8,128)(2,1)}, bf16[64,4096]{1,0:T(8,128)(2,1)S(1)}, u32[]{:S(2)}, u32[]{:S(2)}) collective-permute-start(bf16[64,4096]{1,0:T(8,128)(2,1)} %slice.9), channel_id=1, source_target_pairs={{0,6},{2,0},{4,2},{6,4},{1,7},{3,1},{5,3},{7,5},{8,14},{10,8},{12,... | collective-permute-start | bytes 1572872 | tf_op jit(solution)/shard_map/ppermute | solution.py:127
  154.4 2.8 %copy-start = (bf16[64,3,64,256]{3,2,1,0:T(8,128)(2,1)S(1)}, bf16[64,3,64,256]{3,2,1,0:T(8,128)(2,1)}, u32[]{:S(2)}) copy-start(bf16[64,3,64,256]{3,2,1,0:T(8,128)(2,1)} %all-gather.3.cloned.1.call-done) | copy-start | bytes 18874372
  157.1 15.5 %copy-start.1 = (bf16[64,3,64,256]{3,2,1,0:T(8,128)(2,1)S(1)}, bf16[64,3,64,256]{3,2,1,0:T(8,128)(2,1)}, u32[]{:S(2)}) copy-start(bf16[64,3,64,256]{3,2,1,0:T(8,128)(2,1)} %all-gather.3.cloned.1.call-done) | copy-start | bytes 18874372
  168.1 4.6 %collective-permute-start.7 = (bf16[128,4096]{1,0:T(8,128)(2,1)S(1)}, bf16[128,4096]{1,0:T(8,128)(2,1)S(1)}, u32[]{:S(2)}, u32[]{:S(2)}) collective-permute-start(bf16[128,4096]{1,0:T(8,128)(2,1)S(1)} %shard_map.40.far_ref), channel_id=1, source_target_pairs={{0,1},{1,0},{2,3},{3,2},{4,5},{5,4},{6,7},{7,6},{8,9},{9,8},{10,11... | collective-permute-start | bytes 3145736 | tf_op jit(solution)/shard_map/ppermute | solution.py:127
Sparse Core Ops, SparseCore 0:
  20.1 133.6 all-gather.2

commit v5 on v4

--- a/solution.py
+++ b/solution.py
@@ -39,9 +39,8 @@
         out_ref[:, cut] = pick(order, in_ref[:, cut])
 
 
-def stack_kernel(low_ref, high_ref, after_ref, out_ref):
-    out_ref[:64] = low_ref[...]
-    out_ref[64:] = high_ref[...]
+def hold_kernel(*refs):
+    pass
 
 
 def project(token_refs, weights_ref):
@@ -77,11 +76,11 @@
 
 def near_kernel(place_ref, *refs):
     *token_refs, weights_ref, out_ref = refs
-    for p, mixed in enumerate(attend(project(token_refs, weights_ref), 3, place_ref[1])):
+    for p, mixed in enumerate(attend(project(token_refs, weights_ref), len(token_refs) // 2, place_ref[1])):
         out_ref[256 * p : 256 * (p + 1)] = mixed
 
 
-def far_kernel(place_ref, near_ref, far_ref, other_far_ref, weights_ref, out_ref):
+def far_kernel(place_ref, first_ref, near_ref, far_ref, other_far_ref, weights_ref, out_ref):
     core = place_ref[1]
     (far,) = attend(project((far_ref, other_far_ref), weights_ref), 1, core)
     def source(i):
@@ -89,42 +88,54 @@
 
     order = one_hot(source, 256, 256)
     for k in range(4):
-        cuts = [near_ref[128 * g + 32 * k : 128 * g + 32 * (k + 1)] for g in range(6)]
-        cuts += [far[128 * g + 32 * k : 128 * g + 32 * (k + 1)] for g in range(2)]
+        cuts = [
+            part[128 * g + 32 * k : 128 * g + 32 * (k + 1)]
+            for part, halves in ((first_ref, 2), (near_ref, 4), (far, 2)) for g in range(halves)
+        ]
         out_ref[16 * k : 16 * (k + 1)] = pick(order, jnp.concatenate(cuts, axis=0)).reshape(16, 16, 256)
 
 
 def place_kernel(place_ref, mixed_ref, out_ref):
     def source(i):
-        ahead = (((i >> 5) & 3) - place_ref[0]) & 3
-        slot = jnp.where(ahead == 0, 0, jnp.where(ahead == 3, 1, ahead + 1))
-        return (i & 7) * 64 + ((i >> 3) & 3) * 16 + slot * 4 + (i >> 7)
+        ahead = (((i >> 4) & 3) - place_ref[0]) & 3
+        slot = jnp.where((ahead & 1) == 0, ahead + (ahead >> 1), jnp.where(ahead == 3 - 2 * place_ref[1], 1, 2))
+        return (i & 7) * 32 + ((i >> 3) & 1) * 16 + slot * 4 + (i >> 6)
 
-    order = one_hot(source, 512, 512)
+    order = one_hot(source, 256, 256)
+    mixed = mixed_ref[...].reshape(2, 8, 2, 32, 256)
     for core in range(C):
-        rows = pick(order, mixed_ref[32 * core : 32 * (core + 1)].reshape(512, 256))
-        for f in range(4):
-            for x in range(X):
-                out_ref[f, 64 * x + 32 * core : 64 * x + 32 * (core + 1)] = rows[128 * f + 32 * x : 128 * f + 32 * (x + 1)]
+        for pair in range(2):
+            rows = pick(order, mixed[core, :, pair].reshape(256, 256))
+            for f in range(4):
+                for x in range(X):
+                    start = 64 * x + 32 * core + 16 * pair
+                    out_ref[f, start : start + 16] = rows[64 * f + 16 * x : 64 * f + 16 * (x + 1)]
 
 
-def call(kernel, out_shape, *operands, flops=10**7, far=()):
+def call(kernel, out_shape, *operands, flops=10**7, far=(), in_place=False):
     def spec(i, operand):
-        return pl.BlockSpec(memory_space=pltpu.SMEM if operand.dtype == jnp.int32 else pl.ANY if i in far else VMEM)
+        return pl.BlockSpec(memory_space=pltpu.SMEM if operand.dtype == jnp.int32 else pl.ANY if i in far or in_place else VMEM)
 
-    return pl.pallas_call(
+    shapes = out_shape if isinstance(out_shape, list) else [out_shape]
+    outs = pl.pallas_call(
         kernel,
-        out_shape=jax.ShapeDtypeStruct(out_shape, BF),
+        out_shape=[jax.ShapeDtypeStruct(shape, BF) for shape in shapes],
         in_specs=[spec(i, operand) for i, operand in enumerate(operands)],
-        out_specs=pl.BlockSpec(memory_space=VMEM),
+        out_specs=[pl.BlockSpec(memory_space=pl.ANY if in_place else VMEM)] * len(shapes),
+        input_output_aliases={i: i for i in range(len(shapes))} if in_place else {},
         compiler_params=pltpu.CompilerParams(vmem_limit_bytes=40 * 2**20),
         cost_estimate=pl.CostEstimate(flops=flops, bytes_accessed=2**21, transcendentals=0),
     )(*operands)
+    return outs if isinstance(out_shape, list) else outs[0]
 
 
-def shift(x, axis, by):
-    n = {"z": Z, "y": Y, "x": X, "c": C}[axis]
-    return lax.ppermute(x, axis, [(i, (i + by) % n) for i in range(n)])
+def send(rows, to):
+    pairs = []
+    for x in range(X):
+        for c in range(C):
+            there, core = to(x, c)
+            pairs.append((x * C + c, there % X * C + core))
+    return lax.ppermute(rows, ("x", "c"), pairs)
 
 
 def shards(frames, norm_gain, w_qkv):
@@ -135,15 +146,16 @@
     spread = lax.all_to_all(packed.reshape(8, 16, D), ("y", "c"), 0, 0, tiled=True).reshape(128, D)
     routed = call(route_kernel, (128, D), spread)
     own = lax.all_to_all(routed.reshape(Z, 8, D), "z", 0, 0, tiled=True).reshape(128, D)
-    left = shift(own, "x", 1)
-    right = shift(own, "x", -1)
-    far_low = shift(left[:64], "x", 1)
-    far_high = shift(right[64:], "x", -1)
     place = jnp.stack([lax.axis_index("x"), lax.axis_index("c")]).astype(jnp.int32)
-    pairs = [part for mine in (own, left, right) for part in (mine, shift(mine, "c", 1))]
-    near = call(near_kernel, (768, 256), place, *pairs, weights, flops=6 * 10**9)
-    far = call(stack_kernel, (128, D), far_low, far_high, near, far=(2,))
-    mixed = call(far_kernel, (64, 16, 256), place, near, far, shift(far, "c", 1), weights, flops=2 * 10**9)
+    straight = send(own, lambda x, c: (x + 1 - 2 * c, c))
+    crossed = send(own, lambda x, c: (x - 1 + 2 * c, 1 - c))
+    far = send(straight, lambda x, c: (x + 1 - 2 * c, c))
+    swap = lambda rows: send(rows, lambda x, c: (x, 1 - c))
+    held = call(hold_kernel, [crossed.shape], crossed, flops=10**10, in_place=True)[0]
+    first = call(near_kernel, (256, 256), place, own, swap(own), weights, flops=2 * 10**9)
+    near = call(near_kernel, (512, 256), place, straight, held, swap(held), swap(straight), weights, flops=4 * 10**9)
+    far = call(hold_kernel, [far.shape], far, first, in_place=True)[0]
+    mixed = call(far_kernel, (64, 16, 256), place, first, near, far, swap(far), weights, flops=2 * 10**9)
     mixed = lax.all_to_all(mixed, ("z", "y"), 0, 0, tiled=True)
     return call(place_kernel, (4, 256, 256), place, mixed)
 

time: 232 us -> 226 us (0.974)
  blocking collectives: 153 us -> 150 us
  starting transfers between devices: 19.3 us -> 16.4 us
  local copies, waits for them, and re-layouts: 8.35 us -> 5.65 us
    all_gather x1, waiting for transfers between devices: 0.02 us -> 3.34 us  [shards(): weights = lax.all_gather(weights, 'z', axis=0)]
    all_to_all x1, blocking collectives: 46.2 us -> 43.2 us  [shards(): mixed = lax.all_to_all(mixed, ('z', 'y'), 0, 0, tiled=True)]
    ppermute x8 -> x7, starting transfers between devices: 19.3 us -> 16.4 us  [send(): return lax.ppermute(rows, ('x', 'c'), pairs)]
    slice x2 -> x0, local copies, waits for them, and re-layouts: 2.71 us -> none  [the longest x1 1.88 us: shards(): far_high = shift(right[64:], 'x', -1)]
    ppermute x8 -> x7, waiting for transfers between devices: 21.3 us -> 19.5 us  [send(): return lax.ppermute(rows, ('x', 'c'), pairs)]
    pallas_call x6 -> x8, Pallas kernels: 15.3 us -> 15.6 us  [call(): pl.pallas_call(kernel, out_shape=[jax.ShapeDtypeStruct(shape, BF) for sha...]
  transfers between devices with their start and end apart: 9 -> 8, of which waited for: 4 -> 3; matrix products, arithmetic and copies ran while one was open for 1% -> 0% of each run, Pallas kernels for 4% -> 5%
where the time goes in v5:
time: 226 us; the launch traced here: 224 us
  blocking collectives  150 us (66%)
  waiting for transfers between devices  22.8 us (10%)
  starting transfers between devices  16.4 us (7%)
  Pallas kernels  15.6 us (7%)
  between operations  13.6 us (6%)
  local copies, waits for them, and re-layouts  5.65 us (2%)
    all_to_all x1, blocking collectives, shards(): lax.all_to_all(routed.reshape(Z, 8, D), 'z', 0, 0, tiled=True)  75.8 us
    all_to_all x1, blocking collectives, shards(): mixed = lax.all_to_all(mixed, ('z', 'y'), 0, 0, tiled=True)  43.2 us
    ppermute x7, waiting for transfers between devices, send(): return lax.ppermute(rows, ('x', 'c'), pairs)  19.5 us
    all_to_all x1, blocking collectives, shards(): lax.all_to_all(packed.reshape(8, 16, D), ('y', 'c'), 0, 0, tiled=True)  18.5 us
    ppermute x7, starting transfers between devices, send(): return lax.ppermute(rows, ('x', 'c'), pairs)  16.4 us
    pallas_call x8, Pallas kernels, call(): pl.pallas_call(kernel, out_shape=[jax.ShapeDtypeStruct(shape, BF) for sha...  15.6 us
    all_to_all x1, blocking collectives, shards(): weights = lax.all_to_all(weights, 'y', 0, 0, tiled=True)  12.4 us
    unnamed x8, local copies, waits for them, and re-layouts  4.72 us
  transfers between devices with their start and end apart: 8, of which 3 were waited for; matrix products, arithmetic and copies ran while one was open for 0% of the time, Pallas kernels for 5%

profile of v5, /device:TPU:6, one launch (start us, length us, event | category | flops | bytes accessed | tf_op | source)
XLA Modules:
  0.0 224.1 jit_solution(8028072985560751040)
XLA Ops:
  6.5 0.9 broadcast_in_dim.3
  7.5 12.4 %all_to_all.20 = bf16[4,3,64,256]{3,2,1,0:T(8,128)(2,1)} all-to-all(bf16[4,3,64,256]{3,2,1,0:T(8,128)(2,1)S(1)} %broadcast_in_dim.3), channel_id=1, replica_groups=mesh['z'=16,'y'=4,'x'=4,'c'=2] {'y'}, dimensions={0} | all-to-all | bytes 786432 | tf_op jit(solution)/shard_map/all_to_all | solution.py:143
  19.9 0.0 all-gather.3.cloned.1.call-update
  19.9 0.0 copy-start.2
  19.9 1.2 copy-done.2
  21.2 0.7 copy-done.3
  21.9 0.7 shard_map.37
  22.6 18.5 %all_to_all.21 = bf16[8,16,4096]{2,1,0:T(8,128)(2,1)S(1)} all-to-all(bf16[8,16,4096]{2,1,0:T(8,128)(2,1)S(1)} %bitcast.18), channel_id=1, replica_groups=mesh['z'=16,'y'=4,'x'=4,'c'=2] {'y','c'}, dimensions={0} | all-to-all | bytes 2097152 | tf_op jit(solution)/shard_map/all_to_all | solution.py:146
  41.1 0.4 shard_map.38
  41.6 75.8 %all_to_all.22 = bf16[16,8,4096]{2,1,0:T(8,128)(2,1)S(1)} all-to-all(bf16[16,8,4096]{2,1,0:T(8,128)(2,1)S(1)} %bitcast.17), channel_id=1, replica_groups=mesh['z'=16,'y'=4,'x'=4,'c'=2] {'z'}, dimensions={0} | all-to-all | bytes 2097152 | tf_op jit(solution)/shard_map/all_to_all | solution.py:148
  117.3 2.3 %collective-permute-start.1 = (bf16[128,4096]{1,0:T(8,128)(2,1)S(1)}, bf16[128,4096]{1,0:T(8,128)(2,1)}, u32[]{:S(2)}, u32[]{:S(2)}) collective-permute-start(bf16[128,4096]{1,0:T(8,128)(2,1)S(1)} %bitcast.12), channel_id=1, source_target_pairs={{0,2},{1,7},{2,4},{3,1},{4,6},{5,3},{6,0},{7,5},{8,10},{9,15},{10,... | collective-permute-start | bytes 3145736 | tf_op jit(solution)/shard_map/ppermute | solution.py:138
  119.6 1.9 collective-permute-start.2
  121.6 3.6 %collective-permute-start = (bf16[128,4096]{1,0:T(8,128)(2,1)S(1)}, bf16[128,4096]{1,0:T(8,128)(2,1)S(1)}, u32[]{:S(2)}, u32[]{:S(2)}) collective-permute-start(bf16[128,4096]{1,0:T(8,128)(2,1)S(1)} %bitcast.14), channel_id=1, source_target_pairs={{0,1},{1,0},{2,3},{3,2},{4,5},{5,4},{6,7},{7,6},{8,9},{9,8},{10,11... | collective-permute-start | bytes 3145736 | tf_op jit(solution)/shard_map/ppermute | solution.py:138
  125.1 18.4 %collective-permute-done.1.refs_0_ = bf16[128,4096]{1,0:T(8,128)(2,1)} collective-permute-done((bf16[128,4096]{1,0:T(8,128)(2,1)S(1)}, bf16[128,4096]{1,0:T(8,128)(2,1)}, u32[]{:S(2)}, u32[]{:S(2)}) %collective-permute-start.1) | collective-permute-done | bytes 1048608 | tf_op jit(solution)/shard_map/ppermute | solution.py:138
  143.5 2.4 %collective-permute-start.5 = (bf16[128,4096]{1,0:T(8,128)(2,1)}, bf16[128,4096]{1,0:T(8,128)(2,1)S(1)}, u32[]{:S(2)}, u32[]{:S(2)}) collective-permute-start(bf16[128,4096]{1,0:T(8,128)(2,1)} %collective-permute-done.1.refs_0_), channel_id=1, source_target_pairs={{0,2},{1,7},{2,4},{3,1},{4,6},{5,3},{6,0},{7,5},{8,10},{9,15},{10,... | collective-permute-start | bytes 3145736 | tf_op jit(solution)/shard_map/ppermute | solution.py:138
  145.9 0.0 collective-permute-done.2.refs_0_
  145.9 1.9 collective-permute-start.3
  147.9 2.4 %collective-permute-start.4 = (bf16[128,4096]{1,0:T(8,128)(2,1)}, bf16[128,4096]{1,0:T(8,128)(2,1)}, u32[]{:S(2)}, u32[]{:S(2)}) collective-permute-start(bf16[128,4096]{1,0:T(8,128)(2,1)} %collective-permute-done.1.refs_0_), channel_id=1, source_target_pairs={{0,1},{1,0},{2,3},{3,2},{4,5},{5,4},{6,7},{7,6},{8,9},{9,8},{10,11... | collective-permute-start | bytes 3145736 | tf_op jit(solution)/shard_map/ppermute | solution.py:138
  150.3 0.1 pad_add_fusion.place_ref
  150.4 0.0 collective-permute-done.refs_1_
  150.4 3.3 %all-gather.3.cloned.1.call-done = bf16[64,3,64,256]{3,2,1,0:T(8,128)(2,1)} async-done(((bf16[4,3,64,256]{3,2,1,0:T(8,128)(2,1)}), bf16[64,3,64,256]{3,2,1,0:T(8,128)(2,1)}) %all-gather.3.cloned.1.call-update) | async-done | bytes 6291472 | tf_op jit(solution)/shard_map/all_gather | solution.py:144
  153.7 2.8 %copy-done = bf16[64,3,64,256]{3,2,1,0:T(8,128)(2,1)S(1)} copy-done((bf16[64,3,64,256]{3,2,1,0:T(8,128)(2,1)S(1)}, bf16[64,3,64,256]{3,2,1,0:T(8,128)(2,1)}, u32[]{:S(2)}) %copy-start) | copy-done | bytes 6291480
  156.5 2.8 %shard_map.39.refs_1_.first_ref = bf16[256,256]{1,0:T(8,128)(2,1)S(1)} custom-call(s32[2]{0:T(128)S(1)} %pad_add_fusion.place_ref, bf16[128,4096]{1,0:T(8,128)(2,1)S(1)} %bitcast.15, bf16[128,4096]{1,0:T(8,128)(2,1)S(1)} %collective-permute-done.refs_1_, bf16[16,4,3,64,256]{4,3,2,1,0:T(8,128)(2,1)S(1)} %bitcast.9), custom_call_target="tpu_custom_call" | custom-call | flops 2000000000 | bytes 2097152 | tf_op jit(solution)/shard_map/pallas_call | solution.py:120
  159.3 1.1 collective-permute-done.5.refs_0_
  160.4 1.9 collective-permute-start.6
  162.3 0.0 collective-permute-done.3.refs_2_
  162.4 0.0 collective-permute-done.4.refs_3_
  162.4 6.6 %shard_map.41.near_ref = bf16[512,256]{1,0:T(8,128)(2,1)S(1)} custom-call(s32[2]{0:T(128)S(1)} %pad_add_fusion.place_ref, bf16[128,4096]{1,0:T(8,128)(2,1)} %collective-permute-done.1.refs_0_, bf16[128,4096]{1,0:T(8,128)(2,1)} %shard_map.40.refs_1_, bf16[128,4096]{1,0:T(8,128)(2,1)} %collective-permute-done.3.refs_2_, ...), custom_call_target="tpu_custom_call" | custom-call | flops 4000000000 | bytes 2097152 | tf_op jit(solution)/shard_map/pallas_call | solution.py:120
  169.0 0.0 collective-permute-done.6.other_far_ref
  169.0 3.4 %shard_map.43 = bf16[64,16,256]{2,1,0:T(8,128)(2,1)S(1)} custom-call(s32[2]{0:T(128)S(1)} %pad_add_fusion.place_ref, bf16[256,256]{1,0:T(8,128)(2,1)S(1)} %shard_map.39.refs_1_.first_ref, bf16[512,256]{1,0:T(8,128)(2,1)S(1)} %shard_map.41.near_ref, bf16[128,4096]{1,0:T(8,128)(2,1)S(1)} %shard_map.42.far_ref, ...), custom_call_target="tpu_custom_call" | custom-call | flops 2000000000 | bytes 2097152 | tf_op jit(solution)/shard_map/pallas_call | solution.py:120
  172.4 43.2 %all_to_all.23.mixed_ref = bf16[64,16,256]{2,1,0:T(8,128)(2,1)S(1)} all-to-all(bf16[64,16,256]{2,1,0:T(8,128)(2,1)S(1)} %shard_map.43), channel_id=1, replica_groups=mesh['z'=16,'y'=4,'x'=4,'c'=2] {'z','y'}, dimensions={0} | all-to-all | bytes 1048576 | tf_op jit(solution)/shard_map/all_to_all | solution.py:159
  215.6 1.7 shard_map.44
  (7 shorter events, 0.0 us)
Async XLA Ops:
  6.5 147.2 %all-gather.3.cloned.1.call-start = ((), (), s32[]{:S(2)}) async-start(), calls=%async_computation.4 | async-start | bytes 6684672 | tf_op jit(solution)/shard_map/all_gather | solution.py:144
  19.9 1.2 copy-start.2
  21.2 0.7 copy-start.3
  117.3 26.2 %collective-permute-start.1 = (bf16[128,4096]{1,0:T(8,128)(2,1)S(1)}, bf16[128,4096]{1,0:T(8,128)(2,1)}, u32[]{:S(2)}, u32[]{:S(2)}) collective-permute-start(bf16[128,4096]{1,0:T(8,128)(2,1)S(1)} %bitcast.12), channel_id=1, source_target_pairs={{0,2},{1,7},{2,4},{3,1},{4,6},{5,3},{6,0},{7,5},{8,10},{9,15},{10,... | collective-permute-start | bytes 3145736 | tf_op jit(solution)/shard_map/ppermute | solution.py:138
  119.6 26.3 %collective-permute-start.2 = (bf16[128,4096]{1,0:T(8,128)(2,1)S(1)}, bf16[128,4096]{1,0:T(8,128)(2,1)}, u32[]{:S(2)}, u32[]{:S(2)}) collective-permute-start(bf16[128,4096]{1,0:T(8,128)(2,1)S(1)} %bitcast.13), channel_id=1, source_target_pairs={{0,7},{1,2},{2,1},{3,4},{4,3},{5,6},{6,5},{7,0},{8,15},{9,10},{10,... | collective-permute-start | bytes 3145736 | tf_op jit(solution)/shard_map/ppermute | solution.py:138
  121.6 28.8 %collective-permute-start = (bf16[128,4096]{1,0:T(8,128)(2,1)S(1)}, bf16[128,4096]{1,0:T(8,128)(2,1)S(1)}, u32[]{:S(2)}, u32[]{:S(2)}) collective-permute-start(bf16[128,4096]{1,0:T(8,128)(2,1)S(1)} %bitcast.14), channel_id=1, source_target_pairs={{0,1},{1,0},{2,3},{3,2},{4,5},{5,4},{6,7},{7,6},{8,9},{9,8},{10,11... | collective-permute-start | bytes 3145736 | tf_op jit(solution)/shard_map/ppermute | solution.py:138
  143.5 16.9 %collective-permute-start.5 = (bf16[128,4096]{1,0:T(8,128)(2,1)}, bf16[128,4096]{1,0:T(8,128)(2,1)S(1)}, u32[]{:S(2)}, u32[]{:S(2)}) collective-permute-start(bf16[128,4096]{1,0:T(8,128)(2,1)} %collective-permute-done.1.refs_0_), channel_id=1, source_target_pairs={{0,2},{1,7},{2,4},{3,1},{4,6},{5,3},{6,0},{7,5},{8,10},{9,15},{10,... | collective-permute-start | bytes 3145736 | tf_op jit(solution)/shard_map/ppermute | solution.py:138
  145.9 16.4 %collective-permute-start.3 = (bf16[128,4096]{1,0:T(8,128)(2,1)}, bf16[128,4096]{1,0:T(8,128)(2,1)}, u32[]{:S(2)}, u32[]{:S(2)}) collective-permute-start(bf16[128,4096]{1,0:T(8,128)(2,1)} %shard_map.40.refs_1_), channel_id=1, source_target_pairs={{0,1},{1,0},{2,3},{3,2},{4,5},{5,4},{6,7},{7,6},{8,9},{9,8},{10,11... | collective-permute-start | bytes 3145736 | tf_op jit(solution)/shard_map/ppermute | solution.py:138
  147.9 14.5 %collective-permute-start.4 = (bf16[128,4096]{1,0:T(8,128)(2,1)}, bf16[128,4096]{1,0:T(8,128)(2,1)}, u32[]{:S(2)}, u32[]{:S(2)}) collective-permute-start(bf16[128,4096]{1,0:T(8,128)(2,1)} %collective-permute-done.1.refs_0_), channel_id=1, source_target_pairs={{0,1},{1,0},{2,3},{3,2},{4,5},{5,4},{6,7},{7,6},{8,9},{9,8},{10,11... | collective-permute-start | bytes 3145736 | tf_op jit(solution)/shard_map/ppermute | solution.py:138
  153.7 2.8 %copy-start = (bf16[64,3,64,256]{3,2,1,0:T(8,128)(2,1)S(1)}, bf16[64,3,64,256]{3,2,1,0:T(8,128)(2,1)}, u32[]{:S(2)}) copy-start(bf16[64,3,64,256]{3,2,1,0:T(8,128)(2,1)} %all-gather.3.cloned.1.call-done) | copy-start | bytes 18874372
  156.5 5.9 %copy-start.1 = (bf16[64,3,64,256]{3,2,1,0:T(8,128)(2,1)S(1)}, bf16[64,3,64,256]{3,2,1,0:T(8,128)(2,1)}, u32[]{:S(2)}) copy-start(bf16[64,3,64,256]{3,2,1,0:T(8,128)(2,1)} %all-gather.3.cloned.1.call-done) | copy-start | bytes 18874372
  160.4 8.6 %collective-permute-start.6 = (bf16[128,4096]{1,0:T(8,128)(2,1)S(1)}, bf16[128,4096]{1,0:T(8,128)(2,1)S(1)}, u32[]{:S(2)}, u32[]{:S(2)}) collective-permute-start(bf16[128,4096]{1,0:T(8,128)(2,1)S(1)} %shard_map.42.far_ref), channel_id=1, source_target_pairs={{0,1},{1,0},{2,3},{3,2},{4,5},{5,4},{6,7},{7,6},{8,9},{9,8},{10,11... | collective-permute-start | bytes 3145736 | tf_op jit(solution)/shard_map/ppermute | solution.py:138
Sparse Core Ops, SparseCore 0:
  20.1 133.6 all-gather.2

commit v6 on v5

v6 whole, which is shorter than its diff:
```python
import jax
import jax.numpy as jnp
from jax import lax
from jax.experimental import pallas as pl
from jax.experimental.pallas import tpu as pltpu
from jax.sharding import Mesh, PartitionSpec as P

BF, F32 = jnp.bfloat16, jnp.float32
Z, Y, X, C = 16, 4, 4, 2
D, HEAD = 4096, 128
VMEM = pltpu.VMEM


def iota(shape, dim):
    return lax.broadcasted_iota(jnp.int32, shape, dim)


def one_hot(source, n, m):
    return jnp.where(source(iota((n, m), 0)) == iota((n, m), 1), 1.0, 0.0).astype(BF)


def pick(matrix, rows):
    return jnp.dot(matrix, rows, preferred_element_type=F32).astype(BF)


def normalize_kernel(frames_ref, gain_ref, out_ref):
    rows = frames_ref[...].reshape(128, D).astype(F32)
    scale = lax.rsqrt(jnp.mean(rows * rows, axis=-1, keepdims=True) + 1e-05)
    shuffle = one_hot(
        lambda i: (i & 3) * 128 + ((i >> 3) & 1) * 64 + ((i >> 2) & 1) * 32 + (i >> 4), 512, 512
    )
    for j in range(2):
        cuts = [slice(1024 * q + 512 * j, 1024 * q + 512 * (j + 1)) for q in range(4)]
        normed = jnp.concatenate([(rows[:, cut] * scale * gain_ref[:, cut]).astype(BF) for cut in cuts], axis=0)
        out_ref[:, 512 * j : 512 * (j + 1)] = pick(shuffle, normed)


def merge_kernel(in_ref, out_ref):
    for q in range(4):
        order = one_hot(lambda i: i * 4 + q, 128, 512)
        for j in range(2):
            start = 1024 * q + 512 * j
            out_ref[:, start : start + 512] = pick(order, in_ref[:, 512 * j : 512 * (j + 1)])


def hold_kernel(*refs):
    pass


def project(token_refs, weights_ref, held_ref, arrived):
    parts = [pl.ds(4 * k, 4) for k in range(4)]
    copies = [pltpu.make_async_copy(weights_ref.at[part], held_ref.at[part], arrived.at[k]) for k, part in enumerate(parts)]
    for copy in copies:
        copy.start()
    totals = [None] * 3
    for k, copy in enumerate(copies):
        cut = slice(1024 * k, 1024 * (k + 1))
        rows = jnp.concatenate([ref[:, cut] for ref in token_refs], axis=0)
        copy.wait()
        for c in range(3):
            weights = held_ref[4 * k : 4 * (k + 1), :, c].reshape(1024, 256)
            term = jnp.dot(rows, weights, preferred_element_type=F32)
            totals[c] = term if totals[c] is None else totals[c] + term
    return [total.astype(BF) for total in totals]


def attend(qkv, patches, core):
    def frame(i):
        return ((i & 127) >> 1) * 4 + ((i >> 7) ^ core) * 2 + (i & 1)

    keep = frame(iota((256, 256), 1)) <= frame(iota((256, 256), 0))
    scale = HEAD**-0.5 * 1.4426950408889634
    across = (((1,), (1,)), ((), ()))
    units = [
        [part[256 * p : 256 * (p + 1), HEAD * h : HEAD * (h + 1)] for part in qkv] for p in range(patches) for h in range(2)
    ]
    scores = [lax.dot_general(q, k, across, preferred_element_type=F32) * scale for q, k, _ in units]
    scores = [jnp.where(keep, s, -jnp.inf) for s in scores]
    grown = [jnp.exp2(s - jnp.max(s, axis=-1, keepdims=True)) for s in scores]
    probs = [(g * (1.0 / jnp.sum(g, axis=-1, keepdims=True))).astype(BF) for g in grown]
    heads = [jnp.dot(w, v, preferred_element_type=F32).astype(BF) for w, (_, _, v) in zip(probs, units)]
    return [jnp.concatenate(heads[2 * p : 2 * p + 2], axis=1) for p in range(patches)]


def patches_kernel(place_ref, *refs):
    *token_refs, weights_ref, out_ref, held_ref, arrived = refs
    core = place_ref[1]
    mixed = attend(project(token_refs, weights_ref, held_ref, arrived), 4, core)
    def source(i):
        return ((i >> 2) & 3) * 64 + (((i >> 1) & 1) ^ core) * 32 + (i >> 4) * 2 + (i & 1)

    order = one_hot(source, 256, 256)
    for k in range(4):
        cuts = [part[128 * g + 32 * k : 128 * g + 32 * (k + 1)] for part in mixed for g in range(2)]
        out_ref[16 * k : 16 * (k + 1)] = pick(order, jnp.concatenate(cuts, axis=0)).reshape(16, 16, 256)


def place_kernel(place_ref, mixed_ref, out_ref):
    def source(i):
        ahead = (((i >> 4) & 3) - place_ref[0]) & 3
        slot = jnp.where((ahead & 1) == 0, ahead + (ahead >> 1), jnp.where(ahead == 3 - 2 * place_ref[1], 1, 2))
        return ((i >> 1) & 7) * 32 + (i & 1) * 16 + slot * 4 + (i >> 6)

    order = one_hot(source, 256, 256)
    mixed = mixed_ref[...].reshape(2, 8, 2, 2, 16, 256)
    for core in range(C):
        for upper in range(2):
            rows = pick(order, mixed[upper, :, :, core].reshape(256, 256))
            for f in range(4):
                for x in range(X):
                    start = 64 * x + 32 * core + 16 * upper
                    out_ref[f, start : start + 16] = rows[64 * f + 16 * x : 64 * f + 16 * (x + 1)]


def call(kernel, out_shape, *operands, flops=10**7, far=(), in_place=False, scratch=(), limit=40):
    def spec(i, operand):
        return pl.BlockSpec(memory_space=pltpu.SMEM if operand.dtype == jnp.int32 else pl.ANY if i in far or in_place else VMEM)

    shapes = out_shape if isinstance(out_shape, list) else [out_shape]
    outs = pl.pallas_call(
        kernel,
        out_shape=[jax.ShapeDtypeStruct(shape, BF) for shape in shapes],
        in_specs=[spec(i, operand) for i, operand in enumerate(operands)],
        out_specs=[pl.BlockSpec(memory_space=pl.ANY if in_place else VMEM)] * len(shapes),
        input_output_aliases={i: i for i in range(len(shapes))} if in_place else {},
        scratch_shapes=scratch,
        compiler_params=pltpu.CompilerParams(vmem_limit_bytes=limit * 2**20),
        cost_estimate=pl.CostEstimate(flops=flops, bytes_accessed=2**21, transcendentals=0),
    )(*operands)
    return outs if isinstance(out_shape, list) else outs[0]


def send(rows, to):
    pairs = []
    for x in range(X):
        for c in range(C):
            there, core = to(x, c)
            pairs.append((x * C + c, there % X * C + core))
    return lax.ppermute(rows, ("x", "c"), pairs)


def send_home(rows, to):
    pairs = []
    for y in range(Y):
        for x in range(X):
            for c in range(C):
                there, core = to(x, c)
                held = ((y - y % 2 + c) * X + x) * C + y % 2
                pairs.append((held, (y * X + there % X) * C + core))
    return lax.ppermute(rows, ("y", "x", "c"), pairs)


def shards(frames, norm_gain, w_qkv):
    weights = jnp.broadcast_to(jnp.transpose(w_qkv, (1, 0, 2)), (Y, 3, 64, 256))
    weights = lax.all_to_all(weights, "y", 0, 0, tiled=True)
    weights = lax.all_gather(weights, "z", axis=0)
    packed = call(normalize_kernel, (512, 1024), frames, norm_gain.reshape(1, D))
    spread = lax.all_to_all(packed.reshape(64, 8, 1024), ("z", "y"), 0, 0, tiled=True)
    rows = call(merge_kernel, (128, D), spread.reshape(512, 1024))
    place = jnp.stack([lax.axis_index("x"), lax.axis_index("c")]).astype(jnp.int32)
    straight = send_home(rows, lambda x, c: (x + 1 - 2 * c, c))
    crossed = send_home(rows, lambda x, c: (x - 1 + 2 * c, 1 - c))
    own = send_home(rows, lambda x, c: (x, c))
    far = send(straight, lambda x, c: (x + 1 - 2 * c, c))
    swap = lambda part: send(part, lambda x, c: (x, 1 - c))
    held = call(hold_kernel, [crossed.shape], crossed, flops=10**10, in_place=True)[0]
    tokens = (own, swap(own), straight, held, swap(held), swap(straight), far, swap(far))
    mixed = call(
        patches_kernel, (64, 16, 256), place, *tokens, weights, flops=8 * 10**9, far=(9,), limit=44,
        scratch=(VMEM((Z, Y, 3, 64, 256), BF), pltpu.SemaphoreType.DMA((4,))),
    )
    mixed = lax.all_to_all(mixed, ("z", "y"), 0, 0, tiled=True)
    return call(place_kernel, (4, 256, 256), place, mixed)


def solution(mesh):
    grid = Mesh(mesh.devices.reshape(Z, Y, X, C), ("z", "y", "x", "c"))
    rows, columns = ("z", "y"), ("x", "c")
    return jax.shard_map(
        shards, mesh=grid, in_specs=(P(rows, columns, None), P(), P(rows, None, columns)),
        out_specs=P(rows, None, columns), check_vma=False,
    )
```

time: 226 us -> 219 us (0.969)
  blocking collectives: 150 us -> 135 us
  starting transfers between devices: 16.4 us -> 23.8 us
  local copies, waits for them, and re-layouts: 5.65 us -> 2.86 us
  waiting for transfers between devices: 22.8 us -> 25.3 us
    ppermute x0 -> x3, waiting for transfers between devices: none -> 20.7 us  [send_home(): return lax.ppermute(rows, ('y', 'x', 'c'), pairs)]
    ppermute x7 -> x5, waiting for transfers between devices: 19.5 us -> 4.59 us  [send(): return lax.ppermute(rows, ('x', 'c'), pairs)]
    all_to_all x2 -> x1, blocking collectives: 94.3 us -> 81.8 us  [shards(): lax.all_to_all(packed.reshape(64, 8, 1024), ('z', 'y'), 0, 0, tiled=True)]
    ppermute x0 -> x3, starting transfers between devices: none -> 7.22 us  [send_home(): return lax.ppermute(rows, ('y', 'x', 'c'), pairs)]
    all_gather x1, waiting for transfers between devices: 3.34 us -> 0.01 us  [shards(): weights = lax.all_gather(weights, 'z', axis=0)]
    unnamed x8 -> x4, local copies, waits for them, and re-layouts: 4.72 us -> 1.94 us
    pallas_call x8 -> x5, Pallas kernels: 15.6 us -> 17.4 us  [call(): pl.pallas_call(kernel, out_shape=[jax.ShapeDtypeStruct(shape, BF) for sha...]
    ppermute x7 -> x5, starting transfers between devices: 16.4 us -> 16.6 us  [send(): return lax.ppermute(rows, ('x', 'c'), pairs)]
  transfers between devices with their start and end apart: 8 -> 9, of which waited for: 3 -> 3; matrix products, arithmetic and copies ran while one was open for 0% -> 0% of each run, Pallas kernels for 5% -> 1%
where the time goes in v6:
time: 219 us; the launch traced here: 218 us
  blocking collectives  135 us (62%)
  waiting for transfers between devices  25.3 us (12%)
  starting transfers between devices  23.8 us (11%)
  Pallas kernels  17.4 us (8%)
  between operations  13.5 us (6%)
  local copies, waits for them, and re-layouts  2.86 us (1%)
    all_to_all x1, blocking collectives, shards(): lax.all_to_all(packed.reshape(64, 8, 1024), ('z', 'y'), 0, 0, tiled=True)  81.8 us
    all_to_all x1, blocking collectives, shards(): mixed = lax.all_to_all(mixed, ('z', 'y'), 0, 0, tiled=True)  41.1 us
    ppermute x3, waiting for transfers between devices, send_home(): return lax.ppermute(rows, ('y', 'x', 'c'), pairs)  20.7 us
    pallas_call x5, Pallas kernels, call(): pl.pallas_call(kernel, out_shape=[jax.ShapeDtypeStruct(shape, BF) for sha...  17.4 us
    ppermute x5, starting transfers between devices, send(): return lax.ppermute(rows, ('x', 'c'), pairs)  16.6 us
    all_to_all x1, blocking collectives, shards(): weights = lax.all_to_all(weights, 'y', 0, 0, tiled=True)  12.4 us
    ppermute x3, starting transfers between devices, send_home(): return lax.ppermute(rows, ('y', 'x', 'c'), pairs)  7.22 us
    ppermute x5, waiting for transfers between devices, send(): return lax.ppermute(rows, ('x', 'c'), pairs)  4.59 us
  transfers between devices with their start and end apart: 9, of which 3 were waited for; matrix products, arithmetic and copies ran while one was open for 0% of the time, Pallas kernels for 1%

profile of v6, /device:TPU:6, one launch (start us, length us, event | category | flops | bytes accessed | tf_op | source)
XLA Modules:
  0.0 218.3 jit_solution(15360512659737513606)
XLA Ops:
  6.5 0.0 all-gather.3.cloned.1.call-start
  6.5 0.9 broadcast_in_dim.3
  7.5 12.4 %all_to_all.15 = bf16[4,3,64,256]{3,2,1,0:T(8,128)(2,1)} all-to-all(bf16[4,3,64,256]{3,2,1,0:T(8,128)(2,1)S(1)} %broadcast_in_dim.3), channel_id=1, replica_groups=mesh['z'=16,'y'=4,'x'=4,'c'=2] {'y'}, dimensions={0} | all-to-all | bytes 786432 | tf_op jit(solution)/shard_map/all_to_all | solution.py:155
  19.9 0.0 all-gather.3.cloned.1.call-update
  19.9 0.0 copy-start
  19.9 1.2 copy-done
  21.2 0.0 copy-start.1
  21.2 0.7 copy-done.1
  21.9 1.1 shard_map.37
  22.9 81.8 %all_to_all.16 = bf16[64,8,1024]{2,1,0:T(8,128)(2,1)S(1)} all-to-all(bf16[64,8,1024]{2,1,0:T(8,128)(2,1)S(1)} %bitcast.8), channel_id=1, replica_groups=mesh['z'=16,'y'=4,'x'=4,'c'=2] {'z','y'}, dimensions={0} | all-to-all | bytes 2097152 | tf_op jit(solution)/shard_map/all_to_all | solution.py:158
  104.7 0.7 shard_map.38
  105.4 2.4 %collective-permute-start.2 = (bf16[128,4096]{1,0:T(8,128)(2,1)S(1)}, bf16[128,4096]{1,0:T(8,128)(2,1)S(1)}, u32[]{:S(2)}, u32[]{:S(2)}) collective-permute-start(bf16[128,4096]{1,0:T(8,128)(2,1)S(1)} %shard_map.38), channel_id=1, source_target_pairs={{0,2},{8,7},{2,4},{10,1},{4,6},{12,3},{6,0},{14,5},{1,10},{9,15},{... | collective-permute-start | bytes 3145736 | tf_op jit(solution)/shard_map/ppermute | solution.py:150
  107.9 4.1 %collective-permute-start.3 = (bf16[128,4096]{1,0:T(8,128)(2,1)S(1)}, bf16[128,4096]{1,0:T(8,128)(2,1)}, u32[]{:S(2)}, u32[]{:S(2)}) collective-permute-start(bf16[128,4096]{1,0:T(8,128)(2,1)S(1)} %shard_map.38), channel_id=1, source_target_pairs={{0,7},{8,2},{2,1},{10,4},{4,3},{12,6},{6,5},{14,0},{1,15},{9,10},{... | collective-permute-start | bytes 3145736 | tf_op jit(solution)/shard_map/ppermute | solution.py:150
  112.0 0.7 collective-permute-start
  112.7 20.7 %collective-permute-done.2.refs_2_ = bf16[128,4096]{1,0:T(8,128)(2,1)S(1)} collective-permute-done((bf16[128,4096]{1,0:T(8,128)(2,1)S(1)}, bf16[128,4096]{1,0:T(8,128)(2,1)S(1)}, u32[]{:S(2)}, u32[]{:S(2)}) %collective-permute-start.2) | collective-permute-done | bytes 1048608 | tf_op jit(solution)/shard_map/ppermute | solution.py:150
  133.4 3.3 %collective-permute-start.6 = (bf16[128,4096]{1,0:T(8,128)(2,1)S(1)}, bf16[128,4096]{1,0:T(8,128)(2,1)S(1)}, u32[]{:S(2)}, u32[]{:S(2)}) collective-permute-start(bf16[128,4096]{1,0:T(8,128)(2,1)S(1)} %collective-permute-done.2.refs_2_), channel_id=1, source_target_pairs={{0,2},{1,7},{2,4},{3,1},{4,6},{5,3},{6,0},{7,5},{8,10},{9,15},{10,... | collective-permute-start | bytes 3145736 | tf_op jit(solution)/shard_map/ppermute | solution.py:139
  136.7 0.0 collective-permute-done.3.refs_0_
  136.7 1.9 collective-permute-start.4
  138.6 2.4 %collective-permute-start.5 = (bf16[128,4096]{1,0:T(8,128)(2,1)S(1)}, bf16[128,4096]{1,0:T(8,128)(2,1)}, u32[]{:S(2)}, u32[]{:S(2)}) collective-permute-start(bf16[128,4096]{1,0:T(8,128)(2,1)S(1)} %collective-permute-done.2.refs_2_), channel_id=1, source_target_pairs={{0,1},{1,0},{2,3},{3,2},{4,5},{5,4},{6,7},{7,6},{8,9},{9,8},{10,11... | collective-permute-start | bytes 3145736 | tf_op jit(solution)/shard_map/ppermute | solution.py:139
  141.0 0.0 collective-permute-done.refs_0_
  141.0 7.1 %collective-permute-start.1 = (bf16[128,4096]{1,0:T(8,128)(2,1)S(1)}, bf16[128,4096]{1,0:T(8,128)(2,1)}, u32[]{:S(2)}, u32[]{:S(2)}) collective-permute-start(bf16[128,4096]{1,0:T(8,128)(2,1)S(1)} %collective-permute-done.refs_0_), channel_id=1, source_target_pairs={{0,1},{1,0},{2,3},{3,2},{4,5},{5,4},{6,7},{7,6},{8,9},{9,8},{10,11... | collective-permute-start | bytes 3145736 | tf_op jit(solution)/shard_map/ppermute | solution.py:139
  148.1 1.9 collective-permute-done.6.refs_6_
  150.1 1.9 collective-permute-start.7
  152.0 0.1 pad_add_fusion.place_ref
  152.1 0.0 collective-permute-done.4.refs_4_
  152.1 0.0 collective-permute-done.5.refs_5_
  152.1 0.0 collective-permute-done.1.refs_1_
  152.1 2.7 %collective-permute-done.7.refs_7_ = bf16[128,4096]{1,0:T(8,128)(2,1)} collective-permute-done((bf16[128,4096]{1,0:T(8,128)(2,1)S(1)}, bf16[128,4096]{1,0:T(8,128)(2,1)}, u32[]{:S(2)}, u32[]{:S(2)}) %collective-permute-start.7) | collective-permute-done | bytes 1048608 | tf_op jit(solution)/shard_map/ppermute | solution.py:139
  154.7 0.0 all-gather.3.cloned.1.call-done
  154.7 13.9 %shard_map.40 = bf16[64,16,256]{2,1,0:T(8,128)(2,1)S(1)} custom-call(s32[2]{0:T(128)S(1)} %pad_add_fusion.place_ref, bf16[128,4096]{1,0:T(8,128)(2,1)S(1)} %collective-permute-done.refs_0_, bf16[128,4096]{1,0:T(8,128)(2,1)} %collective-permute-done.1.refs_1_, bf16[128,4096]{1,0:T(8,128)(2,1)S(1)} %collective-permute-done.2.refs_2_, ...), custom_call_target="tpu_custom_call" | custom-call | flops 8000000000 | bytes 2097152 | tf_op jit(solution)/shard_map/pallas_call | solution.py:120
  168.7 41.1 %all_to_all.17.mixed_ref = bf16[64,16,256]{2,1,0:T(8,128)(2,1)S(1)} all-to-all(bf16[64,16,256]{2,1,0:T(8,128)(2,1)S(1)} %shard_map.40), channel_id=1, replica_groups=mesh['z'=16,'y'=4,'x'=4,'c'=2] {'z','y'}, dimensions={0} | all-to-all | bytes 1048576 | tf_op jit(solution)/shard_map/all_to_all | solution.py:172
  209.8 1.7 shard_map.41
  (1 shorter events, 0.0 us)
Async XLA Ops:
  6.5 148.2 %all-gather.3.cloned.1.call-start = ((), (), s32[]{:S(2)}) async-start(), calls=%async_computation.3 | async-start | bytes 6684672 | tf_op jit(solution)/shard_map/all_gather | solution.py:156
  19.9 1.2 copy-start
  21.2 0.7 copy-start.1
  105.4 27.9 %collective-permute-start.2 = (bf16[128,4096]{1,0:T(8,128)(2,1)S(1)}, bf16[128,4096]{1,0:T(8,128)(2,1)S(1)}, u32[]{:S(2)}, u32[]{:S(2)}) collective-permute-start(bf16[128,4096]{1,0:T(8,128)(2,1)S(1)} %shard_map.38), channel_id=1, source_target_pairs={{0,2},{8,7},{2,4},{10,1},{4,6},{12,3},{6,0},{14,5},{1,10},{9,15},{... | collective-permute-start | bytes 3145736 | tf_op jit(solution)/shard_map/ppermute | solution.py:150
  107.9 28.8 %collective-permute-start.3 = (bf16[128,4096]{1,0:T(8,128)(2,1)S(1)}, bf16[128,4096]{1,0:T(8,128)(2,1)}, u32[]{:S(2)}, u32[]{:S(2)}) collective-permute-start(bf16[128,4096]{1,0:T(8,128)(2,1)S(1)} %shard_map.38), channel_id=1, source_target_pairs={{0,7},{8,2},{2,1},{10,4},{4,3},{12,6},{6,5},{14,0},{1,15},{9,10},{... | collective-permute-start | bytes 3145736 | tf_op jit(solution)/shard_map/ppermute | solution.py:150
  112.0 29.1 %collective-permute-start = (bf16[128,4096]{1,0:T(8,128)(2,1)S(1)}, bf16[128,4096]{1,0:T(8,128)(2,1)S(1)}, u32[]{:S(2)}, u32[]{:S(2)}) collective-permute-start(bf16[128,4096]{1,0:T(8,128)(2,1)S(1)} %shard_map.38), channel_id=1, source_target_pairs={{0,0},{8,1},{2,2},{10,3},{4,4},{12,5},{6,6},{14,7},{1,8},{9,9},{3,... | collective-permute-start | bytes 3145736 | tf_op jit(solution)/shard_map/ppermute | solution.py:150
  133.4 16.7 %collective-permute-start.6 = (bf16[128,4096]{1,0:T(8,128)(2,1)S(1)}, bf16[128,4096]{1,0:T(8,128)(2,1)S(1)}, u32[]{:S(2)}, u32[]{:S(2)}) collective-permute-start(bf16[128,4096]{1,0:T(8,128)(2,1)S(1)} %collective-permute-done.2.refs_2_), channel_id=1, source_target_pairs={{0,2},{1,7},{2,4},{3,1},{4,6},{5,3},{6,0},{7,5},{8,10},{9,15},{10,... | collective-permute-start | bytes 3145736 | tf_op jit(solution)/shard_map/ppermute | solution.py:139
  136.7 15.4 %collective-permute-start.4 = (bf16[128,4096]{1,0:T(8,128)(2,1)}, bf16[128,4096]{1,0:T(8,128)(2,1)}, u32[]{:S(2)}, u32[]{:S(2)}) collective-permute-start(bf16[128,4096]{1,0:T(8,128)(2,1)} %shard_map.39.refs_3_), channel_id=1, source_target_pairs={{0,1},{1,0},{2,3},{3,2},{4,5},{5,4},{6,7},{7,6},{8,9},{9,8},{10,11... | collective-permute-start | bytes 3145736 | tf_op jit(solution)/shard_map/ppermute | solution.py:139
  138.6 13.4 %collective-permute-start.5 = (bf16[128,4096]{1,0:T(8,128)(2,1)S(1)}, bf16[128,4096]{1,0:T(8,128)(2,1)}, u32[]{:S(2)}, u32[]{:S(2)}) collective-permute-start(bf16[128,4096]{1,0:T(8,128)(2,1)S(1)} %collective-permute-done.2.refs_2_), channel_id=1, source_target_pairs={{0,1},{1,0},{2,3},{3,2},{4,5},{5,4},{6,7},{7,6},{8,9},{9,8},{10,11... | collective-permute-start | bytes 3145736 | tf_op jit(solution)/shard_map/ppermute | solution.py:139
  141.0 11.0 %collective-permute-start.1 = (bf16[128,4096]{1,0:T(8,128)(2,1)S(1)}, bf16[128,4096]{1,0:T(8,128)(2,1)}, u32[]{:S(2)}, u32[]{:S(2)}) collective-permute-start(bf16[128,4096]{1,0:T(8,128)(2,1)S(1)} %collective-permute-done.refs_0_), channel_id=1, source_target_pairs={{0,1},{1,0},{2,3},{3,2},{4,5},{5,4},{6,7},{7,6},{8,9},{9,8},{10,11... | collective-permute-start | bytes 3145736 | tf_op jit(solution)/shard_map/ppermute | solution.py:139
  150.1 4.7 %collective-permute-start.7 = (bf16[128,4096]{1,0:T(8,128)(2,1)S(1)}, bf16[128,4096]{1,0:T(8,128)(2,1)}, u32[]{:S(2)}, u32[]{:S(2)}) collective-permute-start(bf16[128,4096]{1,0:T(8,128)(2,1)S(1)} %collective-permute-done.6.refs_6_), channel_id=1, source_target_pairs={{0,1},{1,0},{2,3},{3,2},{4,5},{5,4},{6,7},{7,6},{8,9},{9,8},{10,11... | collective-permute-start | bytes 3145736 | tf_op jit(solution)/shard_map/ppermute | solution.py:139
Sparse Core Ops, SparseCore 0:
  20.1 132.0 all-gather.2

commit v7 on v6

--- a/solution.py
+++ b/solution.py
@@ -47,16 +47,24 @@
     pass
 
 
-def project(token_refs, weights_ref, held_ref, arrived):
-    parts = [pl.ds(4 * k, 4) for k in range(4)]
-    copies = [pltpu.make_async_copy(weights_ref.at[part], held_ref.at[part], arrived.at[k]) for k, part in enumerate(parts)]
-    for copy in copies:
-        copy.start()
+def project(token_refs, weights_ref, rows_ref, held_ref, arrived):
+    n = len(token_refs)
+    arrivals = []
+    for k in range(4):
+        part, cut = pl.ds(4 * k, 4), pl.ds(1024 * k, 1024)
+        copies = [
+            pltpu.make_async_copy(ref.at[:, cut], rows_ref.at[pl.ds(128 * p, 128), cut], arrived.at[k, p])
+            for p, ref in enumerate(token_refs)
+        ]
+        copies.append(pltpu.make_async_copy(weights_ref.at[part], held_ref.at[part], arrived.at[k, n]))
+        for copy in copies:
+            copy.start()
+        arrivals.append(copies)
     totals = [None] * 3
-    for k, copy in enumerate(copies):
-        cut = slice(1024 * k, 1024 * (k + 1))
-        rows = jnp.concatenate([ref[:, cut] for ref in token_refs], axis=0)
-        copy.wait()
+    for k, copies in enumerate(arrivals):
+        for copy in copies:
+            copy.wait()
+        rows = rows_ref[:, 1024 * k : 1024 * (k + 1)]
         for c in range(3):
             weights = held_ref[4 * k : 4 * (k + 1), :, c].reshape(1024, 256)
             term = jnp.dot(rows, weights, preferred_element_type=F32)
@@ -83,9 +91,9 @@
 
 
 def patches_kernel(place_ref, *refs):
-    *token_refs, weights_ref, out_ref, held_ref, arrived = refs
+    *token_refs, weights_ref, out_ref, rows_ref, held_ref, arrived = refs
     core = place_ref[1]
-    mixed = attend(project(token_refs, weights_ref, held_ref, arrived), 4, core)
+    mixed = attend(project(token_refs, weights_ref, rows_ref, held_ref, arrived), 4, core)
     def source(i):
         return ((i >> 2) & 3) * 64 + (((i >> 1) & 1) ^ core) * 32 + (i >> 4) * 2 + (i & 1)
 
@@ -166,8 +174,8 @@
     held = call(hold_kernel, [crossed.shape], crossed, flops=10**10, in_place=True)[0]
     tokens = (own, swap(own), straight, held, swap(held), swap(straight), far, swap(far))
     mixed = call(
-        patches_kernel, (64, 16, 256), place, *tokens, weights, flops=8 * 10**9, far=(9,), limit=44,
-        scratch=(VMEM((Z, Y, 3, 64, 256), BF), pltpu.SemaphoreType.DMA((4,))),
+        patches_kernel, (64, 16, 256), place, *tokens, weights, flops=8 * 10**9, far=range(1, 10), limit=44,
+        scratch=(VMEM((1024, D), BF), VMEM((Z, Y, 3, 64, 256), BF), pltpu.SemaphoreType.DMA((4, 9))),
     )
     mixed = lax.all_to_all(mixed, ("z", "y"), 0, 0, tiled=True)
     return call(place_kernel, (4, 256, 256), place, mixed)

time: 219 us -> 218 us (level)
  no operation moved by 1% of the time
where the time goes in v7:
time: 218 us; the launch traced here: 217 us
  blocking collectives  135 us (62%)
  waiting for transfers between devices  25.3 us (12%)
  starting transfers between devices  23.8 us (11%)
  Pallas kernels  16.3 us (7%)
  between operations  13.5 us (6%)
  local copies, waits for them, and re-layouts  2.86 us (1%)
    all_to_all x1, blocking collectives, shards(): lax.all_to_all(packed.reshape(64, 8, 1024), ('z', 'y'), 0, 0, tiled=True)  81.8 us
    all_to_all x1, blocking collectives, shards(): mixed = lax.all_to_all(mixed, ('z', 'y'), 0, 0, tiled=True)  41.1 us
    ppermute x3, waiting for transfers between devices, send_home(): return lax.ppermute(rows, ('y', 'x', 'c'), pairs)  20.7 us
    ppermute x5, starting transfers between devices, send(): return lax.ppermute(rows, ('x', 'c'), pairs)  16.6 us
    pallas_call x5, Pallas kernels, call(): pl.pallas_call(kernel, out_shape=[jax.ShapeDtypeStruct(shape, BF) for sha...  16.3 us
    all_to_all x1, blocking collectives, shards(): weights = lax.all_to_all(weights, 'y', 0, 0, tiled=True)  12.4 us
    ppermute x3, starting transfers between devices, send_home(): return lax.ppermute(rows, ('y', 'x', 'c'), pairs)  7.22 us
    ppermute x5, waiting for transfers between devices, send(): return lax.ppermute(rows, ('x', 'c'), pairs)  4.59 us
  transfers between devices with their start and end apart: 9, of which 3 were waited for; matrix products, arithmetic and copies ran while one was open for 0% of the time, Pallas kernels for 1%

profile of v7, /device:TPU:6, one launch (start us, length us, event | category | flops | bytes accessed | tf_op | source)
XLA Modules:
  0.0 217.2 jit_solution(14181521767070007108)
XLA Ops:
  6.5 0.0 all-gather.3.cloned.1.call-start
  6.5 0.9 broadcast_in_dim.3
  7.5 12.4 %all_to_all.15 = bf16[4,3,64,256]{3,2,1,0:T(8,128)(2,1)} all-to-all(bf16[4,3,64,256]{3,2,1,0:T(8,128)(2,1)S(1)} %broadcast_in_dim.3), channel_id=1, replica_groups=mesh['z'=16,'y'=4,'x'=4,'c'=2] {'y'}, dimensions={0} | all-to-all | bytes 786432 | tf_op jit(solution)/shard_map/all_to_all | solution.py:163
  19.9 0.0 all-gather.3.cloned.1.call-update
  19.9 0.0 copy-start
  19.9 1.2 copy-done
  21.2 0.0 copy-start.1
  21.2 0.7 copy-done.1
  21.9 1.1 shard_map.37
  22.9 81.8 %all_to_all.16 = bf16[64,8,1024]{2,1,0:T(8,128)(2,1)S(1)} all-to-all(bf16[64,8,1024]{2,1,0:T(8,128)(2,1)S(1)} %bitcast.8), channel_id=1, replica_groups=mesh['z'=16,'y'=4,'x'=4,'c'=2] {'z','y'}, dimensions={0} | all-to-all | bytes 2097152 | tf_op jit(solution)/shard_map/all_to_all | solution.py:166
  104.7 0.7 shard_map.38
  105.4 2.4 %collective-permute-start.2 = (bf16[128,4096]{1,0:T(8,128)(2,1)S(1)}, bf16[128,4096]{1,0:T(8,128)(2,1)S(1)}, u32[]{:S(2)}, u32[]{:S(2)}) collective-permute-start(bf16[128,4096]{1,0:T(8,128)(2,1)S(1)} %shard_map.38), channel_id=1, source_target_pairs={{0,2},{8,7},{2,4},{10,1},{4,6},{12,3},{6,0},{14,5},{1,10},{9,15},{... | collective-permute-start | bytes 3145736 | tf_op jit(solution)/shard_map/ppermute | solution.py:158
  107.9 4.1 %collective-permute-start.3 = (bf16[128,4096]{1,0:T(8,128)(2,1)S(1)}, bf16[128,4096]{1,0:T(8,128)(2,1)}, u32[]{:S(2)}, u32[]{:S(2)}) collective-permute-start(bf16[128,4096]{1,0:T(8,128)(2,1)S(1)} %shard_map.38), channel_id=1, source_target_pairs={{0,7},{8,2},{2,1},{10,4},{4,3},{12,6},{6,5},{14,0},{1,15},{9,10},{... | collective-permute-start | bytes 3145736 | tf_op jit(solution)/shard_map/ppermute | solution.py:158
  112.0 0.7 collective-permute-start
  112.7 20.7 %collective-permute-done.2.refs_2_ = bf16[128,4096]{1,0:T(8,128)(2,1)S(1)} collective-permute-done((bf16[128,4096]{1,0:T(8,128)(2,1)S(1)}, bf16[128,4096]{1,0:T(8,128)(2,1)S(1)}, u32[]{:S(2)}, u32[]{:S(2)}) %collective-permute-start.2) | collective-permute-done | bytes 1048608 | tf_op jit(solution)/shard_map/ppermute | solution.py:158
  133.4 3.3 %collective-permute-start.6 = (bf16[128,4096]{1,0:T(8,128)(2,1)S(1)}, bf16[128,4096]{1,0:T(8,128)(2,1)S(1)}, u32[]{:S(2)}, u32[]{:S(2)}) collective-permute-start(bf16[128,4096]{1,0:T(8,128)(2,1)S(1)} %collective-permute-done.2.refs_2_), channel_id=1, source_target_pairs={{0,2},{1,7},{2,4},{3,1},{4,6},{5,3},{6,0},{7,5},{8,10},{9,15},{10,... | collective-permute-start | bytes 3145736 | tf_op jit(solution)/shard_map/ppermute | solution.py:147
  136.7 0.0 collective-permute-done.3.refs_0_
  136.7 1.9 collective-permute-start.4
  138.6 2.4 %collective-permute-start.5 = (bf16[128,4096]{1,0:T(8,128)(2,1)S(1)}, bf16[128,4096]{1,0:T(8,128)(2,1)}, u32[]{:S(2)}, u32[]{:S(2)}) collective-permute-start(bf16[128,4096]{1,0:T(8,128)(2,1)S(1)} %collective-permute-done.2.refs_2_), channel_id=1, source_target_pairs={{0,1},{1,0},{2,3},{3,2},{4,5},{5,4},{6,7},{7,6},{8,9},{9,8},{10,11... | collective-permute-start | bytes 3145736 | tf_op jit(solution)/shard_map/ppermute | solution.py:147
  141.0 0.0 collective-permute-done.refs_0_
  141.0 7.1 %collective-permute-start.1 = (bf16[128,4096]{1,0:T(8,128)(2,1)S(1)}, bf16[128,4096]{1,0:T(8,128)(2,1)}, u32[]{:S(2)}, u32[]{:S(2)}) collective-permute-start(bf16[128,4096]{1,0:T(8,128)(2,1)S(1)} %collective-permute-done.refs_0_), channel_id=1, source_target_pairs={{0,1},{1,0},{2,3},{3,2},{4,5},{5,4},{6,7},{7,6},{8,9},{9,8},{10,11... | collective-permute-start | bytes 3145736 | tf_op jit(solution)/shard_map/ppermute | solution.py:147
  148.1 1.9 collective-permute-done.6.refs_6_
  150.1 1.9 collective-permute-start.7
  152.0 0.1 pad_add_fusion.place_ref
  152.1 0.0 collective-permute-done.4.refs_4_
  152.1 0.0 collective-permute-done.5.refs_5_
  152.1 0.0 collective-permute-done.1.refs_1_
  152.1 2.7 %collective-permute-done.7.refs_7_ = bf16[128,4096]{1,0:T(8,128)(2,1)} collective-permute-done((bf16[128,4096]{1,0:T(8,128)(2,1)S(1)}, bf16[128,4096]{1,0:T(8,128)(2,1)}, u32[]{:S(2)}, u32[]{:S(2)}) %collective-permute-start.7) | collective-permute-done | bytes 1048608 | tf_op jit(solution)/shard_map/ppermute | solution.py:147
  154.7 0.0 all-gather.3.cloned.1.call-done
  154.7 12.9 %shard_map.40 = bf16[64,16,256]{2,1,0:T(8,128)(2,1)S(1)} custom-call(s32[2]{0:T(128)S(1)} %pad_add_fusion.place_ref, bf16[128,4096]{1,0:T(8,128)(2,1)S(1)} %collective-permute-done.refs_0_, bf16[128,4096]{1,0:T(8,128)(2,1)} %collective-permute-done.1.refs_1_, bf16[128,4096]{1,0:T(8,128)(2,1)S(1)} %collective-permute-done.2.refs_2_, ...), custom_call_target="tpu_custom_call" | custom-call | flops 8000000000 | bytes 2097152 | tf_op jit(solution)/shard_map/pallas_call | solution.py:128
  167.6 41.1 %all_to_all.17.mixed_ref = bf16[64,16,256]{2,1,0:T(8,128)(2,1)S(1)} all-to-all(bf16[64,16,256]{2,1,0:T(8,128)(2,1)S(1)} %shard_map.40), channel_id=1, replica_groups=mesh['z'=16,'y'=4,'x'=4,'c'=2] {'z','y'}, dimensions={0} | all-to-all | bytes 1048576 | tf_op jit(solution)/shard_map/all_to_all | solution.py:180
  208.7 1.7 shard_map.41
  (1 shorter events, 0.0 us)
Async XLA Ops:
  6.5 148.2 %all-gather.3.cloned.1.call-start = ((), (), s32[]{:S(2)}) async-start(), calls=%async_computation.3 | async-start | bytes 6684672 | tf_op jit(solution)/shard_map/all_gather | solution.py:164
  19.9 1.2 copy-start
  21.2 0.7 copy-start.1
  105.4 27.9 %collective-permute-start.2 = (bf16[128,4096]{1,0:T(8,128)(2,1)S(1)}, bf16[128,4096]{1,0:T(8,128)(2,1)S(1)}, u32[]{:S(2)}, u32[]{:S(2)}) collective-permute-start(bf16[128,4096]{1,0:T(8,128)(2,1)S(1)} %shard_map.38), channel_id=1, source_target_pairs={{0,2},{8,7},{2,4},{10,1},{4,6},{12,3},{6,0},{14,5},{1,10},{9,15},{... | collective-permute-start | bytes 3145736 | tf_op jit(solution)/shard_map/ppermute | solution.py:158
  107.9 28.8 %collective-permute-start.3 = (bf16[128,4096]{1,0:T(8,128)(2,1)S(1)}, bf16[128,4096]{1,0:T(8,128)(2,1)}, u32[]{:S(2)}, u32[]{:S(2)}) collective-permute-start(bf16[128,4096]{1,0:T(8,128)(2,1)S(1)} %shard_map.38), channel_id=1, source_target_pairs={{0,7},{8,2},{2,1},{10,4},{4,3},{12,6},{6,5},{14,0},{1,15},{9,10},{... | collective-permute-start | bytes 3145736 | tf_op jit(solution)/shard_map/ppermute | solution.py:158
  112.0 29.1 %collective-permute-start = (bf16[128,4096]{1,0:T(8,128)(2,1)S(1)}, bf16[128,4096]{1,0:T(8,128)(2,1)S(1)}, u32[]{:S(2)}, u32[]{:S(2)}) collective-permute-start(bf16[128,4096]{1,0:T(8,128)(2,1)S(1)} %shard_map.38), channel_id=1, source_target_pairs={{0,0},{8,1},{2,2},{10,3},{4,4},{12,5},{6,6},{14,7},{1,8},{9,9},{3,... | collective-permute-start | bytes 3145736 | tf_op jit(solution)/shard_map/ppermute | solution.py:158
  133.4 16.7 %collective-permute-start.6 = (bf16[128,4096]{1,0:T(8,128)(2,1)S(1)}, bf16[128,4096]{1,0:T(8,128)(2,1)S(1)}, u32[]{:S(2)}, u32[]{:S(2)}) collective-permute-start(bf16[128,4096]{1,0:T(8,128)(2,1)S(1)} %collective-permute-done.2.refs_2_), channel_id=1, source_target_pairs={{0,2},{1,7},{2,4},{3,1},{4,6},{5,3},{6,0},{7,5},{8,10},{9,15},{10,... | collective-permute-start | bytes 3145736 | tf_op jit(solution)/shard_map/ppermute | solution.py:147
  136.7 15.4 %collective-permute-start.4 = (bf16[128,4096]{1,0:T(8,128)(2,1)}, bf16[128,4096]{1,0:T(8,128)(2,1)}, u32[]{:S(2)}, u32[]{:S(2)}) collective-permute-start(bf16[128,4096]{1,0:T(8,128)(2,1)} %shard_map.39.refs_3_), channel_id=1, source_target_pairs={{0,1},{1,0},{2,3},{3,2},{4,5},{5,4},{6,7},{7,6},{8,9},{9,8},{10,11... | collective-permute-start | bytes 3145736 | tf_op jit(solution)/shard_map/ppermute | solution.py:147
  138.6 13.4 %collective-permute-start.5 = (bf16[128,4096]{1,0:T(8,128)(2,1)S(1)}, bf16[128,4096]{1,0:T(8,128)(2,1)}, u32[]{:S(2)}, u32[]{:S(2)}) collective-permute-start(bf16[128,4096]{1,0:T(8,128)(2,1)S(1)} %collective-permute-done.2.refs_2_), channel_id=1, source_target_pairs={{0,1},{1,0},{2,3},{3,2},{4,5},{5,4},{6,7},{7,6},{8,9},{9,8},{10,11... | collective-permute-start | bytes 3145736 | tf_op jit(solution)/shard_map/ppermute | solution.py:147
  141.0 11.0 %collective-permute-start.1 = (bf16[128,4096]{1,0:T(8,128)(2,1)S(1)}, bf16[128,4096]{1,0:T(8,128)(2,1)}, u32[]{:S(2)}, u32[]{:S(2)}) collective-permute-start(bf16[128,4096]{1,0:T(8,128)(2,1)S(1)} %collective-permute-done.refs_0_), channel_id=1, source_target_pairs={{0,1},{1,0},{2,3},{3,2},{4,5},{5,4},{6,7},{7,6},{8,9},{9,8},{10,11... | collective-permute-start | bytes 3145736 | tf_op jit(solution)/shard_map/ppermute | solution.py:147
  150.1 4.7 %collective-permute-start.7 = (bf16[128,4096]{1,0:T(8,128)(2,1)S(1)}, bf16[128,4096]{1,0:T(8,128)(2,1)}, u32[]{:S(2)}, u32[]{:S(2)}) collective-permute-start(bf16[128,4096]{1,0:T(8,128)(2,1)S(1)} %collective-permute-done.6.refs_6_), channel_id=1, source_target_pairs={{0,1},{1,0},{2,3},{3,2},{4,5},{5,4},{6,7},{7,6},{8,9},{9,8},{10,11... | collective-permute-start | bytes 3145736 | tf_op jit(solution)/shard_map/ppermute | solution.py:147
Sparse Core Ops, SparseCore 0:
  20.1 132.0 all-gather.2

commit v8 on v7

--- a/solution.py
+++ b/solution.py
@@ -161,8 +161,9 @@
 def shards(frames, norm_gain, w_qkv):
     weights = jnp.broadcast_to(jnp.transpose(w_qkv, (1, 0, 2)), (Y, 3, 64, 256))
     weights = lax.all_to_all(weights, "y", 0, 0, tiled=True)
+    packed = call(normalize_kernel, (512, 1024), frames, norm_gain.reshape(1, D))
+    weights = call(hold_kernel, [weights.shape], weights, packed, in_place=True)[0]
     weights = lax.all_gather(weights, "z", axis=0)
-    packed = call(normalize_kernel, (512, 1024), frames, norm_gain.reshape(1, D))
     spread = lax.all_to_all(packed.reshape(64, 8, 1024), ("z", "y"), 0, 0, tiled=True)
     rows = call(merge_kernel, (128, D), spread.reshape(512, 1024))
     place = jnp.stack([lax.axis_index("x"), lax.axis_index("c")]).astype(jnp.int32)

time: 218 us -> 215 us (0.986)
  blocking collectives: 135 us -> 123 us
  waiting for transfers between devices: 25.3 us -> 31.4 us
  starting transfers between devices: 23.8 us -> 27.3 us
    all_to_all x1 -> x0, blocking collectives: 12.4 us -> none  [shards(): weights = lax.all_to_all(weights, 'y', 0, 0, tiled=True)]
    all_to_all x0 -> x1, waiting for transfers between devices: none -> 5.17 us  [shards(): weights = lax.all_to_all(weights, 'y', 0, 0, tiled=True)]
    all_to_all x0 -> x1, starting transfers between devices: none -> 4.46 us  [shards(): weights = lax.all_to_all(weights, 'y', 0, 0, tiled=True)]
    pallas_call x5 -> x6, Pallas kernels: 16.3 us -> 16.3 us  [call(): pl.pallas_call(kernel, out_shape=[jax.ShapeDtypeStruct(shape, BF) for sha...]
  transfers between devices with their start and end apart: 9 -> 10, of which waited for: 3 -> 4; matrix products, arithmetic and copies ran while one was open for 0% -> 0% of each run, Pallas kernels for 1% -> 1%
where the time goes in v8:
time: 215 us
  blocking collectives  123 us (57%)
  waiting for transfers between devices  31.4 us (15%)
  starting transfers between devices  27.3 us (13%)
  Pallas kernels  16.3 us (8%)
  between operations  13.5 us (6%)
  local copies, waits for them, and re-layouts  3.61 us (2%)
    all_to_all x1, blocking collectives, shards(): lax.all_to_all(packed.reshape(64, 8, 1024), ('z', 'y'), 0, 0, tiled=True)  81.1 us
    all_to_all x1, blocking collectives, shards(): mixed = lax.all_to_all(mixed, ('z', 'y'), 0, 0, tiled=True)  41.6 us
    ppermute x3, waiting for transfers between devices, send_home(): return lax.ppermute(rows, ('y', 'x', 'c'), pairs)  21.3 us
    ppermute x5, starting transfers between devices, send(): return lax.ppermute(rows, ('x', 'c'), pairs)  16.3 us
    pallas_call x6, Pallas kernels, call(): pl.pallas_call(kernel, out_shape=[jax.ShapeDtypeStruct(shape, BF) for sha...  16.3 us
    ppermute x3, starting transfers between devices, send_home(): return lax.ppermute(rows, ('y', 'x', 'c'), pairs)  6.53 us
    all_to_all x1, waiting for transfers between devices, shards(): weights = lax.all_to_all(weights, 'y', 0, 0, tiled=True)  5.17 us
    ppermute x5, waiting for transfers between devices, send(): return lax.ppermute(rows, ('x', 'c'), pairs)  4.88 us
  transfers between devices with their start and end apart: 10, of which 4 were waited for; matrix products, arithmetic and copies ran while one was open for 0% of the time, Pallas kernels for 1%

profile of v8, /device:TPU:6, one launch (start us, length us, event | category | flops | bytes accessed | tf_op | source)
XLA Modules:
  0.0 214.8 jit_solution(5726277979931982349)
XLA Ops:
  6.5 1.7 broadcast_in_dim.3
  8.2 4.5 %all-to-all-start.1 = ((bf16[4,3,64,256]{3,2,1,0:T(8,128)(2,1)}), bf16[4,3,64,256]{3,2,1,0:T(8,128)(2,1)}, u32[]{:S(2)}, u32[]{:S(2)}) async-start(bf16[4,3,64,256]{3,2,1,0:T(8,128)(2,1)} %broadcast_in_dim.3), calls=%async_computation.1 | async-start | bytes 786432 | tf_op jit(solution)/shard_map/all_to_all | solution.py:163
  12.7 0.0 all-gather.3.cloned.1.call-start
  12.7 0.0 copy-start
  12.7 1.2 copy-done
  13.9 0.0 copy-start.1
  13.9 0.7 copy-done.1
  14.6 1.1 shard_map.37.refs_1_
  15.7 5.2 %all-to-all-done.1.refs_0_ = bf16[4,3,64,256]{3,2,1,0:T(8,128)(2,1)} async-done(((bf16[4,3,64,256]{3,2,1,0:T(8,128)(2,1)}), bf16[4,3,64,256]{3,2,1,0:T(8,128)(2,1)}, u32[]{:S(2)}, u32[]{:S(2)}) %all-to-all-start.1) | async-done | bytes 393248 | tf_op jit(solution)/shard_map/all_to_all | solution.py:163
  20.8 0.0 all-gather.3.cloned.1.call-update
  20.9 81.1 %all_to_all.15 = bf16[64,8,1024]{2,1,0:T(8,128)(2,1)S(1)} all-to-all(bf16[64,8,1024]{2,1,0:T(8,128)(2,1)S(1)} %bitcast.7), channel_id=1, replica_groups=mesh['z'=16,'y'=4,'x'=4,'c'=2] {'z','y'}, dimensions={0} | all-to-all | bytes 2097152 | tf_op jit(solution)/shard_map/all_to_all | solution.py:167
  101.9 0.7 shard_map.38
  102.7 2.4 %collective-permute-start.2 = (bf16[128,4096]{1,0:T(8,128)(2,1)S(1)}, bf16[128,4096]{1,0:T(8,128)(2,1)S(1)}, u32[]{:S(2)}, u32[]{:S(2)}) collective-permute-start(bf16[128,4096]{1,0:T(8,128)(2,1)S(1)} %shard_map.38), channel_id=1, source_target_pairs={{0,2},{8,7},{2,4},{10,1},{4,6},{12,3},{6,0},{14,5},{1,10},{9,15},{... | collective-permute-start | bytes 3145736 | tf_op jit(solution)/shard_map/ppermute | solution.py:158
  105.0 3.4 %collective-permute-start.3 = (bf16[128,4096]{1,0:T(8,128)(2,1)S(1)}, bf16[128,4096]{1,0:T(8,128)(2,1)}, u32[]{:S(2)}, u32[]{:S(2)}) collective-permute-start(bf16[128,4096]{1,0:T(8,128)(2,1)S(1)} %shard_map.38), channel_id=1, source_target_pairs={{0,7},{8,2},{2,1},{10,4},{4,3},{12,6},{6,5},{14,0},{1,15},{9,10},{... | collective-permute-start | bytes 3145736 | tf_op jit(solution)/shard_map/ppermute | solution.py:158
  108.5 0.7 collective-permute-start
  109.2 21.3 %collective-permute-done.2.refs_2_ = bf16[128,4096]{1,0:T(8,128)(2,1)S(1)} collective-permute-done((bf16[128,4096]{1,0:T(8,128)(2,1)S(1)}, bf16[128,4096]{1,0:T(8,128)(2,1)S(1)}, u32[]{:S(2)}, u32[]{:S(2)}) %collective-permute-start.2) | collective-permute-done | bytes 1048608 | tf_op jit(solution)/shard_map/ppermute | solution.py:158
  130.5 3.3 %collective-permute-start.6 = (bf16[128,4096]{1,0:T(8,128)(2,1)S(1)}, bf16[128,4096]{1,0:T(8,128)(2,1)S(1)}, u32[]{:S(2)}, u32[]{:S(2)}) collective-permute-start(bf16[128,4096]{1,0:T(8,128)(2,1)S(1)} %collective-permute-done.2.refs_2_), channel_id=1, source_target_pairs={{0,2},{1,7},{2,4},{3,1},{4,6},{5,3},{6,0},{7,5},{8,10},{9,15},{10,... | collective-permute-start | bytes 3145736 | tf_op jit(solution)/shard_map/ppermute | solution.py:147
  133.8 0.0 collective-permute-done.3.refs_0_
  133.9 1.9 collective-permute-start.4
  135.8 2.4 %collective-permute-start.5 = (bf16[128,4096]{1,0:T(8,128)(2,1)S(1)}, bf16[128,4096]{1,0:T(8,128)(2,1)}, u32[]{:S(2)}, u32[]{:S(2)}) collective-permute-start(bf16[128,4096]{1,0:T(8,128)(2,1)S(1)} %collective-permute-done.2.refs_2_), channel_id=1, source_target_pairs={{0,1},{1,0},{2,3},{3,2},{4,5},{5,4},{6,7},{7,6},{8,9},{9,8},{10,11... | collective-permute-start | bytes 3145736 | tf_op jit(solution)/shard_map/ppermute | solution.py:147
  138.2 0.0 collective-permute-done.refs_0_
  138.2 6.8 %collective-permute-start.1 = (bf16[128,4096]{1,0:T(8,128)(2,1)S(1)}, bf16[128,4096]{1,0:T(8,128)(2,1)}, u32[]{:S(2)}, u32[]{:S(2)}) collective-permute-start(bf16[128,4096]{1,0:T(8,128)(2,1)S(1)} %collective-permute-done.refs_0_), channel_id=1, source_target_pairs={{0,1},{1,0},{2,3},{3,2},{4,5},{5,4},{6,7},{7,6},{8,9},{9,8},{10,11... | collective-permute-start | bytes 3145736 | tf_op jit(solution)/shard_map/ppermute | solution.py:147
  145.0 2.2 %collective-permute-done.6.refs_6_ = bf16[128,4096]{1,0:T(8,128)(2,1)S(1)} collective-permute-done((bf16[128,4096]{1,0:T(8,128)(2,1)S(1)}, bf16[128,4096]{1,0:T(8,128)(2,1)S(1)}, u32[]{:S(2)}, u32[]{:S(2)}) %collective-permute-start.6) | collective-permute-done | bytes 1048608 | tf_op jit(solution)/shard_map/ppermute | solution.py:147
  147.2 1.9 collective-permute-start.7
  149.1 0.1 pad_add_fusion.place_ref
  149.2 0.0 collective-permute-done.4.refs_4_
  149.2 0.0 collective-permute-done.5.refs_5_
  149.2 0.0 collective-permute-done.1.refs_1_
  149.2 2.7 %collective-permute-done.7.refs_7_ = bf16[128,4096]{1,0:T(8,128)(2,1)} collective-permute-done((bf16[128,4096]{1,0:T(8,128)(2,1)S(1)}, bf16[128,4096]{1,0:T(8,128)(2,1)}, u32[]{:S(2)}, u32[]{:S(2)}) %collective-permute-start.7) | collective-permute-done | bytes 1048608 | tf_op jit(solution)/shard_map/ppermute | solution.py:147
  151.9 12.9 %shard_map.41 = bf16[64,16,256]{2,1,0:T(8,128)(2,1)S(1)} custom-call(s32[2]{0:T(128)S(1)} %pad_add_fusion.place_ref, bf16[128,4096]{1,0:T(8,128)(2,1)S(1)} %collective-permute-done.refs_0_, bf16[128,4096]{1,0:T(8,128)(2,1)} %collective-permute-done.1.refs_1_, bf16[128,4096]{1,0:T(8,128)(2,1)S(1)} %collective-permute-done.2.refs_2_, ...), custom_call_target="tpu_custom_call" | custom-call | flops 8000000000 | bytes 2097152 | tf_op jit(solution)/shard_map/pallas_call | solution.py:128
  164.8 41.6 %all_to_all.16.mixed_ref = bf16[64,16,256]{2,1,0:T(8,128)(2,1)S(1)} all-to-all(bf16[64,16,256]{2,1,0:T(8,128)(2,1)S(1)} %shard_map.41), channel_id=1, replica_groups=mesh['z'=16,'y'=4,'x'=4,'c'=2] {'z','y'}, dimensions={0} | all-to-all | bytes 1048576 | tf_op jit(solution)/shard_map/all_to_all | solution.py:181
  206.3 1.7 shard_map.42
  (3 shorter events, 0.0 us)
Async XLA Ops:
  8.2 12.6 %all-to-all-start.1 = ((bf16[4,3,64,256]{3,2,1,0:T(8,128)(2,1)}), bf16[4,3,64,256]{3,2,1,0:T(8,128)(2,1)}, u32[]{:S(2)}, u32[]{:S(2)}) async-start(bf16[4,3,64,256]{3,2,1,0:T(8,128)(2,1)} %broadcast_in_dim.3), calls=%async_computation.1 | async-start | bytes 786432 | tf_op jit(solution)/shard_map/all_to_all | solution.py:163
  12.7 139.2 %all-gather.3.cloned.1.call-start = ((), (), s32[]{:S(2)}) async-start(), calls=%async_computation.3 | async-start | bytes 6684672 | tf_op jit(solution)/shard_map/all_gather | solution.py:166
  12.7 1.2 copy-start
  13.9 0.7 copy-start.1
  102.7 27.9 %collective-permute-start.2 = (bf16[128,4096]{1,0:T(8,128)(2,1)S(1)}, bf16[128,4096]{1,0:T(8,128)(2,1)S(1)}, u32[]{:S(2)}, u32[]{:S(2)}) collective-permute-start(bf16[128,4096]{1,0:T(8,128)(2,1)S(1)} %shard_map.38), channel_id=1, source_target_pairs={{0,2},{8,7},{2,4},{10,1},{4,6},{12,3},{6,0},{14,5},{1,10},{9,15},{... | collective-permute-start | bytes 3145736 | tf_op jit(solution)/shard_map/ppermute | solution.py:158
  105.0 28.8 %collective-permute-start.3 = (bf16[128,4096]{1,0:T(8,128)(2,1)S(1)}, bf16[128,4096]{1,0:T(8,128)(2,1)}, u32[]{:S(2)}, u32[]{:S(2)}) collective-permute-start(bf16[128,4096]{1,0:T(8,128)(2,1)S(1)} %shard_map.38), channel_id=1, source_target_pairs={{0,7},{8,2},{2,1},{10,4},{4,3},{12,6},{6,5},{14,0},{1,15},{9,10},{... | collective-permute-start | bytes 3145736 | tf_op jit(solution)/shard_map/ppermute | solution.py:158
  108.5 29.7 %collective-permute-start = (bf16[128,4096]{1,0:T(8,128)(2,1)S(1)}, bf16[128,4096]{1,0:T(8,128)(2,1)S(1)}, u32[]{:S(2)}, u32[]{:S(2)}) collective-permute-start(bf16[128,4096]{1,0:T(8,128)(2,1)S(1)} %shard_map.38), channel_id=1, source_target_pairs={{0,0},{8,1},{2,2},{10,3},{4,4},{12,5},{6,6},{14,7},{1,8},{9,9},{3,... | collective-permute-start | bytes 3145736 | tf_op jit(solution)/shard_map/ppermute | solution.py:158
  130.5 16.7 %collective-permute-start.6 = (bf16[128,4096]{1,0:T(8,128)(2,1)S(1)}, bf16[128,4096]{1,0:T(8,128)(2,1)S(1)}, u32[]{:S(2)}, u32[]{:S(2)}) collective-permute-start(bf16[128,4096]{1,0:T(8,128)(2,1)S(1)} %collective-permute-done.2.refs_2_), channel_id=1, source_target_pairs={{0,2},{1,7},{2,4},{3,1},{4,6},{5,3},{6,0},{7,5},{8,10},{9,15},{10,... | collective-permute-start | bytes 3145736 | tf_op jit(solution)/shard_map/ppermute | solution.py:147
  133.9 15.4 %collective-permute-start.4 = (bf16[128,4096]{1,0:T(8,128)(2,1)}, bf16[128,4096]{1,0:T(8,128)(2,1)}, u32[]{:S(2)}, u32[]{:S(2)}) collective-permute-start(bf16[128,4096]{1,0:T(8,128)(2,1)} %shard_map.39.refs_3_), channel_id=1, source_target_pairs={{0,1},{1,0},{2,3},{3,2},{4,5},{5,4},{6,7},{7,6},{8,9},{9,8},{10,11... | collective-permute-start | bytes 3145736 | tf_op jit(solution)/shard_map/ppermute | solution.py:147
  135.8 13.4 %collective-permute-start.5 = (bf16[128,4096]{1,0:T(8,128)(2,1)S(1)}, bf16[128,4096]{1,0:T(8,128)(2,1)}, u32[]{:S(2)}, u32[]{:S(2)}) collective-permute-start(bf16[128,4096]{1,0:T(8,128)(2,1)S(1)} %collective-permute-done.2.refs_2_), channel_id=1, source_target_pairs={{0,1},{1,0},{2,3},{3,2},{4,5},{5,4},{6,7},{7,6},{8,9},{9,8},{10,11... | collective-permute-start | bytes 3145736 | tf_op jit(solution)/shard_map/ppermute | solution.py:147
  138.2 11.0 %collective-permute-start.1 = (bf16[128,4096]{1,0:T(8,128)(2,1)S(1)}, bf16[128,4096]{1,0:T(8,128)(2,1)}, u32[]{:S(2)}, u32[]{:S(2)}) collective-permute-start(bf16[128,4096]{1,0:T(8,128)(2,1)S(1)} %collective-permute-done.refs_0_), channel_id=1, source_target_pairs={{0,1},{1,0},{2,3},{3,2},{4,5},{5,4},{6,7},{7,6},{8,9},{9,8},{10,11... | collective-permute-start | bytes 3145736 | tf_op jit(solution)/shard_map/ppermute | solution.py:147
  147.2 4.7 %collective-permute-start.7 = (bf16[128,4096]{1,0:T(8,128)(2,1)S(1)}, bf16[128,4096]{1,0:T(8,128)(2,1)}, u32[]{:S(2)}, u32[]{:S(2)}) collective-permute-start(bf16[128,4096]{1,0:T(8,128)(2,1)S(1)} %collective-permute-done.6.refs_6_), channel_id=1, source_target_pairs={{0,1},{1,0},{2,3},{3,2},{4,5},{5,4},{6,7},{7,6},{8,9},{9,8},{10,11... | collective-permute-start | bytes 3145736 | tf_op jit(solution)/shard_map/ppermute | solution.py:147
Sparse Core Ops, SparseCore 0:
  21.0 128.7 all-gather.2

commit v9 on v8

--- a/solution.py
+++ b/solution.py
@@ -170,10 +170,10 @@
     straight = send_home(rows, lambda x, c: (x + 1 - 2 * c, c))
     crossed = send_home(rows, lambda x, c: (x - 1 + 2 * c, 1 - c))
     own = send_home(rows, lambda x, c: (x, c))
-    far = send(straight, lambda x, c: (x + 1 - 2 * c, c))
+    far = send(crossed, lambda x, c: (x + 1 - 2 * c, c))
     swap = lambda part: send(part, lambda x, c: (x, 1 - c))
-    held = call(hold_kernel, [crossed.shape], crossed, flops=10**10, in_place=True)[0]
-    tokens = (own, swap(own), straight, held, swap(held), swap(straight), far, swap(far))
+    held = call(hold_kernel, [straight.shape], straight, flops=10**10, in_place=True)[0]
+    tokens = (own, swap(own), held, crossed, swap(crossed), swap(held), swap(far), far)
     mixed = call(
         patches_kernel, (64, 16, 256), place, *tokens, weights, flops=8 * 10**9, far=range(1, 10), limit=44,
         scratch=(VMEM((1024, D), BF), VMEM((Z, Y, 3, 64, 256), BF), pltpu.SemaphoreType.DMA((4, 9))),

time: 215 us -> 215 us (level)
    ppermute x3, waiting for transfers between devices: 21.3 us -> 23.6 us  [send_home(): return lax.ppermute(rows, ('y', 'x', 'c'), pairs)]
where the time goes in v9:
time: 215 us
  blocking collectives  122 us (57%)
  waiting for transfers between devices  33.5 us (16%)
  starting transfers between devices  25.9 us (12%)
  Pallas kernels  16.3 us (8%)
  between operations  13.5 us (6%)
  local copies, waits for them, and re-layouts  3.61 us (2%)
    all_to_all x1, blocking collectives, shards(): lax.all_to_all(packed.reshape(64, 8, 1024), ('z', 'y'), 0, 0, tiled=True)  81.1 us
    all_to_all x1, blocking collectives, shards(): mixed = lax.all_to_all(mixed, ('z', 'y'), 0, 0, tiled=True)  40.8 us
    ppermute x3, waiting for transfers between devices, send_home(): return lax.ppermute(rows, ('y', 'x', 'c'), pairs)  23.6 us
    ppermute x5, starting transfers between devices, send(): return lax.ppermute(rows, ('x', 'c'), pairs)  16.4 us
    pallas_call x6, Pallas kernels, call(): pl.pallas_call(kernel, out_shape=[jax.ShapeDtypeStruct(shape, BF) for sha...  16.3 us
    all_to_all x1, waiting for transfers between devices, shards(): weights = lax.all_to_all(weights, 'y', 0, 0, tiled=True)  5.17 us
    ppermute x3, starting transfers between devices, send_home(): return lax.ppermute(rows, ('y', 'x', 'c'), pairs)  5.01 us
    ppermute x5, waiting for transfers between devices, send(): return lax.ppermute(rows, ('x', 'c'), pairs)  4.81 us
  transfers between devices with their start and end apart: 10, of which 4 were waited for; matrix products, arithmetic and copies ran while one was open for 0% of the time, Pallas kernels for 1%

profile of v9, /device:TPU:6, one launch (start us, length us, event | category | flops | bytes accessed | tf_op | source)
XLA Modules:
  0.0 214.8 jit_solution(16067925276812652858)
XLA Ops:
  6.5 1.7 broadcast_in_dim.3
  8.2 4.5 %all-to-all-start.1 = ((bf16[4,3,64,256]{3,2,1,0:T(8,128)(2,1)}), bf16[4,3,64,256]{3,2,1,0:T(8,128)(2,1)}, u32[]{:S(2)}, u32[]{:S(2)}) async-start(bf16[4,3,64,256]{3,2,1,0:T(8,128)(2,1)} %broadcast_in_dim.3), calls=%async_computation.1 | async-start | bytes 786432 | tf_op jit(solution)/shard_map/all_to_all | solution.py:163
  12.7 0.0 all-gather.3.cloned.1.call-start
  12.7 0.0 copy-start
  12.7 1.2 copy-done
  13.9 0.0 copy-start.1
  13.9 0.7 copy-done.1
  14.6 1.1 shard_map.37.refs_1_
  15.7 5.2 %all-to-all-done.1.refs_0_ = bf16[4,3,64,256]{3,2,1,0:T(8,128)(2,1)} async-done(((bf16[4,3,64,256]{3,2,1,0:T(8,128)(2,1)}), bf16[4,3,64,256]{3,2,1,0:T(8,128)(2,1)}, u32[]{:S(2)}, u32[]{:S(2)}) %all-to-all-start.1) | async-done | bytes 393248 | tf_op jit(solution)/shard_map/all_to_all | solution.py:163
  20.8 0.0 all-gather.3.cloned.1.call-update
  20.9 81.1 %all_to_all.15 = bf16[64,8,1024]{2,1,0:T(8,128)(2,1)S(1)} all-to-all(bf16[64,8,1024]{2,1,0:T(8,128)(2,1)S(1)} %bitcast.7), channel_id=1, replica_groups=mesh['z'=16,'y'=4,'x'=4,'c'=2] {'z','y'}, dimensions={0} | all-to-all | bytes 2097152 | tf_op jit(solution)/shard_map/all_to_all | solution.py:167
  101.9 0.7 shard_map.38
  102.7 1.9 collective-permute-start.3
  104.6 2.4 %collective-permute-start.2 = (bf16[128,4096]{1,0:T(8,128)(2,1)S(1)}, bf16[128,4096]{1,0:T(8,128)(2,1)}, u32[]{:S(2)}, u32[]{:S(2)}) collective-permute-start(bf16[128,4096]{1,0:T(8,128)(2,1)S(1)} %shard_map.38), channel_id=1, source_target_pairs={{0,2},{8,7},{2,4},{10,1},{4,6},{12,3},{6,0},{14,5},{1,10},{9,15},{... | collective-permute-start | bytes 3145736 | tf_op jit(solution)/shard_map/ppermute | solution.py:158
  107.0 0.7 collective-permute-start
  107.7 23.5 %collective-permute-done.3.refs_3_ = bf16[128,4096]{1,0:T(8,128)(2,1)S(1)} collective-permute-done((bf16[128,4096]{1,0:T(8,128)(2,1)S(1)}, bf16[128,4096]{1,0:T(8,128)(2,1)S(1)}, u32[]{:S(2)}, u32[]{:S(2)}) %collective-permute-start.3) | collective-permute-done | bytes 1048608 | tf_op jit(solution)/shard_map/ppermute | solution.py:158
  131.2 3.3 %collective-permute-start.6 = (bf16[128,4096]{1,0:T(8,128)(2,1)S(1)}, bf16[128,4096]{1,0:T(8,128)(2,1)S(1)}, u32[]{:S(2)}, u32[]{:S(2)}) collective-permute-start(bf16[128,4096]{1,0:T(8,128)(2,1)S(1)} %collective-permute-done.3.refs_3_), channel_id=1, source_target_pairs={{0,2},{1,7},{2,4},{3,1},{4,6},{5,3},{6,0},{7,5},{8,10},{9,15},{10,... | collective-permute-start | bytes 3145736 | tf_op jit(solution)/shard_map/ppermute | solution.py:147
  134.6 0.0 collective-permute-done.2.refs_0_
  134.6 1.9 collective-permute-start.5
  136.5 2.4 %collective-permute-start.4 = (bf16[128,4096]{1,0:T(8,128)(2,1)S(1)}, bf16[128,4096]{1,0:T(8,128)(2,1)}, u32[]{:S(2)}, u32[]{:S(2)}) collective-permute-start(bf16[128,4096]{1,0:T(8,128)(2,1)S(1)} %collective-permute-done.3.refs_3_), channel_id=1, source_target_pairs={{0,1},{1,0},{2,3},{3,2},{4,5},{5,4},{6,7},{7,6},{8,9},{9,8},{10,11... | collective-permute-start | bytes 3145736 | tf_op jit(solution)/shard_map/ppermute | solution.py:147
  138.9 0.0 collective-permute-done.refs_0_
  138.9 6.9 %collective-permute-start.1 = (bf16[128,4096]{1,0:T(8,128)(2,1)S(1)}, bf16[128,4096]{1,0:T(8,128)(2,1)}, u32[]{:S(2)}, u32[]{:S(2)}) collective-permute-start(bf16[128,4096]{1,0:T(8,128)(2,1)S(1)} %collective-permute-done.refs_0_), channel_id=1, source_target_pairs={{0,1},{1,0},{2,3},{3,2},{4,5},{5,4},{6,7},{7,6},{8,9},{9,8},{10,11... | collective-permute-start | bytes 3145736 | tf_op jit(solution)/shard_map/ppermute | solution.py:147
  145.8 2.1 collective-permute-done.6.refs_7_
  147.9 1.9 collective-permute-start.7
  149.9 0.1 pad_add_fusion.place_ref
  149.9 0.0 collective-permute-done.4.refs_4_
  149.9 0.0 collective-permute-done.5.refs_5_
  149.9 0.0 collective-permute-done.1.refs_1_
  149.9 2.7 %collective-permute-done.7.refs_6_ = bf16[128,4096]{1,0:T(8,128)(2,1)} collective-permute-done((bf16[128,4096]{1,0:T(8,128)(2,1)S(1)}, bf16[128,4096]{1,0:T(8,128)(2,1)}, u32[]{:S(2)}, u32[]{:S(2)}) %collective-permute-start.7) | collective-permute-done | bytes 1048608 | tf_op jit(solution)/shard_map/ppermute | solution.py:147
  152.6 12.9 %shard_map.41 = bf16[64,16,256]{2,1,0:T(8,128)(2,1)S(1)} custom-call(s32[2]{0:T(128)S(1)} %pad_add_fusion.place_ref, bf16[128,4096]{1,0:T(8,128)(2,1)S(1)} %collective-permute-done.refs_0_, bf16[128,4096]{1,0:T(8,128)(2,1)} %collective-permute-done.1.refs_1_, bf16[128,4096]{1,0:T(8,128)(2,1)} %shard_map.39.refs_2_, ...), custom_call_target="tpu_custom_call" | custom-call | flops 8000000000 | bytes 2097152 | tf_op jit(solution)/shard_map/pallas_call | solution.py:128
  165.5 40.8 %all_to_all.16.mixed_ref = bf16[64,16,256]{2,1,0:T(8,128)(2,1)S(1)} all-to-all(bf16[64,16,256]{2,1,0:T(8,128)(2,1)S(1)} %shard_map.41), channel_id=1, replica_groups=mesh['z'=16,'y'=4,'x'=4,'c'=2] {'z','y'}, dimensions={0} | all-to-all | bytes 1048576 | tf_op jit(solution)/shard_map/all_to_all | solution.py:181
  206.3 1.7 shard_map.42
  (3 shorter events, 0.0 us)
Async XLA Ops:
  8.2 12.6 %all-to-all-start.1 = ((bf16[4,3,64,256]{3,2,1,0:T(8,128)(2,1)}), bf16[4,3,64,256]{3,2,1,0:T(8,128)(2,1)}, u32[]{:S(2)}, u32[]{:S(2)}) async-start(bf16[4,3,64,256]{3,2,1,0:T(8,128)(2,1)} %broadcast_in_dim.3), calls=%async_computation.1 | async-start | bytes 786432 | tf_op jit(solution)/shard_map/all_to_all | solution.py:163
  12.7 139.9 %all-gather.3.cloned.1.call-start = ((), (), s32[]{:S(2)}) async-start(), calls=%async_computation.3 | async-start | bytes 6684672 | tf_op jit(solution)/shard_map/all_gather | solution.py:166
  12.7 1.2 copy-start
  13.9 0.7 copy-start.1
  102.7 28.6 %collective-permute-start.3 = (bf16[128,4096]{1,0:T(8,128)(2,1)S(1)}, bf16[128,4096]{1,0:T(8,128)(2,1)S(1)}, u32[]{:S(2)}, u32[]{:S(2)}) collective-permute-start(bf16[128,4096]{1,0:T(8,128)(2,1)S(1)} %shard_map.38), channel_id=1, source_target_pairs={{0,7},{8,2},{2,1},{10,4},{4,3},{12,6},{6,5},{14,0},{1,15},{9,10},{... | collective-permute-start | bytes 3145736 | tf_op jit(solution)/shard_map/ppermute | solution.py:158
  104.6 30.0 %collective-permute-start.2 = (bf16[128,4096]{1,0:T(8,128)(2,1)S(1)}, bf16[128,4096]{1,0:T(8,128)(2,1)}, u32[]{:S(2)}, u32[]{:S(2)}) collective-permute-start(bf16[128,4096]{1,0:T(8,128)(2,1)S(1)} %shard_map.38), channel_id=1, source_target_pairs={{0,2},{8,7},{2,4},{10,1},{4,6},{12,3},{6,0},{14,5},{1,10},{9,15},{... | collective-permute-start | bytes 3145736 | tf_op jit(solution)/shard_map/ppermute | solution.py:158
  107.0 32.0 %collective-permute-start = (bf16[128,4096]{1,0:T(8,128)(2,1)S(1)}, bf16[128,4096]{1,0:T(8,128)(2,1)S(1)}, u32[]{:S(2)}, u32[]{:S(2)}) collective-permute-start(bf16[128,4096]{1,0:T(8,128)(2,1)S(1)} %shard_map.38), channel_id=1, source_target_pairs={{0,0},{8,1},{2,2},{10,3},{4,4},{12,5},{6,6},{14,7},{1,8},{9,9},{3,... | collective-permute-start | bytes 3145736 | tf_op jit(solution)/shard_map/ppermute | solution.py:158
  131.2 16.7 %collective-permute-start.6 = (bf16[128,4096]{1,0:T(8,128)(2,1)S(1)}, bf16[128,4096]{1,0:T(8,128)(2,1)S(1)}, u32[]{:S(2)}, u32[]{:S(2)}) collective-permute-start(bf16[128,4096]{1,0:T(8,128)(2,1)S(1)} %collective-permute-done.3.refs_3_), channel_id=1, source_target_pairs={{0,2},{1,7},{2,4},{3,1},{4,6},{5,3},{6,0},{7,5},{8,10},{9,15},{10,... | collective-permute-start | bytes 3145736 | tf_op jit(solution)/shard_map/ppermute | solution.py:147
  134.6 15.4 %collective-permute-start.5 = (bf16[128,4096]{1,0:T(8,128)(2,1)}, bf16[128,4096]{1,0:T(8,128)(2,1)}, u32[]{:S(2)}, u32[]{:S(2)}) collective-permute-start(bf16[128,4096]{1,0:T(8,128)(2,1)} %shard_map.39.refs_2_), channel_id=1, source_target_pairs={{0,1},{1,0},{2,3},{3,2},{4,5},{5,4},{6,7},{7,6},{8,9},{9,8},{10,11... | collective-permute-start | bytes 3145736 | tf_op jit(solution)/shard_map/ppermute | solution.py:147
  136.5 13.4 %collective-permute-start.4 = (bf16[128,4096]{1,0:T(8,128)(2,1)S(1)}, bf16[128,4096]{1,0:T(8,128)(2,1)}, u32[]{:S(2)}, u32[]{:S(2)}) collective-permute-start(bf16[128,4096]{1,0:T(8,128)(2,1)S(1)} %collective-permute-done.3.refs_3_), channel_id=1, source_target_pairs={{0,1},{1,0},{2,3},{3,2},{4,5},{5,4},{6,7},{7,6},{8,9},{9,8},{10,11... | collective-permute-start | bytes 3145736 | tf_op jit(solution)/shard_map/ppermute | solution.py:147
  138.9 11.0 %collective-permute-start.1 = (bf16[128,4096]{1,0:T(8,128)(2,1)S(1)}, bf16[128,4096]{1,0:T(8,128)(2,1)}, u32[]{:S(2)}, u32[]{:S(2)}) collective-permute-start(bf16[128,4096]{1,0:T(8,128)(2,1)S(1)} %collective-permute-done.refs_0_), channel_id=1, source_target_pairs={{0,1},{1,0},{2,3},{3,2},{4,5},{5,4},{6,7},{7,6},{8,9},{9,8},{10,11... | collective-permute-start | bytes 3145736 | tf_op jit(solution)/shard_map/ppermute | solution.py:147
  147.9 4.7 %collective-permute-start.7 = (bf16[128,4096]{1,0:T(8,128)(2,1)S(1)}, bf16[128,4096]{1,0:T(8,128)(2,1)}, u32[]{:S(2)}, u32[]{:S(2)}) collective-permute-start(bf16[128,4096]{1,0:T(8,128)(2,1)S(1)} %collective-permute-done.6.refs_7_), channel_id=1, source_target_pairs={{0,1},{1,0},{2,3},{3,2},{4,5},{5,4},{6,7},{7,6},{8,9},{9,8},{10,11... | collective-permute-start | bytes 3145736 | tf_op jit(solution)/shard_map/ppermute | solution.py:147
Sparse Core Ops, SparseCore 0:
  21.0 128.7 all-gather.2

commit v10 on v8

--- a/solution.py
+++ b/solution.py
@@ -27,7 +27,7 @@
     rows = frames_ref[...].reshape(128, D).astype(F32)
     scale = lax.rsqrt(jnp.mean(rows * rows, axis=-1, keepdims=True) + 1e-05)
     shuffle = one_hot(
-        lambda i: (i & 3) * 128 + ((i >> 3) & 1) * 64 + ((i >> 2) & 1) * 32 + (i >> 4), 512, 512
+        lambda i: (i & 3) * 128 + ((i >> 7) & 1) * 64 + ((i >> 2) & 1) * 32 + ((i >> 3) & 15) * 2 + (i >> 8), 512, 512
     )
     for j in range(2):
         cuts = [slice(1024 * q + 512 * j, 1024 * q + 512 * (j + 1)) for q in range(4)]
@@ -37,7 +37,7 @@
 
 def merge_kernel(in_ref, out_ref):
     for q in range(4):
-        order = one_hot(lambda i: i * 4 + q, 128, 512)
+        order = one_hot(lambda i: ((((i >> 1) & 3) * 16 + (i >> 3)) * 2 + (i & 1)) * 4 + q, 128, 512)
         for j in range(2):
             start = 1024 * q + 512 * j
             out_ref[:, start : start + 512] = pick(order, in_ref[:, 512 * j : 512 * (j + 1)])
@@ -164,7 +164,7 @@
     packed = call(normalize_kernel, (512, 1024), frames, norm_gain.reshape(1, D))
     weights = call(hold_kernel, [weights.shape], weights, packed, in_place=True)[0]
     weights = lax.all_gather(weights, "z", axis=0)
-    spread = lax.all_to_all(packed.reshape(64, 8, 1024), ("z", "y"), 0, 0, tiled=True)
+    spread = lax.all_to_all(packed.reshape(64, 8, 1024), ("y", "z"), 0, 0, tiled=True)
     rows = call(merge_kernel, (128, D), spread.reshape(512, 1024))
     place = jnp.stack([lax.axis_index("x"), lax.axis_index("c")]).astype(jnp.int32)
     straight = send_home(rows, lambda x, c: (x + 1 - 2 * c, c))

time: 215 us -> 215 us (level)
  transfers between devices with their start and end apart: 10 -> 10, of which waited for: 4 -> 5; matrix products, arithmetic and copies ran while one was open for 0% -> 0% of each run, Pallas kernels for 1% -> 1%
where the time goes in v10:
time: 215 us
  blocking collectives  123 us (57%)
  waiting for transfers between devices  30.8 us (14%)
  starting transfers between devices  28 us (13%)
  Pallas kernels  16.3 us (8%)
  between operations  13.5 us (6%)
  local copies, waits for them, and re-layouts  3.61 us (2%)
    all_to_all x1, blocking collectives, shards(): lax.all_to_all(packed.reshape(64, 8, 1024), ('y', 'z'), 0, 0, tiled=True)  79.8 us
    all_to_all x1, blocking collectives, shards(): mixed = lax.all_to_all(mixed, ('z', 'y'), 0, 0, tiled=True)  42.8 us
    ppermute x3, waiting for transfers between devices, send_home(): return lax.ppermute(rows, ('y', 'x', 'c'), pairs)  20.9 us
    ppermute x5, starting transfers between devices, send(): return lax.ppermute(rows, ('x', 'c'), pairs)  16.4 us
    pallas_call x6, Pallas kernels, call(): pl.pallas_call(kernel, out_shape=[jax.ShapeDtypeStruct(shape, BF) for sha...  16.3 us
    ppermute x3, starting transfers between devices, send_home(): return lax.ppermute(rows, ('y', 'x', 'c'), pairs)  7.13 us
    all_to_all x1, waiting for transfers between devices, shards(): weights = lax.all_to_all(weights, 'y', 0, 0, tiled=True)  5.15 us
    ppermute x5, waiting for transfers between devices, send(): return lax.ppermute(rows, ('x', 'c'), pairs)  4.65 us
  transfers between devices with their start and end apart: 10, of which 5 were waited for; matrix products, arithmetic and copies ran while one was open for 0% of the time, Pallas kernels for 1%

profile of v10, /device:TPU:6, one launch (start us, length us, event | category | flops | bytes accessed | tf_op | source)
XLA Modules:
  0.0 214.9 jit_solution(18177852700389700579)
XLA Ops:
  6.5 1.7 broadcast_in_dim.3
  8.2 4.5 %all-to-all-start.1 = ((bf16[4,3,64,256]{3,2,1,0:T(8,128)(2,1)}), bf16[4,3,64,256]{3,2,1,0:T(8,128)(2,1)}, u32[]{:S(2)}, u32[]{:S(2)}) async-start(bf16[4,3,64,256]{3,2,1,0:T(8,128)(2,1)} %broadcast_in_dim.3), calls=%async_computation.1 | async-start | bytes 786432 | tf_op jit(solution)/shard_map/all_to_all | solution.py:163
  12.7 0.0 all-gather.3.cloned.1.call-start
  12.7 1.2 copy-done
  13.9 0.0 copy-start.1
  13.9 0.7 copy-done.1
  14.6 1.1 shard_map.37.refs_1_
  15.7 5.2 %all-to-all-done.1.refs_0_ = bf16[4,3,64,256]{3,2,1,0:T(8,128)(2,1)} async-done(((bf16[4,3,64,256]{3,2,1,0:T(8,128)(2,1)}), bf16[4,3,64,256]{3,2,1,0:T(8,128)(2,1)}, u32[]{:S(2)}, u32[]{:S(2)}) %all-to-all-start.1) | async-done | bytes 393248 | tf_op jit(solution)/shard_map/all_to_all | solution.py:163
  20.8 0.0 all-gather.3.cloned.1.call-update
  20.9 79.8 %all_to_all.15 = bf16[64,8,1024]{2,1,0:T(8,128)(2,1)S(1)} all-to-all(bf16[64,8,1024]{2,1,0:T(8,128)(2,1)S(1)} %bitcast.7), channel_id=1, replica_groups=mesh['z'=16,'y'=4,'x'=4,'c'=2] {'y','z'}, dimensions={0} | all-to-all | bytes 2097152 | tf_op jit(solution)/shard_map/all_to_all | solution.py:167
  100.7 0.7 shard_map.38
  101.4 2.4 %collective-permute-start.2 = (bf16[128,4096]{1,0:T(8,128)(2,1)S(1)}, bf16[128,4096]{1,0:T(8,128)(2,1)S(1)}, u32[]{:S(2)}, u32[]{:S(2)}) collective-permute-start(bf16[128,4096]{1,0:T(8,128)(2,1)S(1)} %shard_map.38), channel_id=1, source_target_pairs={{0,2},{8,7},{2,4},{10,1},{4,6},{12,3},{6,0},{14,5},{1,10},{9,15},{... | collective-permute-start | bytes 3145736 | tf_op jit(solution)/shard_map/ppermute | solution.py:158
  103.9 4.0 %collective-permute-start.3 = (bf16[128,4096]{1,0:T(8,128)(2,1)S(1)}, bf16[128,4096]{1,0:T(8,128)(2,1)}, u32[]{:S(2)}, u32[]{:S(2)}) collective-permute-start(bf16[128,4096]{1,0:T(8,128)(2,1)S(1)} %shard_map.38), channel_id=1, source_target_pairs={{0,7},{8,2},{2,1},{10,4},{4,3},{12,6},{6,5},{14,0},{1,15},{9,10},{... | collective-permute-start | bytes 3145736 | tf_op jit(solution)/shard_map/ppermute | solution.py:158
  107.9 0.7 collective-permute-start
  108.6 20.8 %collective-permute-done.2.refs_2_ = bf16[128,4096]{1,0:T(8,128)(2,1)S(1)} collective-permute-done((bf16[128,4096]{1,0:T(8,128)(2,1)S(1)}, bf16[128,4096]{1,0:T(8,128)(2,1)S(1)}, u32[]{:S(2)}, u32[]{:S(2)}) %collective-permute-start.2) | collective-permute-done | bytes 1048608 | tf_op jit(solution)/shard_map/ppermute | solution.py:158
  129.4 3.3 %collective-permute-start.6 = (bf16[128,4096]{1,0:T(8,128)(2,1)S(1)}, bf16[128,4096]{1,0:T(8,128)(2,1)S(1)}, u32[]{:S(2)}, u32[]{:S(2)}) collective-permute-start(bf16[128,4096]{1,0:T(8,128)(2,1)S(1)} %collective-permute-done.2.refs_2_), channel_id=1, source_target_pairs={{0,2},{1,7},{2,4},{3,1},{4,6},{5,3},{6,0},{7,5},{8,10},{9,15},{10,... | collective-permute-start | bytes 3145736 | tf_op jit(solution)/shard_map/ppermute | solution.py:147
  132.7 0.2 collective-permute-done.3.refs_0_
  132.9 1.9 collective-permute-start.4
  134.8 2.4 %collective-permute-start.5 = (bf16[128,4096]{1,0:T(8,128)(2,1)S(1)}, bf16[128,4096]{1,0:T(8,128)(2,1)}, u32[]{:S(2)}, u32[]{:S(2)}) collective-permute-start(bf16[128,4096]{1,0:T(8,128)(2,1)S(1)} %collective-permute-done.2.refs_2_), channel_id=1, source_target_pairs={{0,1},{1,0},{2,3},{3,2},{4,5},{5,4},{6,7},{7,6},{8,9},{9,8},{10,11... | collective-permute-start | bytes 3145736 | tf_op jit(solution)/shard_map/ppermute | solution.py:147
  137.2 0.0 collective-permute-done.refs_0_
  137.2 6.8 %collective-permute-start.1 = (bf16[128,4096]{1,0:T(8,128)(2,1)S(1)}, bf16[128,4096]{1,0:T(8,128)(2,1)}, u32[]{:S(2)}, u32[]{:S(2)}) collective-permute-start(bf16[128,4096]{1,0:T(8,128)(2,1)S(1)} %collective-permute-done.refs_0_), channel_id=1, source_target_pairs={{0,1},{1,0},{2,3},{3,2},{4,5},{5,4},{6,7},{7,6},{8,9},{9,8},{10,11... | collective-permute-start | bytes 3145736 | tf_op jit(solution)/shard_map/ppermute | solution.py:147
  144.1 2.0 collective-permute-done.6.refs_6_
  146.1 1.9 collective-permute-start.7
  148.0 0.1 pad_add_fusion.place_ref
  148.1 0.0 collective-permute-done.4.refs_4_
  148.1 0.0 collective-permute-done.5.refs_5_
  148.1 0.0 collective-permute-done.1.refs_1_
  148.1 2.7 %collective-permute-done.7.refs_7_ = bf16[128,4096]{1,0:T(8,128)(2,1)} collective-permute-done((bf16[128,4096]{1,0:T(8,128)(2,1)S(1)}, bf16[128,4096]{1,0:T(8,128)(2,1)}, u32[]{:S(2)}, u32[]{:S(2)}) %collective-permute-start.7) | collective-permute-done | bytes 1048608 | tf_op jit(solution)/shard_map/ppermute | solution.py:147
  150.7 0.0 all-gather.3.cloned.1.call-done
  150.7 12.9 %shard_map.41 = bf16[64,16,256]{2,1,0:T(8,128)(2,1)S(1)} custom-call(s32[2]{0:T(128)S(1)} %pad_add_fusion.place_ref, bf16[128,4096]{1,0:T(8,128)(2,1)S(1)} %collective-permute-done.refs_0_, bf16[128,4096]{1,0:T(8,128)(2,1)} %collective-permute-done.1.refs_1_, bf16[128,4096]{1,0:T(8,128)(2,1)S(1)} %collective-permute-done.2.refs_2_, ...), custom_call_target="tpu_custom_call" | custom-call | flops 8000000000 | bytes 2097152 | tf_op jit(solution)/shard_map/pallas_call | solution.py:128
  163.6 42.8 %all_to_all.16.mixed_ref = bf16[64,16,256]{2,1,0:T(8,128)(2,1)S(1)} all-to-all(bf16[64,16,256]{2,1,0:T(8,128)(2,1)S(1)} %shard_map.41), channel_id=1, replica_groups=mesh['z'=16,'y'=4,'x'=4,'c'=2] {'z','y'}, dimensions={0} | all-to-all | bytes 1048576 | tf_op jit(solution)/shard_map/all_to_all | solution.py:181
  206.4 1.7 shard_map.42
  (3 shorter events, 0.0 us)
Async XLA Ops:
  8.2 12.6 %all-to-all-start.1 = ((bf16[4,3,64,256]{3,2,1,0:T(8,128)(2,1)}), bf16[4,3,64,256]{3,2,1,0:T(8,128)(2,1)}, u32[]{:S(2)}, u32[]{:S(2)}) async-start(bf16[4,3,64,256]{3,2,1,0:T(8,128)(2,1)} %broadcast_in_dim.3), calls=%async_computation.1 | async-start | bytes 786432 | tf_op jit(solution)/shard_map/all_to_all | solution.py:163
  12.7 138.1 %all-gather.3.cloned.1.call-start = ((), (), s32[]{:S(2)}) async-start(), calls=%async_computation.3 | async-start | bytes 6684672 | tf_op jit(solution)/shard_map/all_gather | solution.py:166
  12.7 1.2 copy-start
  13.9 0.7 copy-start.1
  101.4 27.9 %collective-permute-start.2 = (bf16[128,4096]{1,0:T(8,128)(2,1)S(1)}, bf16[128,4096]{1,0:T(8,128)(2,1)S(1)}, u32[]{:S(2)}, u32[]{:S(2)}) collective-permute-start(bf16[128,4096]{1,0:T(8,128)(2,1)S(1)} %shard_map.38), channel_id=1, source_target_pairs={{0,2},{8,7},{2,4},{10,1},{4,6},{12,3},{6,0},{14,5},{1,10},{9,15},{... | collective-permute-start | bytes 3145736 | tf_op jit(solution)/shard_map/ppermute | solution.py:158
  103.9 29.1 %collective-permute-start.3 = (bf16[128,4096]{1,0:T(8,128)(2,1)S(1)}, bf16[128,4096]{1,0:T(8,128)(2,1)}, u32[]{:S(2)}, u32[]{:S(2)}) collective-permute-start(bf16[128,4096]{1,0:T(8,128)(2,1)S(1)} %shard_map.38), channel_id=1, source_target_pairs={{0,7},{8,2},{2,1},{10,4},{4,3},{12,6},{6,5},{14,0},{1,15},{9,10},{... | collective-permute-start | bytes 3145736 | tf_op jit(solution)/shard_map/ppermute | solution.py:158
  107.9 29.4 %collective-permute-start = (bf16[128,4096]{1,0:T(8,128)(2,1)S(1)}, bf16[128,4096]{1,0:T(8,128)(2,1)S(1)}, u32[]{:S(2)}, u32[]{:S(2)}) collective-permute-start(bf16[128,4096]{1,0:T(8,128)(2,1)S(1)} %shard_map.38), channel_id=1, source_target_pairs={{0,0},{8,1},{2,2},{10,3},{4,4},{12,5},{6,6},{14,7},{1,8},{9,9},{3,... | collective-permute-start | bytes 3145736 | tf_op jit(solution)/shard_map/ppermute | solution.py:158
  129.4 16.7 %collective-permute-start.6 = (bf16[128,4096]{1,0:T(8,128)(2,1)S(1)}, bf16[128,4096]{1,0:T(8,128)(2,1)S(1)}, u32[]{:S(2)}, u32[]{:S(2)}) collective-permute-start(bf16[128,4096]{1,0:T(8,128)(2,1)S(1)} %collective-permute-done.2.refs_2_), channel_id=1, source_target_pairs={{0,2},{1,7},{2,4},{3,1},{4,6},{5,3},{6,0},{7,5},{8,10},{9,15},{10,... | collective-permute-start | bytes 3145736 | tf_op jit(solution)/shard_map/ppermute | solution.py:147
  132.9 15.2 %collective-permute-start.4 = (bf16[128,4096]{1,0:T(8,128)(2,1)}, bf16[128,4096]{1,0:T(8,128)(2,1)}, u32[]{:S(2)}, u32[]{:S(2)}) collective-permute-start(bf16[128,4096]{1,0:T(8,128)(2,1)} %shard_map.39.refs_3_), channel_id=1, source_target_pairs={{0,1},{1,0},{2,3},{3,2},{4,5},{5,4},{6,7},{7,6},{8,9},{9,8},{10,11... | collective-permute-start | bytes 3145736 | tf_op jit(solution)/shard_map/ppermute | solution.py:147
  134.8 13.2 %collective-permute-start.5 = (bf16[128,4096]{1,0:T(8,128)(2,1)S(1)}, bf16[128,4096]{1,0:T(8,128)(2,1)}, u32[]{:S(2)}, u32[]{:S(2)}) collective-permute-start(bf16[128,4096]{1,0:T(8,128)(2,1)S(1)} %collective-permute-done.2.refs_2_), channel_id=1, source_target_pairs={{0,1},{1,0},{2,3},{3,2},{4,5},{5,4},{6,7},{7,6},{8,9},{9,8},{10,11... | collective-permute-start | bytes 3145736 | tf_op jit(solution)/shard_map/ppermute | solution.py:147
  137.2 10.8 %collective-permute-start.1 = (bf16[128,4096]{1,0:T(8,128)(2,1)S(1)}, bf16[128,4096]{1,0:T(8,128)(2,1)}, u32[]{:S(2)}, u32[]{:S(2)}) collective-permute-start(bf16[128,4096]{1,0:T(8,128)(2,1)S(1)} %collective-permute-done.refs_0_), channel_id=1, source_target_pairs={{0,1},{1,0},{2,3},{3,2},{4,5},{5,4},{6,7},{7,6},{8,9},{9,8},{10,11... | collective-permute-start | bytes 3145736 | tf_op jit(solution)/shard_map/ppermute | solution.py:147
  146.1 4.7 %collective-permute-start.7 = (bf16[128,4096]{1,0:T(8,128)(2,1)S(1)}, bf16[128,4096]{1,0:T(8,128)(2,1)}, u32[]{:S(2)}, u32[]{:S(2)}) collective-permute-start(bf16[128,4096]{1,0:T(8,128)(2,1)S(1)} %collective-permute-done.6.refs_6_), channel_id=1, source_target_pairs={{0,1},{1,0},{2,3},{3,2},{4,5},{5,4},{6,7},{7,6},{8,9},{9,8},{10,11... | collective-permute-start | bytes 3145736 | tf_op jit(solution)/shard_map/ppermute | solution.py:147
Sparse Core Ops, SparseCore 0:
  21.0 128.3 all-gather.2
